TPU v7x, 128 devices: a whole 4x4x4 slice. The times are simulated.
128 devices in a mesh: dp: 2 (over core), ctx: 8 (over x, y_hi), heads: 8 (over y_lo, z).
Axes of the slice: x: 4, y: 4 (y_hi: 2, y_lo: 2; y = y_hi * 2 + y_lo), z: 4, core: 2. Of those that a mesh axis runs over, the one named last changes fastest.
Arguments:
- tokens: bfloat16 [16, 1024, 1536], P(('dp', 'heads'), 'ctx'), may hold values from -6 to 6
- span_order: int32 [16], replicated, may hold values from 0 to 15, each once
- attn_gain: bfloat16 [2, 1536], P(None, ('dp', 'ctx')), may hold values from 0.099609375 to 1.8984375
- w_query: bfloat16 [2, 1536, 1536], P(None, ('dp', 'ctx')), may hold values from -0.15625 to 0.15625
- key_matrix: bfloat16 [2, 1536, 768], P(None, ('dp', 'ctx')), may hold values from -0.15625 to 0.15625
- value_matrix: bfloat16 [2, 1536, 768], P(None, ('dp', 'ctx')), may hold values from -0.15625 to 0.15625
- w_out: bfloat16 [2, 1536, 1536], P(None, ('dp', 'ctx')), may hold values from -0.875 to 0.875
- mlp_gain: bfloat16 [2, 1536], P(None, ('dp', 'ctx')), may hold values from 0.099609375 to 1.8984375
- w_gate: bfloat16 [2, 1536, 4096], P(None, ('dp', 'ctx')), may hold values from -0.15625 to 0.15625
- w_up: bfloat16 [2, 1536, 4096], P(None, ('dp', 'ctx')), may hold values from -0.15625 to 0.15625
- w_down: bfloat16 [2, 4096, 1536], P(None, ('dp', 'ctx')), may hold values from -0.09375 to 0.09375
- cotangent: bfloat16 [16, 1024, 1536], P(('dp', 'heads'), 'ctx'), may hold values from -6 to 6
Outputs:
- block_out: bfloat16 [16, 1024, 1536], P(('dp', 'heads'), 'ctx')
- input_grad: float32 [16, 1024, 1536], P(('dp', 'heads'), 'ctx')
- attn_gain_grad: float32 [2, 1536], P(None, ('dp', 'ctx', 'heads'))
- w_query_grad: float32 [2, 1536, 1536], P(None, ('dp', 'ctx', 'heads'))
- w_key_grad: float32 [2, 1536, 768], P(None, ('dp', 'ctx', 'heads'))
- w_value_grad: float32 [2, 1536, 768], P(None, ('dp', 'ctx', 'heads'))
- w_out_grad: float32 [2, 1536, 1536], P(None, ('dp', 'ctx', 'heads'))
- mlp_gain_grad: float32 [2, 1536], P(None, ('dp', 'ctx', 'heads'))
- w_gate_grad: float32 [2, 1536, 4096], P(None, ('dp', 'ctx', 'heads'))
- w_up_grad: float32 [2, 1536, 4096], P(None, ('dp', 'ctx', 'heads'))
- w_down_grad: float32 [2, 4096, 1536], P(None, ('dp', 'ctx', 'heads'))
Inputs may be any that keep to these rules, and one draw needn't show every extreme that they name: span_order[j] is the place in its sequence of the j-th stored block of 64 positions; every value appears once.
All inputs are finite; a program needn't handle non-finite values.
Results may differ from a plain program's by a relative error of at most 0.039.
Values may be sent and summed in bfloat16 or wider, within the bound.
A program may use at most 320 MiB of HBM per device.

v0:
```python
import math

import jax
import jax.numpy as jnp
from jax import lax
from jax.sharding import PartitionSpec as P

QUERY_HEADS = 16
KEY_VALUE_HEADS = 8
HEAD_SIZE = 96
LAYER_COUNT = 2


rope_base = 100000.0
norm_eps = 1e-05
block_limit = 1024


def matmul(left_side, right_side):
    return jnp.dot(left_side, right_side, preferred_element_type=jnp.float32)


def inner(left_side, right_side):
    return lax.dot_general(
        left_side, right_side, (((0,), (0,)), ((), ())), preferred_element_type=jnp.float32
    )


def outer(left_side, right_side):
    return lax.dot_general(
        left_side, right_side, (((1,), (1,)), ((), ())), preferred_element_type=jnp.float32
    )


def rms_norm(values, gain):
    return values * lax.rsqrt(jnp.mean(values * values, axis=-1, keepdims=True) + norm_eps) * gain


def angle_table(places):
    frequency = rope_base ** (-2.0 * jnp.arange(HEAD_SIZE // 2, dtype=jnp.float32) / HEAD_SIZE)
    return places.astype(jnp.float32)[:, None] * frequency[None, :]


def rotate(values, angles):
    count_of_rows = values.shape[0]
    shaped = values.reshape(count_of_rows, -1, HEAD_SIZE)
    half_dim = HEAD_SIZE // 2
    first_half = shaped[:, :, :half_dim]
    second_half = shaped[:, :, half_dim:]
    cosine = jnp.cos(angles)[:, None, :]
    sine_table = jnp.sin(angles)[:, None, :]
    turned = jnp.concatenate(
        [
            first_half * cosine - second_half * sine_table,
            second_half * cosine + first_half * sine_table,
        ],
        axis=2,
    )
    return turned.reshape(count_of_rows, -1)


def gated_unit(gate_pre, up_pre):
    return jax.nn.silu(gate_pre) * up_pre


def place_rows(span_order, first_row, count_of_rows, span_len):
    row_ids = first_row + jnp.arange(count_of_rows, dtype=jnp.int32)
    slot_ids = jnp.arange(span_order.shape[0], dtype=jnp.int32)
    picked = jnp.sum(
        jnp.where((row_ids // span_len)[:, None] == slot_ids[None, :], span_order[None, :], 0),
        axis=1,
    )
    return picked * span_len + row_ids % span_len


def stack_heads(columns, head_cluster):
    count_of_rows = columns.shape[0]
    return (
        columns.reshape(count_of_rows, head_cluster, HEAD_SIZE)
        .transpose(1, 0, 2)
        .reshape(head_cluster * count_of_rows, HEAD_SIZE)
    )


def split_heads(stacked, head_cluster):
    count_of_rows = stacked.shape[0] // head_cluster
    return (
        stacked.reshape(head_cluster, count_of_rows, HEAD_SIZE)
        .transpose(1, 0, 2)
        .reshape(count_of_rows, head_cluster * HEAD_SIZE)
    )


def by_sequence(gathered, ctx_count, seq_count, tok_rows):
    return (
        gathered.reshape(ctx_count, seq_count, tok_rows, -1)
        .transpose(1, 0, 2, 3)
        .reshape(seq_count, ctx_count * tok_rows, -1)
    )


def from_sequence(grouped, ctx_count, seq_count, tok_rows):
    return (
        grouped.reshape(seq_count, ctx_count, tok_rows, -1)
        .transpose(1, 0, 2, 3)
        .reshape(ctx_count * seq_count * tok_rows, -1)
    )


def feature_split(matrix, owner_groups, head_count):
    return matrix.reshape(
        matrix.shape[0], owner_groups, head_count, matrix.shape[1] // (owner_groups * head_count)
    )


def gain_order(values, owner_groups, head_count):
    return values.reshape(owner_groups, head_count, -1).transpose(1, 0, 2)


def attend_forward(query_rows, query_places, key_row_block, value_row_block, key_places):
    total_rows = query_rows.shape[0]
    blocks = max(1, total_rows // block_limit)
    block_rows = total_rows // blocks
    score_scale = 1.0 / math.sqrt(HEAD_SIZE)

    def one_block(inputs):
        query_block, place_block = inputs
        scores = outer(query_block, key_row_block) * score_scale
        allowed = key_places[None, :] <= place_block[:, None]
        scores = jnp.where(allowed, scores, -1e30)
        row_max = jnp.max(scores, axis=1, keepdims=True)
        weights = jnp.where(allowed, jnp.exp(scores - row_max), 0.0)
        row_total = jnp.sum(weights, axis=1, keepdims=True)
        probabilities = (weights / row_total).astype(jnp.bfloat16)
        result = matmul(probabilities, value_row_block).astype(jnp.bfloat16)
        return (result, (row_max + jnp.log(row_total))[:, 0])

    outputs, log_totals = lax.map(
        one_block,
        (
            query_rows.reshape(blocks, block_rows, HEAD_SIZE),
            query_places.reshape(blocks, block_rows),
        ),
    )
    return (outputs.reshape(total_rows, HEAD_SIZE), log_totals.reshape(total_rows))


def attend_backward(
    query_rows, grad_rows, log_totals, query_places, key_row_block, value_row_block, key_places
):
    total_rows = query_rows.shape[0]
    blocks = max(1, total_rows // block_limit)
    block_rows = total_rows // blocks
    score_scale = 1.0 / math.sqrt(HEAD_SIZE)

    def one_block(running, inputs):
        key_sum, value_sum = running
        query_block, grad_block, log_block, place_block = inputs
        scores = outer(query_block, key_row_block) * score_scale
        allowed = key_places[None, :] <= place_block[:, None]
        probabilities = jnp.where(
            allowed, jnp.exp(jnp.where(allowed, scores, 0.0) - log_block[:, None]), 0.0
        )
        prob_low = probabilities.astype(jnp.bfloat16)
        prob_grad = outer(grad_block, value_row_block)
        row_inner = jnp.sum(probabilities * prob_grad, axis=1, keepdims=True)
        score_grad = (probabilities * (prob_grad - row_inner)).astype(jnp.bfloat16)
        query_grad = matmul(score_grad, key_row_block) * score_scale
        key_sum = key_sum + inner(score_grad, query_block) * score_scale
        value_sum = value_sum + inner(prob_low, grad_block)
        return ((key_sum, value_sum), query_grad.astype(jnp.bfloat16))

    zero_rows = jnp.zeros((key_row_block.shape[0], HEAD_SIZE), jnp.float32)
    sums, query_grads = lax.scan(
        one_block,
        (zero_rows, zero_rows),
        (
            query_rows.reshape(blocks, block_rows, HEAD_SIZE),
            grad_rows.reshape(blocks, block_rows, HEAD_SIZE),
            log_totals.reshape(blocks, block_rows),
            query_places.reshape(blocks, block_rows),
        ),
    )
    return (query_grads.reshape(total_rows, HEAD_SIZE), sums[0], sums[1])


def body(
    tokens,
    span_order,
    attn_gain,
    w_query,
    key_matrix,
    value_matrix,
    w_out,
    mlp_gain,
    w_gate,
    w_up,
    w_down,
    cotangent,
):
    ctx_count = lax.axis_size("ctx")
    seq_count = lax.axis_size("heads")
    owner_groups = lax.axis_size("dp") * ctx_count
    tok_rows = tokens.shape[1]
    seq_len = ctx_count * tok_rows
    span_len = seq_len // (2 * ctx_count)
    ctx_index = lax.axis_index("ctx")
    head_cluster = QUERY_HEADS // KEY_VALUE_HEADS
    own_places = place_rows(span_order, ctx_index * tok_rows, tok_rows, span_len)
    tok_angles = angle_table(own_places)
    query_places = jnp.tile(own_places, head_cluster)
    key_places = place_rows(span_order, 0, seq_len, span_len)

    def forward_heads(query_rows, key_row_block, value_row_block):
        return attend_forward(query_rows, query_places, key_row_block, value_row_block, key_places)

    def backward_heads(query_rows, grad_rows, log_rows, key_row_block, value_row_block):
        return attend_backward(
            query_rows,
            grad_rows,
            log_rows,
            query_places,
            key_row_block,
            value_row_block,
            key_places,
        )

    def stack_all(columns):
        return jax.vmap(lambda item: stack_heads(item, head_cluster))(columns)

    def split_all(stacked):
        return jax.vmap(lambda item: split_heads(item, head_cluster))(stacked).reshape(
            seq_count * tok_rows, head_cluster * HEAD_SIZE
        )

    stream = tokens[0].astype(jnp.float32)
    kept_state = []
    for layer_index in range(LAYER_COUNT):
        full_weights = (
            lax.all_gather(attn_gain[layer_index], ("dp", "ctx"), axis=0, tiled=True),
            lax.all_gather(w_query[layer_index], ("dp", "ctx"), axis=0, tiled=True),
            lax.all_gather(key_matrix[layer_index], ("dp", "ctx"), axis=0, tiled=True),
            lax.all_gather(value_matrix[layer_index], ("dp", "ctx"), axis=0, tiled=True),
            lax.all_gather(w_out[layer_index], ("dp", "ctx"), axis=0, tiled=True),
            lax.all_gather(mlp_gain[layer_index], ("dp", "ctx"), axis=0, tiled=True),
            lax.all_gather(w_gate[layer_index], ("dp", "ctx"), axis=0, tiled=True),
            lax.all_gather(w_up[layer_index], ("dp", "ctx"), axis=0, tiled=True),
            lax.all_gather(w_down[layer_index], ("dp", "ctx"), axis=0, tiled=True),
        )
        gain_attn, query_w, key_w, value_w, out_w, gain_mlp, gate_w, up_w, down_w = full_weights
        normed = rms_norm(stream, gain_attn.astype(jnp.float32)).astype(jnp.bfloat16)
        queries = rotate(matmul(normed, query_w), tok_angles).astype(jnp.bfloat16)
        key_tok = rotate(matmul(normed, key_w), tok_angles).astype(jnp.bfloat16)
        value_tok = matmul(normed, value_w).astype(jnp.bfloat16)
        head_query, head_key, head_value = (
            lax.all_to_all(queries, "heads", split_axis=1, concat_axis=0, tiled=True),
            lax.all_to_all(key_tok, "heads", split_axis=1, concat_axis=0, tiled=True),
            lax.all_to_all(value_tok, "heads", split_axis=1, concat_axis=0, tiled=True),
        )
        gathered_keys, gathered_values = (
            lax.all_gather(head_key, "ctx", axis=0, tiled=True),
            lax.all_gather(head_value, "ctx", axis=0, tiled=True),
        )
        all_keys = by_sequence(gathered_keys, ctx_count, seq_count, tok_rows)
        all_values = by_sequence(gathered_values, ctx_count, seq_count, tok_rows)
        query_seq = head_query.reshape(seq_count, tok_rows, -1)
        log_parts = []
        kv_index = 0
        query_rows = stack_all(query_seq)
        out_rows, log_rows = jax.vmap(forward_heads)(query_rows, all_keys, all_values)
        out_parts = split_all(out_rows)
        log_parts.append(log_rows)
        mixed_tok = lax.all_to_all(out_parts, "heads", split_axis=0, concat_axis=1, tiled=True)
        middle = stream + matmul(mixed_tok, out_w)
        normed_mlp = rms_norm(middle, gain_mlp.astype(jnp.float32)).astype(jnp.bfloat16)
        gate_pre = matmul(normed_mlp, gate_w)
        up_proj = matmul(normed_mlp, up_w)
        hidden = gated_unit(gate_pre, up_proj).astype(jnp.bfloat16)
        kept_state.append(
            (
                stream,
                normed,
                head_query,
                head_key,
                head_value,
                all_keys,
                all_values,
                log_parts,
                mixed_tok,
                middle,
                normed_mlp,
                gate_pre,
                up_proj,
                hidden,
                full_weights,
            )
        )
        stream = middle + matmul(hidden, down_w)
    block_out = stream.astype(jnp.bfloat16)[None]
    stream_grad = cotangent[0].astype(jnp.float32)
    layer_grads = []
    for layer_index in reversed(range(LAYER_COUNT)):
        (
            layer_in,
            normed,
            head_query,
            head_key,
            head_value,
            all_keys,
            all_values,
            log_parts,
            mixed_tok,
            middle,
            normed_mlp,
            gate_pre,
            up_proj,
            hidden,
            full_weights,
        ) = kept_state[layer_index]
        gain_attn, query_w, key_w, value_w, out_w, gain_mlp, gate_w, up_w, down_w = full_weights
        down_grad = stream_grad.astype(jnp.bfloat16)
        hidden_grad = outer(down_grad, down_w)
        _, unit_back = jax.vjp(gated_unit, gate_pre, up_proj)
        gate_grad, up_grad = unit_back(hidden_grad)
        gate_grad = gate_grad.astype(jnp.bfloat16)
        up_grad = up_grad.astype(jnp.bfloat16)
        mlp_in_grad = outer(gate_grad, gate_w) + outer(up_grad, up_w)
        _, mlp_norm_back = jax.vjp(rms_norm, middle, gain_mlp.astype(jnp.float32))
        middle_part, mlp_gain_part = mlp_norm_back(mlp_in_grad)
        middle_grad = stream_grad + middle_part
        out_grad = middle_grad.astype(jnp.bfloat16)
        mixed_grad = outer(out_grad, out_w).astype(jnp.bfloat16)
        head_grad = lax.all_to_all(mixed_grad, "heads", split_axis=1, concat_axis=0, tiled=True)
        query_seq = head_query.reshape(seq_count, tok_rows, -1)
        grad_seq = head_grad.reshape(seq_count, tok_rows, -1)
        kv_index = 0
        columns = slice(
            kv_index * head_cluster * HEAD_SIZE, (kv_index + 1) * head_cluster * HEAD_SIZE
        )
        query_grad, key_sum, value_sum = jax.vmap(backward_heads)(
            stack_all(query_seq), stack_all(grad_seq), log_parts[kv_index], all_keys, all_values
        )
        query_parts = split_all(query_grad)
        key_terms = from_sequence(key_sum, ctx_count, seq_count, tok_rows)
        value_terms = from_sequence(value_sum, ctx_count, seq_count, tok_rows)
        own_keys, own_values = (
            lax.psum_scatter(
                key_terms.astype(jnp.bfloat16), "ctx", scatter_dimension=0, tiled=True
            ).astype(jnp.float32),
            lax.psum_scatter(
                value_terms.astype(jnp.bfloat16), "ctx", scatter_dimension=0, tiled=True
            ).astype(jnp.float32),
        )
        tok_query, tok_key, tok_value = (
            lax.all_to_all(query_parts, "heads", split_axis=0, concat_axis=1, tiled=True),
            lax.all_to_all(
                own_keys.astype(jnp.bfloat16), "heads", split_axis=0, concat_axis=1, tiled=True
            ),
            lax.all_to_all(
                own_values.astype(jnp.bfloat16), "heads", split_axis=0, concat_axis=1, tiled=True
            ),
        )
        query_pre = rotate(tok_query.astype(jnp.float32), -tok_angles).astype(jnp.bfloat16)
        key_pre = rotate(tok_key.astype(jnp.float32), -tok_angles).astype(jnp.bfloat16)
        normed_grad = outer(query_pre, query_w) + outer(key_pre, key_w) + outer(tok_value, value_w)
        _, attn_norm_back = jax.vjp(rms_norm, layer_in, gain_attn.astype(jnp.float32))
        stream_part, attn_gain_part = attn_norm_back(normed_grad)
        stream_grad = middle_grad + stream_part
        normed_all, mixed_all, mlp_all, hidden_all = (
            lax.all_to_all(
                feature_split(normed, owner_groups, seq_count),
                "heads",
                split_axis=2,
                concat_axis=0,
                tiled=True,
            ),
            lax.all_to_all(
                feature_split(mixed_tok, owner_groups, seq_count),
                "heads",
                split_axis=2,
                concat_axis=0,
                tiled=True,
            ),
            lax.all_to_all(
                feature_split(normed_mlp, owner_groups, seq_count),
                "heads",
                split_axis=2,
                concat_axis=0,
                tiled=True,
            ),
            lax.all_to_all(
                feature_split(hidden, owner_groups, seq_count),
                "heads",
                split_axis=2,
                concat_axis=0,
                tiled=True,
            ),
        )
        normed_all = normed_all.reshape(normed_all.shape[0], -1)
        mixed_all = mixed_all.reshape(mixed_all.shape[0], -1)
        mlp_all = mlp_all.reshape(mlp_all.shape[0], -1)
        hidden_all = hidden_all.reshape(hidden_all.shape[0], -1)
        (
            query_rows_all,
            key_rows_all,
            value_rows_all,
            out_rows_all,
            gate_rows_all,
            up_rows_all,
            down_rows_all,
        ) = (
            lax.all_gather(query_pre, "heads", axis=0, tiled=True),
            lax.all_gather(key_pre, "heads", axis=0, tiled=True),
            lax.all_gather(tok_value, "heads", axis=0, tiled=True),
            lax.all_gather(out_grad, "heads", axis=0, tiled=True),
            lax.all_gather(gate_grad, "heads", axis=0, tiled=True),
            lax.all_gather(up_grad, "heads", axis=0, tiled=True),
            lax.all_gather(down_grad, "heads", axis=0, tiled=True),
        )
        gain_attn_sum, gain_mlp_sum = (
            lax.psum_scatter(
                gain_order(attn_gain_part, owner_groups, seq_count),
                "heads",
                scatter_dimension=0,
                tiled=True,
            ),
            lax.psum_scatter(
                gain_order(mlp_gain_part, owner_groups, seq_count),
                "heads",
                scatter_dimension=0,
                tiled=True,
            ),
        )
        owned = (
            lax.psum_scatter(
                gain_attn_sum.reshape(-1).astype(jnp.bfloat16),
                ("dp", "ctx"),
                scatter_dimension=0,
                tiled=True,
            ).astype(jnp.float32),
            lax.psum_scatter(
                inner(normed_all, query_rows_all).astype(jnp.bfloat16),
                ("dp", "ctx"),
                scatter_dimension=0,
                tiled=True,
            ).astype(jnp.float32),
            lax.psum_scatter(
                inner(normed_all, key_rows_all).astype(jnp.bfloat16),
                ("dp", "ctx"),
                scatter_dimension=0,
                tiled=True,
            ).astype(jnp.float32),
            lax.psum_scatter(
                inner(normed_all, value_rows_all).astype(jnp.bfloat16),
                ("dp", "ctx"),
                scatter_dimension=0,
                tiled=True,
            ).astype(jnp.float32),
            lax.psum_scatter(
                inner(mixed_all, out_rows_all).astype(jnp.bfloat16),
                ("dp", "ctx"),
                scatter_dimension=0,
                tiled=True,
            ).astype(jnp.float32),
            lax.psum_scatter(
                gain_mlp_sum.reshape(-1).astype(jnp.bfloat16),
                ("dp", "ctx"),
                scatter_dimension=0,
                tiled=True,
            ).astype(jnp.float32),
            lax.psum_scatter(
                inner(mlp_all, gate_rows_all).astype(jnp.bfloat16),
                ("dp", "ctx"),
                scatter_dimension=0,
                tiled=True,
            ).astype(jnp.float32),
            lax.psum_scatter(
                inner(mlp_all, up_rows_all).astype(jnp.bfloat16),
                ("dp", "ctx"),
                scatter_dimension=0,
                tiled=True,
            ).astype(jnp.float32),
            lax.psum_scatter(
                inner(hidden_all, down_rows_all).astype(jnp.bfloat16),
                ("dp", "ctx"),
                scatter_dimension=0,
                tiled=True,
            ).astype(jnp.float32),
        )
        layer_grads.insert(0, owned)
    stacked = [jnp.stack([owned[member] for owned in layer_grads]) for member in range(9)]
    return (
        block_out,
        stream_grad[None],
        stacked[0],
        stacked[1],
        stacked[2],
        stacked[3],
        stacked[4],
        stacked[5],
        stacked[6],
        stacked[7],
        stacked[8],
    )


def solution(mesh):
    in_specs = (
        P(("dp", "heads"), "ctx", None),
        P(),
        P(None, ("dp", "ctx")),
        P(None, ("dp", "ctx"), None),
        P(None, ("dp", "ctx"), None),
        P(None, ("dp", "ctx"), None),
        P(None, ("dp", "ctx"), None),
        P(None, ("dp", "ctx")),
        P(None, ("dp", "ctx"), None),
        P(None, ("dp", "ctx"), None),
        P(None, ("dp", "ctx"), None),
        P(("dp", "heads"), "ctx", None),
    )
    out_specs = (
        P(("dp", "heads"), "ctx", None),
        P(("dp", "heads"), "ctx", None),
        P(None, ("dp", "ctx", "heads")),
        P(None, ("dp", "ctx", "heads"), None),
        P(None, ("dp", "ctx", "heads"), None),
        P(None, ("dp", "ctx", "heads"), None),
        P(None, ("dp", "ctx", "heads"), None),
        P(None, ("dp", "ctx", "heads")),
        P(None, ("dp", "ctx", "heads"), None),
        P(None, ("dp", "ctx", "heads"), None),
        P(None, ("dp", "ctx", "heads"), None),
    )
    return jax.shard_map(body, mesh=mesh, in_specs=in_specs, out_specs=out_specs, check_vma=False)
```

profile of v0, /device:TPU:5, one launch (start us, length us, event | category | flops | bytes accessed | tf_op | source)
XLA Modules:
  0.0 3180.2 jit_solution(8687086794872530214)
XLA Ops:
  17.2 65.2 %all-reduce.33 = (bf16[1536]{0:T(1024)(128)(2,1)S(1)}, bf16[1536]{0:T(1024)(128)(2,1)}, bf16[1536]{0:T(1024)(128)(2,1)}, bf16[1536]{0:T(1024)(128)(2,1)S(1)}) all-reduce(bf16[1536]{0:T(1024)(128)(2,1)S(1)} %dynamic-update-slice, bf16[1536]{0:T(1024)(128)(2,1)S(1)} %dynamic-update-slice.1, ...), channel_id=2, replica_groups=mesh['dp'=2,'ctx'=8,'heads'=8] {'dp','ctx'}, use_global_device_ids=true, to_apply=%add | all-reduce | flops 6144 | bytes 24576
  137.7 37.4 %all-gather.86.cloned.1.call-done = bf16[1,1536,1536]{2,1,0:T(8,128)(2,1)} async-done(((bf16[1,96,1536]{2,1,0:T(8,128)(2,1)}), bf16[1,1536,1536]{2,1,0:T(8,128)(2,1)}) %all-gather.86.cloned.1.call-update) | async-done | bytes 4718608 | tf_op jit(solution)/shard_map/all_gather | solution.py:241
  232.2 45.2 %all-gather.54.cloned.1.call-done = bf16[8192,96]{0,1:T(8,128)(2,1)} async-done(((bf16[1024,96]{0,1:T(8,128)(2,1)}), bf16[8192,96]{0,1:T(8,128)(2,1)}) %all-gather.54.cloned.1.call-update) | async-done | bytes 1572880 | tf_op jit(solution)/shard_map/all_gather | solution.py:262
  298.6 40.4 %all-gather.92.cloned.1.call-done = bf16[1,1536,1536]{2,1,0:T(8,128)(2,1)} async-done(((bf16[1,96,1536]{2,1,0:T(8,128)(2,1)}), bf16[1,1536,1536]{2,1,0:T(8,128)(2,1)}) %all-gather.92.cloned.1.call-update) | async-done | bytes 4718608 | tf_op jit(solution)/shard_map/all_gather | solution.py:244
  342.6 88.5 %all-gather.94.cloned.1.call-done = bf16[1,1536,4096]{2,1,0:T(8,128)(2,1)} async-done(((bf16[1,96,4096]{2,1,0:T(8,128)(2,1)}), bf16[1,1536,4096]{2,1,0:T(8,128)(2,1)}) %all-gather.94.cloned.1.call-update) | async-done | bytes 12582928 | tf_op jit(solution)/shard_map/all_gather | solution.py:246
  438.8 83.4 %all-gather.96.cloned.1.call-done = bf16[1,1536,4096]{2,1,0:T(8,128)(2,1)} async-done(((bf16[1,96,4096]{2,1,0:T(8,128)(2,1)}), bf16[1,1536,4096]{2,1,0:T(8,128)(2,1)}) %all-gather.96.cloned.1.call-update) | async-done | bytes 12582928 | tf_op jit(solution)/shard_map/all_gather | solution.py:247
  531.2 82.2 %all-gather.98.cloned.1.call-done = bf16[1,4096,1536]{2,1,0:T(8,128)(2,1)} async-done(((bf16[1,256,1536]{2,1,0:T(8,128)(2,1)}), bf16[1,4096,1536]{2,1,0:T(8,128)(2,1)}) %all-gather.98.cloned.1.call-update) | async-done | bytes 12582928 | tf_op jit(solution)/shard_map/all_gather | solution.py:248
  620.4 42.6 %all-gather.102.cloned.1.call-done = bf16[1,1536,768]{2,1,0:T(8,128)(2,1)} async-done(((bf16[1,96,768]{2,1,0:T(8,128)(2,1)}), bf16[1,1536,768]{2,1,0:T(8,128)(2,1)}) %all-gather.102.cloned.1.call-update) | async-done | bytes 2359312 | tf_op jit(solution)/shard_map/all_gather | solution.py:242
  676.4 37.8 %all-gather.104.cloned.1.call-done = bf16[1,1536,768]{2,1,0:T(8,128)(2,1)} async-done(((bf16[1,96,768]{2,1,0:T(8,128)(2,1)}), bf16[1,1536,768]{2,1,0:T(8,128)(2,1)}) %all-gather.104.cloned.1.call-update) | async-done | bytes 2359312 | tf_op jit(solution)/shard_map/all_gather | solution.py:243
  729.4 44.4 %all-gather.100.cloned.1.call-done = bf16[1,1536,1536]{2,1,0:T(8,128)(2,1)} async-done(((bf16[1,96,1536]{2,1,0:T(8,128)(2,1)}), bf16[1,1536,1536]{2,1,0:T(8,128)(2,1)}) %all-gather.100.cloned.1.call-update) | async-done | bytes 4718608 | tf_op jit(solution)/shard_map/all_gather | solution.py:241
  832.5 45.8 %all-gather.58.cloned.1.call-done = bf16[8192,96]{0,1:T(8,128)(2,1)} async-done(((bf16[1024,96]{0,1:T(8,128)(2,1)}), bf16[8192,96]{0,1:T(8,128)(2,1)}) %all-gather.58.cloned.1.call-update) | async-done | bytes 1572880 | tf_op jit(solution)/shard_map/all_gather | solution.py:262
  900.1 72.5 %all-gather.112.cloned.1.call-done = bf16[1,4096,1536]{2,1,0:T(8,128)(2,1)} async-done(((bf16[1,256,1536]{2,1,0:T(8,128)(2,1)}), bf16[1,4096,1536]{2,1,0:T(8,128)(2,1)}) %all-gather.112.cloned.1.call-update) | async-done | bytes 12582928 | tf_op jit(solution)/shard_map/all_gather | solution.py:248
  982.6 48.7 %all-gather.106.cloned.1.call-done = bf16[1,1536,1536]{2,1,0:T(8,128)(2,1)} async-done(((bf16[1,96,1536]{2,1,0:T(8,128)(2,1)}), bf16[1,1536,1536]{2,1,0:T(8,128)(2,1)}) %all-gather.106.cloned.1.call-update) | async-done | bytes 4718608 | tf_op jit(solution)/shard_map/all_gather | solution.py:244
  1036.3 86.9 %all-gather.110.cloned.1.call-done = bf16[1,1536,4096]{2,1,0:T(8,128)(2,1)} async-done(((bf16[1,96,4096]{2,1,0:T(8,128)(2,1)}), bf16[1,1536,4096]{2,1,0:T(8,128)(2,1)}) %all-gather.110.cloned.1.call-update) | async-done | bytes 12582928 | tf_op jit(solution)/shard_map/all_gather | solution.py:247
  1131.1 83.7 %all-gather.108.cloned.1.call-done = bf16[1,1536,4096]{2,1,0:T(8,128)(2,1)} async-done(((bf16[1,96,4096]{2,1,0:T(8,128)(2,1)}), bf16[1,1536,4096]{2,1,0:T(8,128)(2,1)}) %all-gather.108.cloned.1.call-update) | async-done | bytes 12582928 | tf_op jit(solution)/shard_map/all_gather | solution.py:246
  1359.7 70.9 %reduce-scatter.37.cloned.1.call-done = bf16[1024,96]{0,1:T(8,128)(2,1)} async-done(((bf16[8192,96]{0,1:T(8,128)(2,1)}), bf16[1024,96]{0,1:T(8,128)(2,1)}) %reduce-scatter.37.cloned.1.call-update) | async-done | bytes 196624 | tf_op jit(solution)/shard_map/reduce_scatter | solution.py:350
  1547.7 37.9 %reduce-scatter.39.cloned.1.call-done = bf16[1024,96]{0,1:T(8,128)(2,1)} async-done(((bf16[8192,96]{0,1:T(8,128)(2,1)}), bf16[1024,96]{0,1:T(8,128)(2,1)}) %reduce-scatter.39.cloned.1.call-update) | async-done | bytes 196624 | tf_op jit(solution)/shard_map/reduce_scatter | solution.py:347
  1591.4 71.0 %reduce-scatter.41.cloned.1.call-done = bf16[1024,96]{0,1:T(8,128)(2,1)} async-done(((bf16[8192,96]{0,1:T(8,128)(2,1)}), bf16[1024,96]{0,1:T(8,128)(2,1)}) %reduce-scatter.41.cloned.1.call-update) | async-done | bytes 196624 | tf_op jit(solution)/shard_map/reduce_scatter | solution.py:350
  1840.9 47.3 %all-gather.74.cloned.1.call-done = bf16[1024,1536]{1,0:T(8,128)(2,1)} async-done(((bf16[128,1536]{1,0:T(8,128)(2,1)}), bf16[1024,1536]{1,0:T(8,128)(2,1)}) %all-gather.74.cloned.1.call-update) | async-done | bytes 3145744 | tf_op jit(solution)/shard_map/all_gather | solution.py:415
  1890.9 49.3 %all-gather.62.cloned.1.call-done = bf16[1024,1536]{0,1:T(8,128)(2,1)} async-done(((bf16[128,1536]{0,1:T(8,128)(2,1)}), bf16[1024,1536]{0,1:T(8,128)(2,1)}) %all-gather.62.cloned.1.call-update) | async-done | bytes 3145744 | tf_op jit(solution)/shard_map/all_gather | solution.py:412
  1944.1 40.9 %all-gather.70.cloned.1.call-done = bf16[1024,768]{0,1:T(8,128)(2,1)} async-done(((bf16[128,768]{0,1:T(8,128)(2,1)}), bf16[1024,768]{0,1:T(8,128)(2,1)}) %all-gather.70.cloned.1.call-update) | async-done | bytes 1572880 | tf_op jit(solution)/shard_map/all_gather | solution.py:414
  1987.8 41.2 %all-gather.66.cloned.1.call-done = bf16[1024,768]{0,1:T(8,128)(2,1)} async-done(((bf16[128,768]{0,1:T(8,128)(2,1)}), bf16[1024,768]{0,1:T(8,128)(2,1)}) %all-gather.66.cloned.1.call-update) | async-done | bytes 1572880 | tf_op jit(solution)/shard_map/all_gather | solution.py:413
  2069.4 39.3 %all-reduce.32 = (bf16[192]{0:T(256)(128)(2,1)S(1)}, bf16[192]{0:T(256)(128)(2,1)S(1)}, bf16[192]{0:T(256)(128)(2,1)S(1)}, bf16[192]{0:T(256)(128)(2,1)S(1)}) all-reduce(bf16[192]{0:T(256)(128)(2,1)S(1)} %convert_element_type.424, ...), channel_id=28, replica_groups=mesh['dp'=2,'ctx'=8,'heads'=8] {'dp','ctx'}, use_global_device_ids=true, to_apply=%region_25.26.clone | all-reduce | flops 768 | bytes 3072
  2122.6 39.6 %all-gather.72.cloned.1.call-done = bf16[1024,1536]{1,0:T(8,128)(2,1)} async-done(((bf16[128,1536]{1,0:T(8,128)(2,1)}), bf16[1024,1536]{1,0:T(8,128)(2,1)}) %all-gather.72.cloned.1.call-update) | async-done | bytes 3145744 | tf_op jit(solution)/shard_map/all_gather | solution.py:415
  2164.9 49.2 %all-gather.60.cloned.1.call-done = bf16[1024,1536]{0,1:T(8,128)(2,1)} async-done(((bf16[128,1536]{0,1:T(8,128)(2,1)}), bf16[1024,1536]{0,1:T(8,128)(2,1)}) %all-gather.60.cloned.1.call-update) | async-done | bytes 3145744 | tf_op jit(solution)/shard_map/all_gather | solution.py:412
  2217.2 41.6 %all-gather.68.cloned.1.call-done = bf16[1024,768]{0,1:T(8,128)(2,1)} async-done(((bf16[128,768]{0,1:T(8,128)(2,1)}), bf16[1024,768]{0,1:T(8,128)(2,1)}) %all-gather.68.cloned.1.call-update) | async-done | bytes 1572880 | tf_op jit(solution)/shard_map/all_gather | solution.py:414
  2260.8 41.9 %all-gather.64.cloned.1.call-done = bf16[1024,768]{0,1:T(8,128)(2,1)} async-done(((bf16[128,768]{0,1:T(8,128)(2,1)}), bf16[1024,768]{0,1:T(8,128)(2,1)}) %all-gather.64.cloned.1.call-update) | async-done | bytes 1572880 | tf_op jit(solution)/shard_map/all_gather | solution.py:413
  2305.5 95.9 %all-gather.82.cloned.1.call-done = bf16[1024,4096]{1,0:T(8,128)(2,1)} async-done(((bf16[128,4096]{1,0:T(8,128)(2,1)}), bf16[1024,4096]{1,0:T(8,128)(2,1)}) %all-gather.82.cloned.1.call-update) | async-done | bytes 8388624 | tf_op jit(solution)/shard_map/all_gather | solution.py:417
  2407.7 86.1 %all-gather.78.cloned.1.call-done = bf16[1024,4096]{1,0:T(8,128)(2,1)} async-done(((bf16[128,4096]{1,0:T(8,128)(2,1)}), bf16[1024,4096]{1,0:T(8,128)(2,1)}) %all-gather.78.cloned.1.call-update) | async-done | bytes 8388624 | tf_op jit(solution)/shard_map/all_gather | solution.py:416
  2500.2 86.0 %all-gather.80.cloned.1.call-done = bf16[1024,4096]{1,0:T(8,128)(2,1)} async-done(((bf16[128,4096]{1,0:T(8,128)(2,1)}), bf16[1024,4096]{1,0:T(8,128)(2,1)}) %all-gather.80.cloned.1.call-update) | async-done | bytes 8388624 | tf_op jit(solution)/shard_map/all_gather | solution.py:417
  2592.5 86.1 %all-gather.76.cloned.1.call-done = bf16[1024,4096]{1,0:T(8,128)(2,1)} async-done(((bf16[128,4096]{1,0:T(8,128)(2,1)}), bf16[1024,4096]{1,0:T(8,128)(2,1)}) %all-gather.76.cloned.1.call-update) | async-done | bytes 8388624 | tf_op jit(solution)/shard_map/all_gather | solution.py:416
  2685.1 283.9 %fusion.221 = (bf16[16,1536]{1,0:T(8,128)(2,1)S(1)}, bf16[16,1536]{1,0:T(8,128)(2,1)S(1)}, bf16[16,768]{1,0:T(8,128)(2,1)S(1)}, bf16[16,768]{1,0:T(8,128)(2,1)},...) fusion(bf16[192,1536]{1,0:T(8,128)(2,1)S(1)} %copy-done.29, ...), kind=kCustom, calls=%all-reduce-scatter.12 | all-reduce-scatter fusion | flops 6553601 | bytes 10650112
  (667 shorter events, 1048.3 us)
Async XLA Ops:
  12.8 212.5 %all-gather.52.cloned.1.call-start = ((), (), s32[]{:S(2)}) async-start(), calls=%async_computation.34 | async-start | bytes 1769472 | tf_op jit(solution)/shard_map/all_gather | solution.py:261
  131.1 300.1 %all-gather.94.cloned.1.call-start = ((), (), s32[]{:S(2)}) async-start(), calls=%async_computation.65 | async-start | bytes 13369344 | tf_op jit(solution)/shard_map/all_gather | solution.py:246
  132.4 389.9 %all-gather.96.cloned.1.call-start = ((), (), s32[]{:S(2)}) async-start(), calls=%async_computation.66 | async-start | bytes 13369344 | tf_op jit(solution)/shard_map/all_gather | solution.py:247
  133.8 479.6 %all-gather.98.cloned.1.call-start = ((), (), s32[]{:S(2)}) async-start(), calls=%async_computation.67 | async-start | bytes 13369344 | tf_op jit(solution)/shard_map/all_gather | solution.py:248
  135.6 527.3 %all-gather.102.cloned.1.call-start = ((), (), s32[]{:S(2)}) async-start(), calls=%async_computation.69 | async-start | bytes 2506752 | tf_op jit(solution)/shard_map/all_gather | solution.py:242
  136.2 578.0 %all-gather.104.cloned.1.call-start = ((), (), s32[]{:S(2)}) async-start(), calls=%async_computation.70 | async-start | bytes 2506752 | tf_op jit(solution)/shard_map/all_gather | solution.py:243
  137.0 636.8 %all-gather.100.cloned.1.call-start = ((), (), s32[]{:S(2)}) async-start(), calls=%async_computation.68 | async-start | bytes 5013504 | tf_op jit(solution)/shard_map/all_gather | solution.py:241
  298.3 527.3 %all-gather.56.cloned.1.call-start = ((), (), s32[]{:S(2)}) async-start(), calls=%async_computation.36 | async-start | bytes 1769472 | tf_op jit(solution)/shard_map/all_gather | solution.py:261
  727.1 245.5 %all-gather.112.cloned.1.call-start = ((), (), s32[]{:S(2)}) async-start(), calls=%async_computation.74 | async-start | bytes 13369344 | tf_op jit(solution)/shard_map/all_gather | solution.py:248
  727.7 303.6 %all-gather.106.cloned.1.call-start = ((), (), s32[]{:S(2)}) async-start(), calls=%async_computation.71 | async-start | bytes 5013504 | tf_op jit(solution)/shard_map/all_gather | solution.py:244
  728.3 394.9 %all-gather.110.cloned.1.call-start = ((), (), s32[]{:S(2)}) async-start(), calls=%async_computation.73 | async-start | bytes 13369344 | tf_op jit(solution)/shard_map/all_gather | solution.py:247
  728.9 485.9 %all-gather.108.cloned.1.call-start = ((), (), s32[]{:S(2)}) async-start(), calls=%async_computation.72 | async-start | bytes 13369344 | tf_op jit(solution)/shard_map/all_gather | solution.py:246
  1522.5 283.6 %reduce-scatter.49.cloned.1.call-start = ((), (), s32[]{:S(2)}) async-start(), calls=%async_computation.53 | async-start | bytes 73728 | tf_op jit(solution)/shard_map/reduce_scatter | solution.py:427
  1523.4 287.8 %all-gather.114.cloned.1.call-start = ((), (), s32[]{:S(2)}) async-start(), calls=%async_computation.75 | async-start | bytes 3538944 | tf_op jit(solution)/shard_map/all_gather | solution.py:418
  1523.9 292.2 %reduce-scatter.47.cloned.1.call-start = ((), (), s32[]{:S(2)}) async-start(), calls=%async_computation.52 | async-start | bytes 73728 | tf_op jit(solution)/shard_map/reduce_scatter | solution.py:427
  1524.8 315.4 %reduce-scatter.45.cloned.1.call-start = ((), (), s32[]{:S(2)}) async-start(), calls=%async_computation.43 | async-start | bytes 73728 | tf_op jit(solution)/shard_map/reduce_scatter | solution.py:421
  1525.6 362.6 %all-gather.74.cloned.1.call-start = ((), (), s32[]{:S(2)}) async-start(), calls=%async_computation.51 | async-start | bytes 3538944 | tf_op jit(solution)/shard_map/all_gather | solution.py:415
  1526.2 414.0 %all-gather.62.cloned.1.call-start = ((), (), s32[]{:S(2)}) async-start(), calls=%async_computation.45 | async-start | bytes 3538944 | tf_op jit(solution)/shard_map/all_gather | solution.py:412
  1526.9 458.0 %all-gather.70.cloned.1.call-start = ((), (), s32[]{:S(2)}) async-start(), calls=%async_computation.49 | async-start | bytes 1769472 | tf_op jit(solution)/shard_map/all_gather | solution.py:414
  1535.6 493.4 %all-gather.66.cloned.1.call-start = ((), (), s32[]{:S(2)}) async-start(), calls=%async_computation.47 | async-start | bytes 1769472 | tf_op jit(solution)/shard_map/all_gather | solution.py:413
  1668.4 400.3 %reduce-scatter.43.cloned.1.call-start = ((), (), s32[]{:S(2)}) async-start(), calls=%async_computation.42 | async-start | bytes 73728 | tf_op jit(solution)/shard_map/reduce_scatter | solution.py:421
  1678.6 438.8 %all-gather.84.cloned.1.call-start = ((), (), s32[]{:S(2)}) async-start(), calls=%async_computation.58 | async-start | bytes 3538944 | tf_op jit(solution)/shard_map/all_gather | solution.py:418
  1679.3 482.9 %all-gather.72.cloned.1.call-start = ((), (), s32[]{:S(2)}) async-start(), calls=%async_computation.50 | async-start | bytes 3538944 | tf_op jit(solution)/shard_map/all_gather | solution.py:415
  1679.9 534.2 %all-gather.60.cloned.1.call-start = ((), (), s32[]{:S(2)}) async-start(), calls=%async_computation.44 | async-start | bytes 3538944 | tf_op jit(solution)/shard_map/all_gather | solution.py:412
  1680.6 578.1 %all-gather.68.cloned.1.call-start = ((), (), s32[]{:S(2)}) async-start(), calls=%async_computation.48 | async-start | bytes 1769472 | tf_op jit(solution)/shard_map/all_gather | solution.py:414
  1681.4 621.3 %all-gather.64.cloned.1.call-start = ((), (), s32[]{:S(2)}) async-start(), calls=%async_computation.46 | async-start | bytes 1769472 | tf_op jit(solution)/shard_map/all_gather | solution.py:413
  1681.9 719.4 %all-gather.82.cloned.1.call-start = ((), (), s32[]{:S(2)}) async-start(), calls=%async_computation.57 | async-start | bytes 9437184 | tf_op jit(solution)/shard_map/all_gather | solution.py:417
  1682.5 811.3 %all-gather.78.cloned.1.call-start = ((), (), s32[]{:S(2)}) async-start(), calls=%async_computation.55 | async-start | bytes 9437184 | tf_op jit(solution)/shard_map/all_gather | solution.py:416
  1683.3 902.8 %all-gather.80.cloned.1.call-start = ((), (), s32[]{:S(2)}) async-start(), calls=%async_computation.56 | async-start | bytes 9437184 | tf_op jit(solution)/shard_map/all_gather | solution.py:417
  1683.9 994.7 %all-gather.76.cloned.1.call-start = ((), (), s32[]{:S(2)}) async-start(), calls=%async_computation.54 | async-start | bytes 9437184 | tf_op jit(solution)/shard_map/all_gather | solution.py:416
  1790.1 1188.5 %reduce-scatter.53.cloned.1.call-start = ((), (), s32[]{:S(2)}) async-start(), calls=%async_computation.60 | async-start | bytes 1671168 | tf_op jit(solution)/shard_map/reduce_scatter | solution.py:483
  1816.0 1162.6 %reduce-scatter.51.cloned.1.call-start = ((), (), s32[]{:S(2)}) async-start(), calls=%async_computation.59 | async-start | bytes 1671168 | tf_op jit(solution)/shard_map/reduce_scatter | solution.py:483
  (155 other events, 5595.7 us)
Sparse Core Ops, SparseCore 0:
  11.0 50.8 all-gather.87
  64.9 49.9 all-gather.89
  118.0 57.0 all-gather.85
  177.2 47.9 all-gather.51
  227.5 49.9 all-gather.53
  280.3 58.6 all-gather.91
  341.5 89.5 all-gather.93
  433.5 88.6 all-gather.95
  524.7 88.6 all-gather.97
  615.7 47.2 all-gather.101
  666.0 48.1 all-gather.103
  717.0 56.7 all-gather.99
  776.2 49.3 all-gather.55
  828.3 49.9 all-gather.57
  880.6 91.9 all-gather.111
  975.5 55.7 all-gather.105
  1033.6 89.5 all-gather.109
  1126.1 88.6 all-gather.107
  1281.6 72.2 reduce-scatter.34
  1357.5 73.0 reduce-scatter.36
  1511.6 73.9 reduce-scatter.38
  1589.3 73.0 reduce-scatter.40
  1700.1 63.5 all-gather.113
  1889.9 50.2 all-gather.61
  2070.3 47.0 all-gather.83
  2163.8 50.2 all-gather.59
  2304.2 97.1 all-gather.81
  2403.0 90.7 all-gather.77
  2495.3 90.7 all-gather.79
  2587.8 90.7 all-gather.75
  2682.4 78.6 reduce-scatter.52
  2765.0 81.4 reduce-scatter.50
  (10 shorter events, 400.0 us)
where the time goes:
time: 3200 us; the launch traced here: 3180 us
  waiting for transfers between devices  2100 us (66%)
  blocking collectives  443 us (14%)
  matrix products  269 us (8%)
  starting transfers between devices  168 us (5%)
  local copies, waits for them, and re-layouts  155 us (5%)
    unnamed x3, blocking collectives  388 us
    all_gather x2, waiting for transfers between devices, body(): lax.all_gather(up_grad, 'heads', axis=0, tiled=True)  182 us
    all_gather x2, waiting for transfers between devices, body(): lax.all_gather(w_gate[layer_index], ('dp', 'ctx'), axis=0, tiled=True)  172 us
    all_gather x2, waiting for transfers between devices, body(): lax.all_gather(gate_grad, 'heads', axis=0, tiled=True)  172 us
    all_gather x2, waiting for transfers between devices, body(): lax.all_gather(w_up[layer_index], ('dp', 'ctx'), axis=0, tiled=True)  170 us
    all_gather x2, waiting for transfers between devices, body(): lax.all_gather(w_down[layer_index], ('dp', 'ctx'), axis=0, tiled=True)  155 us
    reduce_scatter x2, waiting for transfers between devices, body(): lax.psum_scatter(value_terms.astype(jnp.bfloat16), 'ctx', scatter_dimensi...  142 us
    dot_general x18, matrix products, outer(): lax.dot_general(left_side, right_side, (((1,), (1,)), ((), ())), preferre...  111 us
  transfers between devices with their start and end apart: 109, of which 62 were waited for; matrix products, arithmetic and copies ran while one was open for 19% of the time, Pallas kernels for 0%

commit v1 on v0

v1 whole, which is shorter than its diff:
```python
import functools
import math

import jax
import jax.numpy as jnp
import numpy as np
from jax import lax
from jax.experimental import pallas as pl
from jax.experimental.pallas import tpu as pltpu
from jax.sharding import Mesh, PartitionSpec as P

HEAD = 96
LAYERS = 2
ROPE_BASE = 100000.0
EPS = 1e-05
CTX = ("x", "yh")
TP = ("z", "core")
OWN = ("core", "x", "yh")
ALL = ("core", "x", "yh", "yl", "z")
BF = jnp.bfloat16
F32 = jnp.float32
MESH = pl.DeviceIdType.MESH
SCALE = 1.0 / math.sqrt(HEAD)
WIDE = 1536


def mm(a, b):
    return jnp.dot(a, b, preferred_element_type=F32)


def mm_tn(a, b):
    return lax.dot_general(a, b, (((0,), (0,)), ((), ())), preferred_element_type=F32)


def mm_nt(a, b):
    return lax.dot_general(a, b, (((1,), (1,)), ((), ())), preferred_element_type=F32)


def place_rows(span_order, first, count, span):
    ids = first + jnp.arange(count, dtype=jnp.int32)
    slots = jnp.arange(span_order.shape[0], dtype=jnp.int32)
    picked = jnp.sum(
        jnp.where((ids // span)[:, None] == slots[None, :], span_order[None, :], 0), axis=1
    )
    return picked * span + ids % span


def rope_tables(places):
    freq = ROPE_BASE ** (-2.0 * jnp.arange(HEAD // 2, dtype=F32) / HEAD)
    angles = places.astype(F32)[:, None] * freq[None, :]
    cos, sin = jnp.cos(angles), jnp.sin(angles)
    one, zero = jnp.ones((places.shape[0], 16), F32), jnp.zeros((places.shape[0], 16), F32)
    return (
        jnp.concatenate([cos, one, cos, one], axis=1),
        jnp.concatenate([-sin, zero, sin, zero], axis=1),
    )


def pack_heads(wq, wk, wv):
    lead = wq.shape[:-1]
    q = wq.reshape(*lead, 8, 2, HEAD)
    k = wk.reshape(*lead, 8, 1, HEAD)
    v = wv.reshape(*lead, 8, 3, 32)
    qk = jnp.concatenate([q, k], axis=-2)
    tiles = jnp.concatenate([qk[..., :48], v[..., :16], qk[..., 48:], v[..., 16:]], axis=-1)
    return tiles.reshape(*lead, 8, 384)


def unpack_grads(packed):
    lead = packed.shape[:-2]
    tiles = packed.reshape(*lead, 8, 3, 128)
    qk = jnp.concatenate([tiles[..., :48], tiles[..., 64:112]], axis=-1)
    v = jnp.concatenate([tiles[..., 48:64], tiles[..., 112:]], axis=-1)
    return (
        qk[..., :2, :].reshape(*lead, 1536),
        qk[..., 2, :].reshape(*lead, 768),
        v.reshape(*lead, 768),
    )


def spread_rows(rows):
    r = rows.reshape(3, 2, 16, -1)
    z = jnp.zeros_like(r[0, 0])
    return jnp.concatenate(
        [r[1, 1], r[2, 1], z, r[0, 0], r[1, 0], r[2, 0], z, r[0, 1]], axis=0
    )


def gather_rows(padded):
    c = padded.reshape(8, 16, -1)
    return jnp.concatenate([c[3], c[7], c[4], c[0], c[5], c[1]], axis=0)


class Place:
    def __init__(self):
        self.z, self.core = lax.axis_index("z"), lax.axis_index("core")
        self.c = lax.axis_index("x") * 2 + lax.axis_index("yh")
        self.zp, self.zm, self.zo = (lax.rem(self.z + k, 4) for k in (1, 3, 2))
        self.oc = 1 - self.core

    def greet(self):
        barrier = pltpu.get_barrier_semaphore()
        for dev in ({"z": self.zp}, {"z": self.zm}, {"core": self.oc}):
            pl.semaphore_signal(barrier, inc=1, device_id=dev, device_id_type=MESH)
        for k in range(1, 8):
            there = lax.rem(self.c + k, 8)
            pl.semaphore_signal(barrier, inc=1, device_id=at_ctx(there), device_id_type=MESH)
        pl.semaphore_wait(barrier, 10)


def at_ctx(c):
    return {"x": c // 2, "yh": lax.rem(c, 2)}


def span_of(start, size):
    return pl.ds(pl.multiple_of(start, 64), size)


def slot_rows(zz, cc, half=None):
    base = (zz * 2 + cc) * 128
    return span_of(base, 128) if half is None else span_of(base + 64 * half, 64)


def all_gather(me, buf, ssem, rsem, on_pair):
    z, zp, zm, zo, core, oc = me.z, me.zp, me.zm, me.zo, me.core, me.oc
    up, down, across = {"z": zp}, {"z": zm}, {"core": oc}
    sent = [
        (z, core, 0, up), (z, core, 1, up), (z, core, 1, down), (z, core, 0, down),
        (zm, core, 0, up), (zp, core, 1, down), (z, core, None, across),
        (zm, core, 0, across), (zm, core, 1, across), (zp, core, 1, across), (zp, core, 0, across),
        (zo, core, 0, across), (zo, core, 1, across),
    ]
    come = [
        (zm, core, 0), (zm, core, 1), (zp, core, 1), (zp, core, 0), (zo, core, 0), (zo, core, 1),
        (z, oc, None), (zm, oc, 0), (zm, oc, 1), (zp, oc, 1), (zp, oc, 0), (zo, oc, 0), (zo, oc, 1),
    ]

    def copy(i, rows, dev):
        return pltpu.make_async_remote_copy(
            src_ref=buf.at[rows], dst_ref=buf.at[rows], send_sem=ssem.at[i], recv_sem=rsem.at[i],
            device_id=dev, device_id_type=MESH,
        )

    def send(*which):
        for i in which:
            copy(i, slot_rows(*sent[i][:3]), sent[i][3]).start()

    def arrive(*which):
        for i in which:
            copy(i, slot_rows(*come[i]), sent[i][3]).wait_recv()

    send(0, 2, 1, 3, 6)
    arrive(6)
    on_pair(z)
    arrive(0)
    send(4, 7)
    arrive(2)
    send(5, 9)
    arrive(1)
    send(8)
    arrive(3)
    send(10)
    arrive(7, 8)
    on_pair(zm)
    arrive(9, 10)
    on_pair(zp)
    arrive(4)
    send(11)
    arrive(5)
    send(12)
    arrive(11, 12)
    on_pair(zo)

    def finish():
        for i in range(13):
            copy(i, slot_rows(*sent[i][:3]), sent[i][3]).wait_send()

    return finish


def reduce_scatter(me, part, parts, give, take, ring_out, ring_in, ssem, rsem):
    z, zp, zm, zo, core, oc = me.z, me.zp, me.zm, me.zo, me.core, me.oc
    up, down, across = {"z": zp}, {"z": zm}, {"core": oc}
    mine = span_of(core * 128, 128)
    theirs = span_of(oc * 128, 128)

    def swap(k):
        return pltpu.make_async_remote_copy(
            src_ref=give.at[k], dst_ref=take.at[k], send_sem=ssem.at[k], recv_sem=rsem.at[k],
            device_id=across, device_id_type=MESH,
        )

    def ring(i):
        return pltpu.make_async_remote_copy(
            src_ref=ring_out.at[i], dst_ref=ring_in.at[i], send_sem=ssem.at[4 + i], recv_sem=rsem.at[4 + i],
            device_id=up if i < 3 else down, device_id_type=MESH,
        )

    def make(k, zz):
        parts[k] = part(zz)
        give[k] = parts[k, theirs].astype(BF)
        swap(k).start()

    def merged(k, half):
        rows = span_of(core * 128 + 64 * half, 64)
        return parts[k, rows] + take[k, 64 * half : 64 * half + 64].astype(F32)

    def push(i, value):
        ring_out[i] = value.astype(BF)
        ring(i).start()

    make(0, zo)
    make(1, zp)
    swap(0).wait_recv()
    push(0, merged(0, 0))
    push(3, merged(0, 1))
    make(2, zm)
    swap(1).wait_recv()
    push(1, merged(1, 1))
    swap(2).wait_recv()
    push(4, merged(2, 0))
    make(3, z)
    ring(0).wait_recv()
    push(2, merged(1, 0) + ring_in[0].astype(F32))
    ring(3).wait_recv()
    push(5, merged(2, 1) + ring_in[3].astype(F32))
    swap(3).wait_recv()
    own = [merged(3, 0), merged(3, 1)]
    ring(1).wait_recv()
    own[1] = own[1] + ring_in[1].astype(F32)
    ring(4).wait_recv()
    own[0] = own[0] + ring_in[4].astype(F32)
    ring(2).wait_recv()
    own[0] = own[0] + ring_in[2].astype(F32)
    ring(5).wait_recv()
    own[1] = own[1] + ring_in[5].astype(F32)

    def finish():
        for k in range(4):
            swap(k).wait_send()
        for i in range(6):
            ring(i).wait_send()

    return jnp.concatenate(own, axis=0), finish


class Exchange:
    def __init__(self, me, src, dst, ssem, rsem):
        self.me, self.src, self.dst, self.ssem, self.rsem = me, src, dst, ssem, rsem

    def copy(self, s, come):
        return pltpu.make_async_remote_copy(
            src_ref=self.src.at[span_of(s * 128, 128)], dst_ref=self.dst.at[span_of(come * 128, 128)],
            send_sem=self.ssem.at[s], recv_sem=self.rsem.at[come],
            device_id=at_ctx(s), device_id_type=MESH,
        )

    def send(self, s):
        c = self.me.c

        @pl.when(s != c)
        def _():
            self.copy(s, c).start()

        @pl.when(s == c)
        def _():
            rows = span_of(s * 128, 128)
            self.dst[rows] = self.src[rows]

    def arrive(self):
        @pl.loop(1, 8)
        def _(k):
            there = lax.rem(self.me.c + k, 8)
            self.copy(there, there).wait_recv()

    def finish(self):
        @pl.loop(1, 8)
        def _(k):
            there = lax.rem(self.me.c + k, 8)
            self.copy(there, self.me.c).wait_send()


def lane_masks(rows):
    lane = lax.broadcasted_iota(jnp.int32, (rows, 128), 1)
    v0 = ((lane >= 48) & (lane < 64)) | (lane >= 112)
    v1 = ((lane >= 64) & (lane < 80)) | (lane < 16)
    v2 = ((lane >= 80) & (lane < 96)) | ((lane >= 16) & (lane < 32))
    return v0, v1, v2


def split_packed(packed, key_ref, value_ref):
    v0, v1, v2 = lane_masks(128)

    @pl.loop(0, 8)
    def _(p):
        rows = span_of(p * 128, 128)
        t0, t1, t2 = (packed[rows, 128 * t : 128 * t + 128].astype(F32) for t in range(3))
        key_ref[rows] = jnp.where(v0, 0.0, t2).astype(BF)
        value = jnp.where(v0, t0, 0.0)
        value = value + jnp.where(v1, pltpu.roll(t1, 16, 1), 0.0)
        value = value + jnp.where(v2, pltpu.roll(t2, 32, 1), 0.0)
        value_ref[rows] = value.astype(BF)


def flip(ref):
    return jnp.transpose(ref[...].astype(F32)).astype(BF)


def stacked(ref, rows):
    return jnp.concatenate([ref[rows, 0:128], ref[rows, 128:256]], axis=0)


def rms_of(values):
    return lax.rsqrt(jnp.mean(values * values, axis=-1, keepdims=True) + EPS)


def fwd_kernel(
    stream, gains, cos, sin, pcol, prow, h_in, h_o, h_g, h_u, h_d,
    o_stream, o_middle, o_lse, o_normed, o_qkv, o_mixed, o_nmlp, o_gate, o_up, o_hidden,
    w_in, w_o, w_g, w_u, w_d, buf1, buf2, qs, qr, ms, mr, gate_v, up_v, hid, keys, vals, vals_t, middle,
    parts, give, take, ring_out, ring_in, give2, take2, ring_out2, ring_in2,
    ag_s, ag_r, ag2_s, ag2_r, rs_s, rs_r, rs2_s, rs2_r, ax_s, ax_r, bx_s, bx_r, loc, loc2,
):
    me = Place()
    loads = [
        pltpu.make_async_copy(h, v, loc.at[i])
        for i, (h, v) in enumerate(((h_in, w_in), (h_o, w_o), (h_g, w_g), (h_u, w_u), (h_d, w_d)))
    ]
    for load in loads:
        load.start()
    stores = []

    def store(src, dst):
        stores.append(pltpu.make_async_copy(src, dst, loc2.at[len(stores)]))
        stores[-1].start()

    s = stream[...]
    buf1[slot_rows(me.z, me.core)] = (s * rms_of(s) * gains[0:1, :]).astype(BF)
    me.greet()
    ax = Exchange(me, qs, qr, ax_s, ax_r)
    loads[0].wait()

    def project(zz):
        rows = span_of(zz * 256, 256)
        y = mm(buf1[rows], w_in[...])
        for t in range(3):
            tile = y[:, 128 * t : 128 * t + 128]
            tile = tile * cos[...] + pltpu.roll(tile, 64, 1) * sin[...]
            qs[rows, 128 * t : 128 * t + 128] = tile.astype(BF)
        ax.send(zz * 2)
        ax.send(zz * 2 + 1)

    done_ag = all_gather(me, buf1, ag_s, ag_r, project)
    ax.arrive()
    store(buf1, o_normed)
    store(qr, o_qkv)
    split_packed(qr, keys, vals)
    vals_t[...] = flip(vals)
    bx = Exchange(me, ms, mr, bx_s, bx_r)

    @pl.loop(0, 8)
    def _(k):
        p = lax.rem(me.c + 1 + k, 8)
        rows = span_of(p * 128, 128)
        q = stacked(qr, rows)
        scores = mm_nt(keys[...], q) * SCALE
        scores = jnp.where(pcol[...] <= prow[pl.ds(p, 1), :], scores, -1e30)
        top = jnp.max(scores, axis=0, keepdims=True)
        weights = jnp.exp(scores - top)
        total = jnp.sum(weights, axis=0, keepdims=True)
        o_lse[pl.ds(p, 1), :] = top + jnp.log(total)
        probs = (weights / total).astype(BF)
        out = jnp.transpose(mm(vals_t[...], probs)).astype(BF)
        ms[rows, 0:128] = out[0:128]
        ms[rows, 128:256] = out[128:256]
        bx.send(p)

    bx.arrive()
    store(mr, o_mixed)
    loads[1].wait()

    def out_part(zz):
        return mm(mr[span_of(zz * 256, 256)], w_o[...])

    total, done_rs = reduce_scatter(me, out_part, parts, give, take, ring_out, ring_in, rs_s, rs_r)
    mid = stream[...] + total
    middle[...] = mid
    o_middle[...] = mid
    buf2[slot_rows(me.z, me.core)] = (mid * rms_of(mid) * gains[1:2, :]).astype(BF)
    for load in loads[2:]:
        load.wait()

    def gated(zz):
        rows = span_of(zz * 256, 256)
        gate = mm(buf2[rows], w_g[...])
        gate_v[rows] = gate
        up = mm(buf2[rows], w_u[...])
        up_v[rows] = up
        hid[rows] = (gate / (1.0 + jnp.exp(-gate)) * up).astype(BF)

    done_ag2 = all_gather(me, buf2, ag2_s, ag2_r, gated)
    store(buf2, o_nmlp)
    store(gate_v, o_gate)
    store(up_v, o_up)
    store(hid, o_hidden)

    def down_part(zz):
        return mm(hid[span_of(zz * 256, 256)], w_d[...])

    total, done_rs2 = reduce_scatter(me, down_part, parts, give2, take2, ring_out2, ring_in2, rs2_s, rs2_r)
    o_stream[...] = middle[...] + total
    for done in (done_ag, ax.finish, bx.finish, done_rs, done_ag2, done_rs2):
        done()
    for item in stores:
        item.wait()


def norm_back_of(e, values, gain):
    q = rms_of(values)
    n = values * q
    dn = e * gain
    part = q * (dn - n * jnp.mean(dn * n, axis=-1, keepdims=True))
    return part, jnp.sum(e * n, axis=0, keepdims=True)


def bwd_kernel(
    grad, stream, middle, gains, cos, sin, pcol, prow, lse, h_in, h_o, h_g, h_u, h_d, h_qkv, h_gate, h_up,
    o_grad, o_gains, o_down, o_out, o_gg, o_ug, o_pre,
    w_in, w_o, w_g, w_u, w_d, buf1, buf2, qr, gate_v, up_v, gg, ug, mgs, mgr, keys, vals, keys_t, dk, dv,
    dqs, ps, pr, mid_grad, parts, give, take, ring_out, ring_in, give2, take2, ring_out2, ring_in2,
    ag_s, ag_r, ag2_s, ag2_r, rs_s, rs_r, rs2_s, rs2_r, ax_s, ax_r, bx_s, bx_r, loc, loc2,
):
    me = Place()
    pairs = ((h_d, w_d), (h_gate, gate_v), (h_up, up_v), (h_g, w_g), (h_u, w_u), (h_o, w_o), (h_qkv, qr), (h_in, w_in))
    loads = [pltpu.make_async_copy(h, v, loc.at[i]) for i, (h, v) in enumerate(pairs)]
    for load in loads:
        load.start()
    stores = []

    def store(src, dst):
        stores.append(pltpu.make_async_copy(src, dst, loc2.at[len(stores)]))
        stores[-1].start()

    buf1[slot_rows(me.z, me.core)] = grad[...].astype(BF)
    me.greet()
    for load in loads[:3]:
        load.wait()

    def unit(zz):
        rows = span_of(zz * 256, 256)
        hg = mm_nt(buf1[rows], w_d[...])
        gate, up = gate_v[rows], up_v[rows]
        sig = 1.0 / (1.0 + jnp.exp(-gate))
        gg[rows] = (hg * up * (sig * (1.0 + gate * (1.0 - sig)))).astype(BF)
        ug[rows] = (hg * (gate * sig)).astype(BF)

    done_ag = all_gather(me, buf1, ag_s, ag_r, unit)
    store(buf1, o_down)
    store(gg, o_gg)
    store(ug, o_ug)
    for load in loads[3:5]:
        load.wait()

    def mlp_part(zz):
        rows = span_of(zz * 256, 256)
        return mm_nt(gg[rows], w_g[...]) + mm_nt(ug[rows], w_u[...])

    e, done_rs = reduce_scatter(me, mlp_part, parts, give, take, ring_out, ring_in, rs_s, rs_r)
    part, gain_part = norm_back_of(e, middle[...], gains[1:2, :])
    o_gains[1:2, :] = gain_part
    gm = grad[...] + part
    mid_grad[...] = gm
    buf2[slot_rows(me.z, me.core)] = gm.astype(BF)
    for load in loads[5:7]:
        load.wait()
    ax = Exchange(me, mgs, mgr, ax_s, ax_r)

    def mixed_back(zz):
        rows = span_of(zz * 256, 256)
        mgs[rows] = mm_nt(buf2[rows], w_o[...]).astype(BF)
        ax.send(zz * 2)
        ax.send(zz * 2 + 1)

    done_ag2 = all_gather(me, buf2, ag2_s, ag2_r, mixed_back)
    store(buf2, o_out)
    split_packed(qr, keys, vals)
    keys_t[...] = flip(keys)
    dk[...] = jnp.zeros_like(dk)
    dv[...] = jnp.zeros_like(dv)
    ax.arrive()

    @pl.loop(0, 8)
    def _(p):
        rows = span_of(p * 128, 128)
        q = stacked(qr, rows)
        mg = stacked(mgr, rows)
        scores = mm_nt(keys[...], q) * SCALE
        allowed = pcol[...] <= prow[pl.ds(p, 1), :]
        probs = jnp.where(allowed, jnp.exp(scores - lse[pl.ds(p, 1), :]), 0.0)
        pg = mm_nt(vals[...], mg)
        inner = jnp.sum(probs * pg, axis=0, keepdims=True)
        sg = (probs * (pg - inner)).astype(BF)
        dk[...] += mm(sg, q)
        dv[...] += mm(probs.astype(BF), mg)
        dq = jnp.transpose(mm(keys_t[...], sg)) * SCALE
        dqs[rows, 0:128] = dq[0:128]
        dqs[rows, 128:256] = dq[128:256]

    bx = Exchange(me, ps, pr, bx_s, bx_r)
    v0, _, _ = lane_masks(128)

    @pl.loop(0, 8)
    def _(k):
        p = lax.rem(me.c + 1 + k, 8)
        rows = span_of(p * 128, 128)
        value = dv[rows]
        ps[rows, 0:128] = jnp.where(v0, value, dqs[rows, 0:128]).astype(BF)
        ps[rows, 128:256] = jnp.where(v0, pltpu.roll(value, 112, 1), dqs[rows, 128:256]).astype(BF)
        ps[rows, 256:384] = jnp.where(v0, pltpu.roll(value, 96, 1), dk[rows] * SCALE).astype(BF)
        bx.send(p)

    loads[7].wait()
    bx.arrive()

    def in_part(zz):
        rows = span_of(zz * 256, 256)
        for t in range(3):
            cols = slice(128 * t, 128 * t + 128)
            tile = pr[rows, cols].astype(F32)
            mgs_tile = tile * cos[...] - pltpu.roll(tile, 64, 1) * sin[...]
            ps2[rows, cols] = mgs_tile.astype(BF)
        return mm_nt(ps2[rows], w_in[...])

    ps2 = qr
    e, done_rs2 = reduce_scatter(me, in_part, parts, give2, take2, ring_out2, ring_in2, rs2_s, rs2_r)
    store(ps2, o_pre)
    part, gain_part = norm_back_of(e, stream[...], gains[0:1, :])
    o_gains[0:1, :] = gain_part
    o_grad[...] = mid_grad[...] + part
    for done in (done_ag, done_rs, done_ag2, ax.finish, bx.finish, done_rs2):
        done()
    for item in stores:
        item.wait()


def vm(shape, dtype=BF):
    return pltpu.VMEM(shape, dtype)


def rs_scratch():
    return [vm((4, 128, WIDE)), vm((4, 128, WIDE)), vm((6, 64, WIDE)), vm((6, 64, WIDE))]


def sems():
    dma = pltpu.SemaphoreType.DMA
    return [dma((n,)) for n in (13, 13, 13, 13, 10, 10, 10, 10, 8, 8, 8, 8, 8, 8)]


WEIGHTS = [(WIDE, 384), (256, WIDE), (WIDE, 512), (WIDE, 512), (512, WIDE)]


def run_kernel(kernel, name, cid, ins, in_vmem, outs, out_vmem, scratch, flops):
    place = {True: pltpu.VMEM, False: pl.ANY}
    return pl.pallas_call(
        kernel,
        name=name,
        out_shape=[jax.ShapeDtypeStruct(s, d) for s, d in outs],
        in_specs=[pl.BlockSpec(memory_space=place[i < in_vmem]) for i in range(len(ins))],
        out_specs=[pl.BlockSpec(memory_space=place[i < out_vmem]) for i in range(len(outs))],
        scratch_shapes=scratch,
        cost_estimate=pl.CostEstimate(flops=flops, bytes_accessed=60 * 2**20, transcendentals=0),
        compiler_params=pltpu.CompilerParams(
            collective_id=cid, has_side_effects=True, vmem_limit_bytes=60 * 2**20
        ),
    )(*ins)


def layer_fwd(l, stream, gains, cos, sin, pcol, prow, weights):
    outs = [
        ((128, WIDE), F32), ((128, WIDE), F32), ((8, 256), F32),
        ((1024, WIDE), BF), ((1024, 384), BF), ((1024, 256), BF), ((1024, WIDE), BF),
        ((1024, 512), F32), ((1024, 512), F32), ((1024, 512), BF),
    ]
    scratch = [vm(s) for s in WEIGHTS] + [
        vm((1024, WIDE)), vm((1024, WIDE)), vm((1024, 384)), vm((1024, 384)), vm((1024, 256)), vm((1024, 256)),
        vm((1024, 512), F32), vm((1024, 512), F32), vm((1024, 512)),
        vm((1024, 128)), vm((1024, 128)), vm((128, 1024)), vm((128, WIDE), F32), vm((4, 256, WIDE), F32),
    ] + rs_scratch() + rs_scratch() + sems()
    ins = [stream, gains, cos, sin, pcol, prow, *weights]
    return run_kernel(fwd_kernel, f"layer_forward_{l}", 1 + l, ins, 6, outs, 3, scratch, 40 * 10**9)


def layer_bwd(l, grad, stream, middle, gains, cos, sin, pcol, prow, lse, weights, qkv, gate, up):
    outs = [
        ((128, WIDE), F32), ((2, WIDE), F32),
        ((1024, WIDE), BF), ((1024, WIDE), BF), ((1024, 512), BF), ((1024, 512), BF), ((1024, 384), BF),
    ]
    scratch = [vm(s) for s in WEIGHTS] + [
        vm((1024, WIDE)), vm((1024, WIDE)), vm((1024, 384)), vm((1024, 512), F32), vm((1024, 512), F32),
        vm((1024, 512)), vm((1024, 512)), vm((1024, 256)), vm((1024, 256)),
        vm((1024, 128)), vm((1024, 128)), vm((128, 1024)), vm((1024, 128), F32), vm((1024, 128), F32),
        vm((1024, 256), F32), vm((1024, 384)), vm((1024, 384)), vm((128, WIDE), F32), vm((4, 256, WIDE), F32),
    ] + rs_scratch() + rs_scratch() + sems()
    ins = [grad, stream, middle, gains, cos, sin, pcol, prow, lse, *weights, qkv, gate, up]
    return run_kernel(bwd_kernel, f"layer_backward_{l}", 3 + l, ins, 9, outs, 2, scratch, 60 * 10**9)


def collect(rows):
    l, r, _, n = rows.shape
    got = lax.all_gather(rows, OWN, axis=0, tiled=False)
    got = lax.dynamic_index_in_dim(got, lax.axis_index("core"), axis=3, keepdims=False)
    return got.transpose(1, 0, 2, 3).reshape(l, 16 * r, n)


def body(
    tokens, span_order, attn_gain, w_query, key_matrix, value_matrix, w_out, mlp_gain, w_gate, w_up,
    w_down, cotangent,
):
    rows = tokens.shape[1]
    ctx = lax.axis_index("x") * 2 + lax.axis_index("yh")
    core, z = lax.axis_index("core"), lax.axis_index("z")
    member = core * 4 + z
    seq_len = 8 * rows
    span = seq_len // span_order.shape[0]
    cos, sin = rope_tables(place_rows(span_order, ctx * rows, rows, span))
    cos, sin = jnp.tile(cos, (2, 1)), jnp.tile(sin, (2, 1))
    places = place_rows(span_order, 0, seq_len, span)
    pcol = places[:, None]
    prow = jnp.tile(places.reshape(8, rows), (1, 2))

    def mine(packed):
        l, r, _, n = packed.shape
        return lax.dynamic_index_in_dim(packed.reshape(l, r, 2, 4, n), z, axis=3, keepdims=False)

    gains = lax.all_gather(
        jnp.concatenate([attn_gain, mlp_gain], axis=0), OWN, axis=1, tiled=True
    ).astype(F32)
    w_in = collect(mine(pack_heads(w_query, key_matrix, value_matrix)))

    def hidden_split(w):
        return w.reshape(LAYERS, -1, 16, 8, 32).transpose(0, 1, 3, 2, 4).reshape(LAYERS, -1, 8, 512)

    w_g = collect(mine(hidden_split(w_gate)))
    w_u = collect(mine(hidden_split(w_up)))
    w_d = collect(mine(w_down.reshape(LAYERS, 8, 32, 1536).transpose(0, 2, 1, 3)))
    w_o_all = lax.all_gather(w_out, OWN, axis=1, tiled=True)
    w_o_two = lax.dynamic_slice_in_dim(w_o_all, member * 192, 192, axis=1)
    w_o = [
        jnp.concatenate([spread_rows(w_o_two[l, :96]), spread_rows(w_o_two[l, 96:])], axis=0)
        for l in range(LAYERS)
    ]

    stream = tokens[0].astype(F32)
    kept = []
    for l in range(LAYERS):
        weights = (w_in[l], w_o[l], w_g[l], w_u[l], w_d[l])
        two = jnp.stack([gains[l], gains[2 + l]])
        outs = layer_fwd(l, stream, two, cos, sin, pcol, prow, weights)
        kept.append((stream, two, weights, outs))
        stream = outs[0]
    block_out = stream.astype(BF)[None]

    g = cotangent[0].astype(F32)
    gain_parts = [None] * 4
    grads = [None] * LAYERS
    for l in reversed(range(LAYERS)):
        stream, two, weights, outs = kept[l]
        _, middle, lse, normed, qkv, mixed, nmlp, gate, up, hidden = outs
        g, gp, down_grad, out_grad, gate_grad, up_grad, pre = layer_bwd(
            l, g, stream, middle, two, cos, sin, pcol, prow, lse, weights, qkv, gate, up
        )
        gain_parts[l], gain_parts[2 + l] = gp[0], gp[1]
        d_wo = mm_tn(mixed, out_grad)
        d_wo = jnp.concatenate([gather_rows(d_wo[:128]), gather_rows(d_wo[128:])], axis=0)
        d_wgu = jnp.concatenate([mm_tn(nmlp, gate_grad), mm_tn(nmlp, up_grad)], axis=1)
        grads[l] = (mm_tn(normed, pre), d_wgu, mm_tn(hidden, down_grad), d_wo)

    def by_columns(both):
        l, _, n = both.shape
        t = both.astype(BF).reshape(l, 2, 8, 2, 4, 12, n).transpose(2, 3, 1, 4, 0, 5, 6)
        t = t.reshape(16, 8, l, 12, n)
        t = lax.psum_scatter(t, ("x", "yh", "yl"), scatter_dimension=0, tiled=True)[0]
        t = lax.all_to_all(t, ("core", "z"), split_axis=0, concat_axis=0, tiled=True)
        return t.astype(F32).transpose(1, 2, 0, 3)

    d_in = by_columns(jnp.stack([grads[l][0] for l in range(LAYERS)]))
    d_q, d_k, d_v = unpack_grads(d_in)
    d_gu = by_columns(jnp.stack([grads[l][1] for l in range(LAYERS)]))

    def hidden_join(d):
        return d.reshape(LAYERS, 12, 8, 16, 32).transpose(0, 1, 3, 2, 4).reshape(LAYERS, 12, 4096)

    d_g, d_u = hidden_join(d_gu[..., :512]), hidden_join(d_gu[..., 512:])

    d_d = jnp.stack([grads[l][2] for l in range(LAYERS)]).astype(BF)
    d_d = d_d.reshape(LAYERS, 2, 8, 32, 1536).transpose(2, 1, 0, 3, 4).reshape(16, LAYERS, 32, 1536)
    d_d = lax.psum_scatter(d_d, ("x", "yh", "yl"), scatter_dimension=0, tiled=True)[0]
    d_d = lax.ppermute(d_d, ("core", "yl"), [(0, 0), (1, 2), (2, 1), (3, 3)]).astype(F32)

    d_o = jnp.stack([grads[l][3] for l in range(LAYERS)]).astype(BF)
    d_o = d_o.reshape(LAYERS, 2, 2, 4, 12, 1536).transpose(3, 1, 2, 0, 4, 5).reshape(16, LAYERS, 12, 1536)
    d_o = lax.psum_scatter(d_o, ("x", "yh", "yl"), scatter_dimension=0, tiled=True)[0]
    d_o = lax.ppermute(
        d_o, ("x", "z"), [(a * 4 + b, b * 4 + a) for a in range(4) for b in range(4)]
    ).astype(F32)

    gp = jnp.stack(gain_parts).reshape(4, 128, 12).transpose(1, 0, 2)
    gp = lax.psum_scatter(gp, ALL, scatter_dimension=0, tiled=True)[0]
    return (block_out, g[None], gp[:2], d_q, d_k, d_v, d_o, gp[2:], d_g, d_u, d_d)


def solution(mesh):
    fine = Mesh(mesh.devices.reshape(2, 4, 2, 2, 4), ALL)
    seq, ctx, own, every = ("core", "yl", "z"), CTX, OWN, ALL
    act = P(seq, ctx, None)
    in_specs = (act, P(), P(None, own)) + (P(None, own, None),) * 4 + (P(None, own),) + (P(None, own, None),) * 3 + (act,)
    grad = P(None, every, None)
    out_specs = (act, act, P(None, every)) + (grad,) * 4 + (P(None, every),) + (grad,) * 3
    return jax.shard_map(body, mesh=fine, in_specs=in_specs, out_specs=out_specs, check_vma=False)
```

time: 3200 us -> 1160 us (0.36)
  waiting for transfers between devices: 2100 us -> 394 us
  Pallas kernels: 0 us -> 415 us
  blocking collectives: 443 us -> 100 us
  matrix products: 269 us -> 31.9 us
  starting transfers between devices: 168 us -> 20 us
    all_gather x32 -> x5, waiting for transfers between devices: 1640 us -> 261 us  [the longest x4 193 us: collect(): got = lax.all_gather(rows, OWN, axis=0, tiled=False)]
    pallas_call x0 -> x4, Pallas kernels: none -> 415 us  [run_kernel(): pl.pallas_call(kernel, name=name, out_shape=[jax.ShapeDtypeStruct(s, d) f...]
    unnamed x3 -> x1, blocking collectives: 388 us -> 67.5 us
    reduce_scatter x10 -> x0, waiting for transfers between devices: 276 us -> none  [the longest x2 142 us: body(): lax.psum_scatter(value_terms.astype(jnp.bfloat16), 'ctx', scatter_dimensi...]
    dot_general x54 -> x10, matrix products: 269 us -> 31.9 us  [mm_tn(): lax.dot_general(a, b, (((0,), (0,)), ((), ())), preferred_element_type=F32)]
    unnamed x48 -> x4, starting transfers between devices: 88.1 us -> 0.16 us
    all_to_all x19 -> x2, waiting for transfers between devices: 82.8 us -> 4.18 us  [by_columns(): lax.all_to_all(t, ('core', 'z'), split_axis=0, concat_axis=0, tiled=True)]
    all_to_all x19 -> x2, starting transfers between devices: 76.3 us -> 10.3 us  [by_columns(): lax.all_to_all(t, ('core', 'z'), split_axis=0, concat_axis=0, tiled=True)]
  transfers between devices with their start and end apart: 109 -> 13, of which waited for: 62 -> 10; matrix products, arithmetic and copies ran while one was open for 19% -> 13% of each run, Pallas kernels for 0% -> 0%
where the time goes in v1:
time: 1160 us; the launch traced here: 1150 us
  Pallas kernels  415 us (36%)
  waiting for transfers between devices  394 us (34%)
  local copies, waits for them, and re-layouts  139 us (12%)
  blocking collectives  100 us (9%)
  matrix products  31.9 us (3%)
  other arithmetic  30 us (3%)
  starting transfers between devices  20 us (2%)
  between operations  15.6 us (1%)
    pallas_call x4, Pallas kernels, run_kernel(): pl.pallas_call(kernel, name=name, out_shape=[jax.ShapeDtypeStruct(s, d) f...  415 us
    all_gather x4, waiting for transfers between devices, collect(): got = lax.all_gather(rows, OWN, axis=0, tiled=False)  193 us
    unnamed x13, waiting for transfers between devices  127 us
    all_gather x1, waiting for transfers between devices, body(): w_o_all = lax.all_gather(w_out, OWN, axis=1, tiled=True)  68.3 us
    unnamed x1, blocking collectives  67.5 us
    all_gather x1, blocking collectives, body(): lax.all_gather(jnp.concatenate([attn_gain, mlp_gain], axis=0), OWN, axis=...  32.8 us
    dot_general x10, matrix products, mm_tn(): lax.dot_general(a, b, (((0,), (0,)), ((), ())), preferred_element_type=F32)  31.9 us
    transpose x2, local copies, waits for them, and re-layouts, by_columns(): both.astype(BF).reshape(l, 2, 8, 2, 4, 12, n).transpose(2, 3, 1, 4, 0, 5, 6)  25.7 us
  transfers between devices with their start and end apart: 13, of which 10 were waited for; matrix products, arithmetic and copies ran while one was open for 13% of the time, Pallas kernels for 0%

profile of v1, /device:TPU:5, one launch (start us, length us, event | category | flops | bytes accessed | tf_op | source)
XLA Modules:
  0.0 1145.9 jit_solution(11045174939217841661)
XLA Ops:
  20.7 7.8 fusion.2
  48.4 32.8 %all-gather.4 = bf16[16,96,4]{1,2,0:T(4,128)(2,1)S(1)} all-gather(bf16[1,96,4]{1,2,0:T(4,128)(2,1)S(1)} %maximum_bitcast_fusion.4), channel_id=1, replica_groups=mesh['core'=2,'x'=4,'yh'=2,'yl'=2,'z'=4] {'core','x','yh'}, dimensions={0}, use_global_device_ids=true | all-gather | bytes 13056 | tf_op jit(solution)/shard_map/all_gather | solution.py:635
  86.5 5.5 all-gather.13.cloned.1.call-done
  95.6 62.5 %all-gather.17.cloned.1.call-done = bf16[32,96,2,1,512]{4,1,3,2,0:T(8,128)(2,1)} async-done(((bf16[2,96,2,1,512]{4,1,3,2,0:T(8,128)(2,1)}), bf16[32,96,2,1,512]{4,1,3,2,0:T(8,128)(2,1)}) %all-gather.17.cloned.1.call-update) | async-done | bytes 6291472 | tf_op jit(solution)/shard_map/all_gather | solution.py:610
  158.1 65.6 %all-gather.15.cloned.1.call-done = bf16[32,96,2,1,512]{4,1,3,2,0:T(8,128)(2,1)} async-done(((bf16[2,96,2,1,512]{4,1,3,2,0:T(8,128)(2,1)}), bf16[32,96,2,1,512]{4,1,3,2,0:T(8,128)(2,1)}) %all-gather.15.cloned.1.call-update) | async-done | bytes 6291472 | tf_op jit(solution)/shard_map/all_gather | solution.py:610
  223.7 6.2 dynamic-slice_bitcast_fusion.1
  229.9 59.3 %all-gather.19.cloned.1.call-done = bf16[32,32,2,1,1536]{4,1,3,2,0:T(8,128)(2,1)} async-done(((bf16[2,32,2,1,1536]{4,1,3,2,0:T(8,128)(2,1)}), bf16[32,32,2,1,1536]{4,1,3,2,0:T(8,128)(2,1)}) %all-gather.19.cloned.1.call-update) | async-done | bytes 6291472 | tf_op jit(solution)/shard_map/all_gather | solution.py:610
  298.9 68.3 %all-gather.11.cloned.1.call-done = bf16[2,1536,1536]{2,1,0:T(8,128)(2,1)} async-done(((bf16[2,96,1536]{2,1,0:T(8,128)(2,1)}), bf16[2,1536,1536]{2,1,0:T(8,128)(2,1)}) %all-gather.11.cloned.1.call-update) | async-done | bytes 9437200 | tf_op jit(solution)/shard_map/all_gather | solution.py:646
  370.3 100.0 %layer_forward_0.1 = (f32[128,1536]{1,0:T(8,128)}, f32[128,1536]{1,0:T(8,128)}, f32[8,256]{1,0:T(8,128)}, bf16[1024,1536]{1,0:T(8,128)(2,1)}, bf16[1024,384]{1,0...) custom-call(f32[128,1536]{1,0:T(8,128)} %bitcast_convert_fusion.1.st, ...), custom_call_target="tpu_custom_call" | custom-call | flops 40000000000 | bytes 62914560 | tf_op jit(solution)/shard_map/layer_forward_0/pallas_call | solution.py:564
  470.3 102.8 %layer_forward_1.1 = (f32[128,1536]{1,0:T(8,128)}, f32[128,1536]{1,0:T(8,128)}, f32[8,256]{1,0:T(8,128)}, bf16[1024,1536]{1,0:T(8,128)(2,1)}, bf16[1024,384]{1,0...) custom-call(f32[128,1536]{1,0:T(8,128)} %get-tuple-element.45.stream, ...), custom_call_target="tpu_custom_call" | custom-call | flops 40000000000 | bytes 62914560 | tf_op jit(solution)/shard_map/layer_forward_1/pallas_call | solution.py:564
  573.1 105.0 %layer_backward_1.1 = (f32[128,1536]{1,0:T(8,128)}, f32[2,1536]{1,0:T(2,128)}, bf16[1024,1536]{1,0:T(8,128)(2,1)}, bf16[1024,1536]{1,0:T(8,128)(2,1)}, bf16[1024...) custom-call(f32[128,1536]{1,0:T(8,128)} %bitcast_convert_fusion.grad, ...), custom_call_target="tpu_custom_call" | custom-call | flops 60000002048 | bytes 62914560 | tf_op jit(solution)/shard_map/layer_backward_1/pallas_call | solution.py:564
  681.4 107.2 %layer_backward_0.1 = (f32[128,1536]{1,0:T(8,128)}, f32[2,1536]{1,0:T(2,128)}, bf16[1024,1536]{1,0:T(8,128)(2,1)}, bf16[1024,1536]{1,0:T(8,128)(2,1)}, bf16[1024...) custom-call(f32[128,1536]{1,0:T(8,128)} %get-tuple-element.52.grad, ...), custom_call_target="tpu_custom_call" | custom-call | flops 60000002048 | bytes 62914560 | tf_op jit(solution)/shard_map/layer_backward_0/pallas_call | solution.py:564
  798.5 5.0 convolution_convert_fusion.7
  806.3 3.9 copy.215
  812.2 3.9 convolution_convert_fusion.2
  819.9 4.9 copy.224
  824.7 6.2 stack.55
  830.9 3.9 convolution_convert_fusion.4
  838.5 4.7 copy.223
  843.2 6.1 stack.54
  849.3 8.1 maximum_bitcast_fusion
  857.4 21.8 %copy.225 = bf16[8,2,2,4,2,12,1024]{6,4,5,3,2,1,0:T(2,128)(2,1)S(1)} copy(bf16[8,2,2,4,2,12,1024]{6,5,3,1,0,2,4:T(8,128)(2,1)} %maximum_bitcast_fusion) | data formatting | bytes 12582912 | tf_op jit(solution)/shard_map/transpose | solution.py:680
  879.2 6.8 copy.226
  886.2 4.2 convolution_convert_fusion
  896.3 67.5 %all-reduce = f32[128,4,12]{2,1,0:T(4,128)S(1)} all-reduce(f32[128,4,12]{2,1,0:T(4,128)S(1)} %copy.214), channel_id=6, replica_groups=mesh['core'=2,'x'=4,'yh'=2,'yl'=2,'z'=4] {'core','x','yh','yl','z'}, use_global_device_ids=true, to_apply=%region_2.3.clone | all-reduce | flops 6144 | bytes 49152
  966.2 4.6 collective-permute-start
  972.6 4.1 all-to-all-start
  978.2 4.2 all-to-all-done
  982.8 59.1 %reduce-scatter.12.cloned.1.call-done = bf16[1,8,2,12,1024]{4,1,3,2,0:T(8,128)(2,1)} async-done(((bf16[16,8,2,12,1024]{4,1,3,2,0:T(8,128)(2,1)}), bf16[1,8,2,12,1024]{4,1,3,2,0:T(8,128)(2,1)}) %reduce-scatter.12.cloned.1.call-update) | async-done | bytes 393232
  1044.0 6.2 all-to-all-start.1
  1051.4 67.6 %reduce-scatter.14.cloned.1.call-done = bf16[1,2,32,1536]{3,2,1,0:T(8,128)(2,1)} async-done(((bf16[16,2,32,1536]{3,2,1,0:T(8,128)(2,1)}), bf16[1,2,32,1536]{3,2,1,0:T(8,128)(2,1)}) %reduce-scatter.14.cloned.1.call-update) | async-done | bytes 196624
  1119.0 4.8 collective-permute-start.1
  (240 shorter events, 109.8 us)
Async XLA Ops:
  7.2 39.8 %copy-start = (bf16[2,256,1536]{2,1,0:T(8,128)(2,1)S(1)}, bf16[2,256,1536]{2,1,0:T(8,128)(2,1)}, u32[]{:S(2)}) copy-start(bf16[2,256,1536]{2,1,0:T(8,128)(2,1)} %param.22) | copy-start | bytes 4718596
  7.2 84.8 %all-gather.13.cloned.1.call-start = ((), (), s32[]{:S(2)}) async-start(), calls=%async_computation.6 | async-start | bytes 5013504 | tf_op jit(solution)/shard_map/all_gather | solution.py:610
  32.6 125.5 %all-gather.17.cloned.1.call-start = ((), (), s32[]{:S(2)}) async-start(), calls=%async_computation.8 | async-start | bytes 6684672 | tf_op jit(solution)/shard_map/all_gather | solution.py:610
  39.7 184.0 %all-gather.15.cloned.1.call-start = ((), (), s32[]{:S(2)}) async-start(), calls=%async_computation.7 | async-start | bytes 6684672 | tf_op jit(solution)/shard_map/all_gather | solution.py:610
  43.6 4.8 copy-start.14
  43.6 4.8 copy-start.15
  45.8 35.6 %copy-start.13 = (s32[16]{0:T(128)S(1)}, s32[16]{0:T(128)}, u32[]{:S(2)}) copy-start(s32[16]{0:T(128)} %param.13) | copy-start | bytes 196
  45.9 38.7 %copy-start.7 = (bf16[1,128,1536]{2,1,0:T(8,128)(2,1)S(1)}, bf16[1,128,1536]{2,1,0:T(8,128)(2,1)}, u32[]{:S(2)}) copy-start(bf16[1,128,1536]{2,1,0:T(8,128)(2,1)} %param.12) | copy-start | bytes 1179652
  46.9 38.7 %copy-start.8 = (bf16[1,128,1536]{2,1,0:T(8,128)(2,1)S(1)}, bf16[1,128,1536]{2,1,0:T(8,128)(2,1)}, u32[]{:S(2)}) copy-start(bf16[1,128,1536]{2,1,0:T(8,128)(2,1)} %param.23) | copy-start | bytes 1179652
  46.9 242.3 %all-gather.19.cloned.1.call-start = ((), (), s32[]{:S(2)}) async-start(), calls=%async_computation.9 | async-start | bytes 6684672 | tf_op jit(solution)/shard_map/all_gather | solution.py:610
  47.8 319.4 %all-gather.11.cloned.1.call-start = ((), (), s32[]{:S(2)}) async-start(), calls=%async_computation.5 | async-start | bytes 10027008 | tf_op jit(solution)/shard_map/all_gather | solution.py:646
  48.4 916.3 %all-reduce.7.cloned.1.call-start = ((), (), s32[]{:S(2)}) async-start(), calls=%async_computation.10 | async-start | bytes 2359296
  292.1 3.0 copy-start.2
  368.9 101.4 %copy-start.12 = (bf16[256,1536]{1,0:T(8,128)(2,1)}, bf16[256,1536]{1,0:T(8,128)(2,1)S(1)}, u32[]{:S(2)}) copy-start(bf16[256,1536]{1,0:T(8,128)(2,1)S(1)} %constant_dynamic-update-slice_fusion.16.h_o) | copy-start | bytes 2359300
  573.1 105.0 %copy-start.20 = (bf16[1024,256]{1,0:T(8,128)(2,1)S(1)}, bf16[1024,256]{1,0:T(8,128)(2,1)}, u32[]{:S(2)}) copy-start(bf16[1024,256]{1,0:T(8,128)(2,1)} %get-tuple-element.67) | copy-start | bytes 1572868
  681.4 107.2 %copy-start.19 = (bf16[1024,256]{1,0:T(8,128)(2,1)S(1)}, bf16[1024,256]{1,0:T(8,128)(2,1)}, u32[]{:S(2)}) copy-start(bf16[1024,256]{1,0:T(8,128)(2,1)} %get-tuple-element.65) | copy-start | bytes 1572868
  794.2 176.6 %reduce-scatter.10.cloned.1.call-start = ((), (), s32[]{:S(2)}) async-start(), calls=%async_computation.11 | async-start | bytes 2506752
  812.1 229.7 %reduce-scatter.12.cloned.1.call-start = ((), (), s32[]{:S(2)}) async-start(), calls=%async_computation.12 | async-start | bytes 6684672
  812.2 3.9 copy-start.22
  812.2 3.9 copy-start.24
  824.7 6.2 copy-start.27
  830.9 3.9 copy-start.21
  830.9 3.9 copy-start.26
  886.1 4.3 copy-start.18
  886.1 232.9 %reduce-scatter.14.cloned.1.call-start = ((), (), s32[]{:S(2)}) async-start(), calls=%async_computation.13 | async-start | bytes 3342336
  886.2 4.2 copy-start.17
  894.5 69.3 %copy-start.6 = (f32[128,1536]{1,0:T(8,128)S(1)}, f32[128,1536]{1,0:T(8,128)}, u32[]{:S(2)}) copy-start(f32[128,1536]{1,0:T(8,128)} %get-tuple-element.46) | copy-start | bytes 2359300
  966.2 11.2 collective-permute-start
  972.6 9.8 all-to-all-start
  1044.0 83.8 %all-to-all-start.1 = ((bf16[8,2,12,1024]{3,1,2,0:T(2,128)(2,1)}), bf16[8,2,12,1024]{3,1,2,0:T(2,128)(2,1)S(1)}, u32[]{:S(2)}, u32[]{:S(2)}) async-start(bf16[8,2,12,1024]{3,1,2,0:T(2,128)(2,1)} %copy.227), calls=%async_computation.1 | async-start | bytes 786432 | tf_op jit(solution)/shard_map/all_to_all | solution.py:683
  1119.0 8.1 collective-permute-start.1
  1132.0 6.8 copy-start.1
  (9 other events, 16.2 us)
Sparse Core Ops, SparseCore 0:
  32.8 59.2 all-gather.12
  95.0 63.0 all-gather.16
  161.1 62.5 all-gather.14
  226.6 62.5 all-gather.18
  291.6 75.4 all-gather.10
  794.4 84.1 all-reduce.6
  881.8 74.4 reduce-scatter.9
  959.8 82.0 reduce-scatter.11
  1045.2 73.7 reduce-scatter.13

commit v2 on v1

v2 whole, which is shorter than its diff:
```python
import functools
import math

import jax
import jax.numpy as jnp
import numpy as np
from jax import lax
from jax.experimental import pallas as pl
from jax.experimental.pallas import tpu as pltpu
from jax.sharding import Mesh, PartitionSpec as P

HEAD = 96
LAYERS = 2
ROPE_BASE = 100000.0
EPS = 1e-05
CTX = ("x", "yh")
TP = ("z", "core")
OWN = ("core", "x", "yh")
ALL = ("core", "x", "yh", "yl", "z")
BF = jnp.bfloat16
F32 = jnp.float32
MESH = pl.DeviceIdType.MESH
SCALE = 1.0 / math.sqrt(HEAD)
WIDE = 1536


def mm(a, b):
    return jnp.dot(a, b, preferred_element_type=F32)


def mm_tn(a, b):
    return lax.dot_general(a, b, (((0,), (0,)), ((), ())), preferred_element_type=F32)


def mm_nt(a, b):
    return lax.dot_general(a, b, (((1,), (1,)), ((), ())), preferred_element_type=F32)


def place_rows(span_order, first, count, span):
    ids = first + jnp.arange(count, dtype=jnp.int32)
    slots = jnp.arange(span_order.shape[0], dtype=jnp.int32)
    picked = jnp.sum(
        jnp.where((ids // span)[:, None] == slots[None, :], span_order[None, :], 0), axis=1
    )
    return picked * span + ids % span


def rope_tables(places):
    freq = ROPE_BASE ** (-2.0 * jnp.arange(HEAD // 2, dtype=F32) / HEAD)
    angles = places.astype(F32)[:, None] * freq[None, :]
    cos, sin = jnp.cos(angles), jnp.sin(angles)
    one, zero = jnp.ones((places.shape[0], 16), F32), jnp.zeros((places.shape[0], 16), F32)
    return (
        jnp.concatenate([cos, one, cos, one], axis=1),
        jnp.concatenate([-sin, zero, sin, zero], axis=1),
    )


def pack_heads(q, k, v):
    lead = q.shape[:-1]
    qk = jnp.concatenate([q.reshape(*lead, 2, HEAD), k.reshape(*lead, 1, HEAD)], axis=-2)
    v = v.reshape(*lead, 3, 32)
    tiles = jnp.concatenate([qk[..., :48], v[..., :16], qk[..., 48:], v[..., 16:]], axis=-1)
    return tiles.reshape(*lead, 384)


def unpack_grads(packed):
    lead = packed.shape[:-2]
    tiles = packed.reshape(*lead, 8, 3, 128)
    qk = jnp.concatenate([tiles[..., :48], tiles[..., 64:112]], axis=-1)
    v = jnp.concatenate([tiles[..., 48:64], tiles[..., 112:]], axis=-1)
    return (
        qk[..., :2, :].reshape(*lead, 1536),
        qk[..., 2, :].reshape(*lead, 768),
        v.reshape(*lead, 768),
    )


def spread_rows(rows):
    r = rows.reshape(3, 2, 16, -1)
    z = jnp.zeros_like(r[0, 0])
    return jnp.concatenate(
        [r[1, 1], r[2, 1], z, r[0, 0], r[1, 0], r[2, 0], z, r[0, 1]], axis=0
    )


class Place:
    def __init__(self):
        self.z, self.core = lax.axis_index("z"), lax.axis_index("core")
        self.x, self.yh, self.yl = lax.axis_index("x"), lax.axis_index("yh"), lax.axis_index("yl")
        self.y = self.yh * 2 + self.yl
        self.c = self.x * 2 + self.yh
        self.zp, self.zm, self.zo = (lax.rem(self.z + k, 4) for k in (1, 3, 2))
        self.oc = 1 - self.core

    def near(self, axis, k):
        if axis == "x":
            return {"x": lax.rem(self.x + k, 4)}
        return at_y(lax.rem(self.y + k, 4))

    def greet(self, others, mirror=False):
        barrier = pltpu.get_barrier_semaphore()
        for dev in others:
            pl.semaphore_signal(barrier, inc=1, device_id=dev, device_id_type=MESH)
        if not mirror:
            pl.semaphore_wait(barrier, len(others))
            return

        @pl.when(self.x != self.z)
        def _():
            there = {"x": self.z, "z": self.x}
            pl.semaphore_signal(barrier, inc=1, device_id=there, device_id_type=MESH)
            pl.semaphore_wait(barrier, len(others) + 1)

        @pl.when(self.x == self.z)
        def _():
            pl.semaphore_wait(barrier, len(others))

    def layer_partners(self):
        return (
            [{"z": self.zp}, {"z": self.zm}, {"core": self.oc}]
            + [at_ctx(lax.rem(self.c + k, 8)) for k in range(1, 8)]
            + [{"yl": 1 - self.yl}, {"yh": 1 - self.yh, "yl": 1 - self.yl}]
        )


def at_y(y):
    return {"yh": y // 2, "yl": lax.rem(y, 2)}


def at_ctx(c):
    return {"x": c // 2, "yh": lax.rem(c, 2)}


def span_of(start, size):
    return pl.ds(pl.multiple_of(start, 64), size)


def slot_rows(zz, cc, half=None):
    base = (zz * 2 + cc) * 128
    return span_of(base, 128) if half is None else span_of(base + 64 * half, 64)


def all_gather(me, buf, ssem, rsem, on_pair, hooks=()):
    z, zp, zm, zo, core, oc = me.z, me.zp, me.zm, me.zo, me.core, me.oc
    up, down, across = {"z": zp}, {"z": zm}, {"core": oc}
    sent = [
        (z, core, 0, up), (z, core, 1, up), (z, core, 1, down), (z, core, 0, down),
        (zm, core, 0, up), (zp, core, 1, down), (z, core, None, across),
        (zm, core, 0, across), (zm, core, 1, across), (zp, core, 1, across), (zp, core, 0, across),
        (zo, core, 0, across), (zo, core, 1, across),
    ]
    come = [
        (zm, core, 0), (zm, core, 1), (zp, core, 1), (zp, core, 0), (zo, core, 0), (zo, core, 1),
        (z, oc, None), (zm, oc, 0), (zm, oc, 1), (zp, oc, 1), (zp, oc, 0), (zo, oc, 0), (zo, oc, 1),
    ]

    def copy(i, rows, dev):
        return pltpu.make_async_remote_copy(
            src_ref=buf.at[rows], dst_ref=buf.at[rows], send_sem=ssem.at[i], recv_sem=rsem.at[i],
            device_id=dev, device_id_type=MESH,
        )

    def send(*which):
        for i in which:
            copy(i, slot_rows(*sent[i][:3]), sent[i][3]).start()

    def arrive(*which):
        for i in which:
            copy(i, slot_rows(*come[i]), sent[i][3]).wait_recv()

    def hook(i):
        if i < len(hooks):
            hooks[i]()

    send(0, 2, 1, 3, 6)
    hook(0)
    arrive(6)
    on_pair(z)
    arrive(0)
    send(4, 7)
    arrive(2)
    send(5, 9)
    hook(1)
    arrive(1)
    send(8)
    arrive(3)
    send(10)
    hook(2)
    arrive(7, 8)
    on_pair(zm)
    arrive(9, 10)
    on_pair(zp)
    hook(3)
    arrive(4)
    send(11)
    arrive(5)
    send(12)
    arrive(11, 12)
    on_pair(zo)

    def finish():
        for i in range(13):
            copy(i, slot_rows(*sent[i][:3]), sent[i][3]).wait_send()

    return finish


def reduce_scatter(me, part, parts, give, take, ring_out, ring_in, ssem, rsem, fill=lambda n: None):
    z, zp, zm, zo, core, oc = me.z, me.zp, me.zm, me.zo, me.core, me.oc
    up, down, across = {"z": zp}, {"z": zm}, {"core": oc}
    mine = span_of(core * 128, 128)
    theirs = span_of(oc * 128, 128)

    def swap(k):
        return pltpu.make_async_remote_copy(
            src_ref=give.at[k], dst_ref=take.at[k], send_sem=ssem.at[k], recv_sem=rsem.at[k],
            device_id=across, device_id_type=MESH,
        )

    def ring(i):
        return pltpu.make_async_remote_copy(
            src_ref=ring_out.at[i], dst_ref=ring_in.at[i], send_sem=ssem.at[4 + i], recv_sem=rsem.at[4 + i],
            device_id=up if i < 3 else down, device_id_type=MESH,
        )

    def make(k, zz):
        parts[k] = part(zz)
        give[k] = parts[k, theirs].astype(BF)
        swap(k).start()

    def merged(k, half):
        rows = span_of(core * 128 + 64 * half, 64)
        return parts[k, rows] + take[k, 64 * half : 64 * half + 64].astype(F32)

    def push(i, value):
        ring_out[i] = value.astype(BF)
        ring(i).start()

    make(0, zo)
    make(1, zp)
    swap(0).wait_recv()
    push(0, merged(0, 0))
    push(3, merged(0, 1))
    make(2, zm)
    swap(1).wait_recv()
    push(1, merged(1, 1))
    swap(2).wait_recv()
    push(4, merged(2, 0))
    make(3, z)
    fill(0)
    ring(0).wait_recv()
    push(2, merged(1, 0) + ring_in[0].astype(F32))
    ring(3).wait_recv()
    push(5, merged(2, 1) + ring_in[3].astype(F32))
    swap(3).wait_recv()
    fill(1)
    own = [merged(3, 0), merged(3, 1)]
    ring(1).wait_recv()
    own[1] = own[1] + ring_in[1].astype(F32)
    ring(4).wait_recv()
    own[0] = own[0] + ring_in[4].astype(F32)
    fill(2)
    ring(2).wait_recv()
    own[0] = own[0] + ring_in[2].astype(F32)
    ring(5).wait_recv()
    own[1] = own[1] + ring_in[5].astype(F32)

    def finish():
        for k in range(4):
            swap(k).wait_send()
        for i in range(6):
            ring(i).wait_send()

    return jnp.concatenate(own, axis=0), finish


class Exchange:
    def __init__(self, me, src, dst, ssem, rsem):
        self.me, self.src, self.dst, self.ssem, self.rsem = me, src, dst, ssem, rsem

    def copy(self, s, come):
        return pltpu.make_async_remote_copy(
            src_ref=self.src.at[span_of(s * 128, 128)], dst_ref=self.dst.at[span_of(come * 128, 128)],
            send_sem=self.ssem.at[s], recv_sem=self.rsem.at[come],
            device_id=at_ctx(s), device_id_type=MESH,
        )

    def send(self, s):
        c = self.me.c

        @pl.when(s != c)
        def _():
            self.copy(s, c).start()

        @pl.when(s == c)
        def _():
            rows = span_of(s * 128, 128)
            self.dst[rows] = self.src[rows]

    def arrive(self):
        @pl.loop(1, 8)
        def _(k):
            there = lax.rem(self.me.c + k, 8)
            self.copy(there, there).wait_recv()

    def finish(self):
        @pl.loop(1, 8)
        def _(k):
            there = lax.rem(self.me.c + k, 8)
            self.copy(there, self.me.c).wait_send()


def push(src, dst, ssem, rsem, dev):
    return pltpu.make_async_remote_copy(
        src_ref=src, dst_ref=dst, send_sem=ssem, recv_sem=rsem, device_id=dev, device_id_type=MESH
    )


class Gather:
    def __init__(self, me, src, dst, ssem, rsem, loc, order):
        self.me, self.src, self.dst, self.ssem, self.rsem, self.order = me, src, dst, ssem, rsem, order
        x, yh, yl = me.x, me.yh, me.yl
        self.own = lambda: pltpu.make_async_copy(src.at[me.core], dst.at[me.core, x, yh, yl], loc)
        self.cross = lambda: push(
            src.at[me.oc], dst.at[me.core, x, yh, yl], ssem.at[0], rsem.at[0], {"core": me.oc}
        )

    def region(self, stage, k):
        me = self.me
        if stage == 0:
            back = 4 - k
            x = lax.rem(me.x + back, 4) if self.order[0] == "x" else me.x
            y = lax.rem(me.y + back, 4) if self.order[0] == "y" else me.y
            return self.dst.at[:, x, y // 2, lax.rem(y, 2)]
        if self.order[1] == "y":
            y = lax.rem(me.y + 4 - k, 4)
            return self.dst.at[:, :, y // 2, lax.rem(y, 2)]
        return self.dst.at[:, lax.rem(me.x + 4 - k, 4)]

    def copy(self, stage, k, come):
        ref = self.region(stage, k if come else 0)
        i = 1 + 3 * stage + k - 1
        return push(ref, ref, self.ssem.at[i], self.rsem.at[i], self.me.near(self.order[stage], k))

    def zero(self):
        self.own().start()
        self.cross().start()

    def one(self):
        me = self.me
        self.own().wait()
        here = self.dst.at[me.oc, me.x, me.yh, me.yl]
        push(here, here, self.ssem.at[0], self.rsem.at[0], {"core": me.oc}).wait_recv()
        for k in (2, 1, 3):
            self.copy(0, k, False).start()

    def two(self):
        for k in (1, 3, 2):
            self.copy(0, k, True).wait_recv()
        for k in (2, 1, 3):
            self.copy(1, k, False).start()

    def three(self):
        for k in (1, 3, 2):
            self.copy(1, k, True).wait_recv()

    def finish(self):
        self.cross().wait_send()
        for stage in (0, 1):
            for k in (1, 2, 3):
                self.copy(stage, k, False).wait_send()


class OutGather:
    def __init__(self, me, src, dst, ssem, rsem, loc):
        self.me, self.dst, self.ssem, self.rsem = me, dst, ssem, rsem
        self.own = pltpu.make_async_copy(src, dst.at[me.y], loc)
        self.far = lax.rem(me.x + 4 - me.z, 4)

    def copy(self, stage, k, come):
        me = self.me
        y = lax.rem(me.y + 4 - k, 4) if stage and come else me.y
        ref, i = self.dst.at[y], 3 * stage + k - 1
        return push(ref, ref, self.ssem.at[i], self.rsem.at[i], me.near("xy"[stage], k))

    def zero(self):
        @pl.when(self.far == 0)
        def _():
            self.own.start()

    def one(self):
        @pl.when(self.far == 0)
        def _():
            self.own.wait()
            for k in (2, 1, 3):
                self.copy(0, k, False).start()

    def two(self):
        for k in (1, 2, 3):

            @pl.when(self.far == k)
            def _(k=k):
                self.copy(0, k, True).wait_recv()

        for k in (2, 1, 3):
            self.copy(1, k, False).start()

    def three(self):
        for k in (1, 3, 2):
            self.copy(1, k, True).wait_recv()

    def finish(self):
        @pl.when(self.far == 0)
        def _():
            for k in (1, 2, 3):
                self.copy(0, k, False).wait_send()

        for k in (1, 2, 3):
            self.copy(1, k, False).wait_send()


class Reduce:
    def __init__(self, me, quarter, inner, mine, got1, sum1, got2, ssem, rsem, loc, order):
        self.me, self.quarter, self.inner, self.order = me, quarter, inner, order
        self.mine, self.got1, self.sum1, self.got2, self.ssem, self.rsem = mine, got1, sum1, got2, ssem, rsem
        self.load = pltpu.make_async_copy(quarter(order[0], self.at(order[0], 0)), mine, loc)

    def at(self, axis, k):
        return lax.rem((self.me.x if axis == "x" else self.me.y) + k, 4)

    def copy(self, stage, k):
        axis = self.order[stage]
        to = self.at(axis, k)
        src = self.inner(self.sum1, to) if stage else self.quarter(axis, to)
        dst = (self.got2 if stage else self.got1).at[k - 1]
        i = 3 * stage + k - 1
        return push(src, dst, self.ssem.at[i], self.rsem.at[i], self.me.near(axis, k))

    def one(self):
        self.load.start()
        for k in (2, 1, 3):
            self.copy(0, k).start()

    def two(self):
        self.load.wait()
        for k in (1, 2, 3):
            self.copy(0, k).wait_recv()
        lead = math.prod(self.sum1.shape[:-2])
        dims = self.sum1.shape[:-2]

        @pl.loop(0, lead)
        def _(n):
            at = []
            for d in reversed(dims):
                at.insert(0, lax.rem(n, d))
                n = n // d
            at = tuple(at)
            total = self.mine[at].astype(F32)
            for k in range(3):
                total = total + self.got1[(k, *at)].astype(F32)
            self.sum1[at] = total.astype(self.sum1.dtype)

        for k in (2, 1, 3):
            self.copy(1, k).start()

    def three(self):
        for k in (1, 2, 3):
            self.copy(1, k).wait_recv()
        total = self.inner(self.sum1, self.at(self.order[1], 0))[...].astype(F32)
        for k in range(3):
            total = total + self.got2[k].astype(F32)
        return total

    def finish(self):
        for stage in (0, 1):
            for k in (1, 2, 3):
                self.copy(stage, k).wait_send()


def lane_masks(rows):
    lane = lax.broadcasted_iota(jnp.int32, (rows, 128), 1)
    v0 = ((lane >= 48) & (lane < 64)) | (lane >= 112)
    v1 = ((lane >= 64) & (lane < 80)) | (lane < 16)
    v2 = ((lane >= 80) & (lane < 96)) | ((lane >= 16) & (lane < 32))
    return v0, v1, v2


def split_packed(packed, key_ref, value_ref):
    v0, v1, v2 = lane_masks(128)

    @pl.loop(0, 8)
    def _(p):
        rows = span_of(p * 128, 128)
        t0, t1, t2 = (packed[rows, 128 * t : 128 * t + 128].astype(F32) for t in range(3))
        key_ref[rows] = jnp.where(v0, 0.0, t2).astype(BF)
        value = jnp.where(v0, t0, 0.0)
        value = value + jnp.where(v1, pltpu.roll(t1, 16, 1), 0.0)
        value = value + jnp.where(v2, pltpu.roll(t2, 32, 1), 0.0)
        value_ref[rows] = value.astype(BF)


def flip(ref):
    return jnp.transpose(ref[...].astype(F32)).astype(BF)


def stacked(ref, rows):
    return jnp.concatenate([ref[rows, 0:128], ref[rows, 128:256]], axis=0)


def rms_of(values):
    return lax.rsqrt(jnp.mean(values * values, axis=-1, keepdims=True) + EPS)


def fwd_kernel(
    first, stream, gains_in, cos, sin, pcol, prow, s_gain, s_in, s_o, s_g, s_u, s_d,
    o_stream, o_middle, o_lse, o_gains, o_normed, o_qkv, o_mixed, o_nmlp, o_gate, o_up, o_hidden,
    o_win, o_wo, o_wg, o_wu, o_wd,
    w_in, w_o, w_g, w_u, w_d, w_gain, buf1, buf2, qs, qr, ms, mr, gate_v, up_v, hid, keys, vals, vals_t, middle,
    parts, give, take, ring_out, ring_in,
    ag_s, ag_r, ag2_s, ag2_r, rs_s, rs_r, rs2_s, rs2_r, ax_s, ax_r, bx_s, bx_r, loc, loc2, ga_s, ga_r,
):
    me = Place()
    stores = []

    def store(src, dst):
        stores.append(pltpu.make_async_copy(src, dst, loc2.at[len(stores)]))
        stores[-1].start()

    items = ((s_in, w_in, "xy"), (s_g, w_g, "xy"), (s_u, w_u, "yx"), (s_d, w_d, "xy"), (s_gain, w_gain, "yx"))
    g_in, g_g, g_u, g_d, g_gain = (
        Gather(me, s, d, ga_s.at[i], ga_r.at[i], loc.at[i], order) for i, (s, d, order) in enumerate(items)
    )
    g_o = OutGather(me, s_o, w_o, ga_s.at[5], ga_r.at[5], loc.at[5])
    own_rows = slot_rows(me.z, me.core)
    if first:
        buf2[own_rows] = stream[...]
    else:
        o_gains[...] = gains_in[...]
        s = stream[...]
        buf1[own_rows] = (s * rms_of(s) * gains_in[0:1, :]).astype(BF)
    me.greet(me.layer_partners())
    if first:
        g_gain.zero()
    g_in.zero()
    g_o.zero()
    g_g.zero()
    g_u.zero()
    g_d.zero()

    def hook0():
        if first:
            g_gain.one()
        g_in.one()

    def hook1():
        if first:
            g_gain.two()
        g_in.two()

    def hook2():
        g_o.one()

    def skip(zz):
        pass

    done_ag = all_gather(me, buf2 if first else buf1, ag_s, ag_r, skip, (hook0, hook1, hook2))
    if first:
        g_gain.three()
        o_gains[...] = jnp.zeros_like(o_gains)
        for owner in range(16):
            base = 96 * owner // 128 * 128
            width = min(256, WIDE - base)
            row = w_gain[owner // 8, owner % 8 // 2, owner % 2, 0]
            o_gains[:, base : base + width] += row[:, :width]

        @pl.loop(0, 8)
        def _(p):
            rows = span_of(p * 128, 128)
            s = buf2[rows].astype(F32)
            buf1[rows] = (s * rms_of(s) * o_gains[0:1, :]).astype(BF)

    done_ag()

    ax = Exchange(me, qs, qr, ax_s, ax_r)
    g_in.three()

    @pl.loop(0, 4)
    def _(k):
        zz = lax.rem(me.z + k, 4)
        rows = span_of(zz * 256, 256)
        y = mm(buf1[rows], w_in[...].reshape(WIDE, 384))
        for t in range(3):
            tile = y[:, 128 * t : 128 * t + 128]
            tile = tile * cos[...] + pltpu.roll(tile, 64, 1) * sin[...]
            qs[rows, 128 * t : 128 * t + 128] = tile.astype(BF)
        ax.send(zz * 2)
        ax.send(zz * 2 + 1)

    g_o.two()
    g_g.one()
    g_u.one()
    ax.arrive()
    store(buf1, o_normed)
    store(qr, o_qkv)
    split_packed(qr, keys, vals)
    vals_t[...] = flip(vals)
    bx = Exchange(me, ms, mr, bx_s, bx_r)

    @pl.loop(0, 8)
    def _(k):
        p = lax.rem(me.c + 1 + k, 8)
        rows = span_of(p * 128, 128)
        q = stacked(qr, rows)
        scores = mm_nt(keys[...], q) * SCALE
        scores = jnp.where(pcol[...] <= prow[pl.ds(p, 1), :], scores, -1e30)
        top = jnp.max(scores, axis=0, keepdims=True)
        weights = jnp.exp(scores - top)
        total = jnp.sum(weights, axis=0, keepdims=True)
        o_lse[pl.ds(p, 1), :] = top + jnp.log(total)
        probs = (weights / total).astype(BF)
        out = jnp.transpose(mm(vals_t[...], probs)).astype(BF)
        ms[rows, 0:128] = out[0:128]
        ms[rows, 128:256] = out[128:256]
        bx.send(p)

    g_g.two()
    g_u.two()
    g_d.one()
    g_o.three()
    bx.arrive()
    store(mr, o_mixed)

    def out_part(zz):
        return mm(mr[span_of(zz * 256, 256)], w_o[...].reshape(256, WIDE))

    rs = (parts, give, take, ring_out, ring_in)
    total, done_rs = reduce_scatter(me, out_part, *rs, rs_s, rs_r)
    mid = total + (stream[...].astype(F32) if first else stream[...])
    middle[...] = mid
    o_middle[...] = mid
    buf2[own_rows] = (mid * rms_of(mid) * o_gains[1:2, :]).astype(BF)
    waited = []

    def gated(zz):
        if not waited:
            g_g.three()
            g_u.three()
            waited.append(1)
        rows = span_of(zz * 256, 256)
        gate = mm(buf2[rows], w_g[...].reshape(WIDE, 512))
        gate_v[rows] = gate
        up = mm(buf2[rows], w_u[...].reshape(WIDE, 512))
        up_v[rows] = up
        hid[rows] = (gate / (1.0 + jnp.exp(-gate)) * up).astype(BF)

    done_ag2 = all_gather(me, buf2, ag2_s, ag2_r, gated, (g_d.two,))
    store(buf2, o_nmlp)
    store(gate_v, o_gate)
    store(up_v, o_up)
    store(hid, o_hidden)
    g_d.three()
    done_rs()
    for w, o in ((w_in, o_win), (w_o, o_wo), (w_g, o_wg), (w_u, o_wu), (w_d, o_wd)):
        store(w, o)

    def down_part(zz):
        return mm(hid[span_of(zz * 256, 256)], w_d[...].reshape(512, WIDE))

    total, done_rs2 = reduce_scatter(me, down_part, *rs, rs2_s, rs2_r)
    o_stream[...] = middle[...] + total
    for done in (ax.finish, bx.finish, done_ag2, done_rs2):
        done()
    for item in (g_in, g_g, g_u, g_d, g_o) + ((g_gain,) if first else ()):
        item.finish()
    for item in stores:
        item.wait()


def norm_back_of(e, values, gain):
    q = rms_of(values)
    n = values * q
    dn = e * gain
    part = q * (dn - n * jnp.mean(dn * n, axis=-1, keepdims=True))
    return part, jnp.sum(e * n, axis=0, keepdims=True)


def bwd_kernel(
    grad, stream, middle, gains, cos, sin, pcol, prow, lse,
    h_in, h_o, h_g, h_u, h_d, h_qkv, h_gate, h_up, h_normed, h_mixed, h_nmlp, h_hidden,
    o_grad, o_gains, o_din, o_dgu, o_dd, o_do,
    w_in, w_o, w_g, w_u, w_d, buf1, buf2, qr, gate_v, up_v, gu, mgs, mgr, keys, vals, keys_t, dk, dv,
    dqs, ps, pr, mid_grad, normed, mixed, nmlp, hid, d_in, d_gu, d_d, d_o,
    parts, give, take, ring_out, ring_in,
    ag_s, ag_r, ag2_s, ag2_r, rs_s, rs_r, rs2_s, rs2_r, ax_s, ax_r, bx_s, bx_r, loc, loc2,
):
    me = Place()
    pairs = (
        (h_d, w_d), (h_gate, gate_v), (h_up, up_v), (h_g, w_g), (h_u, w_u), (h_o, w_o), (h_qkv, qr), (h_in, w_in),
        (h_hidden, hid), (h_nmlp, nmlp), (h_mixed, mixed), (h_normed, normed),
    )
    loads = [pltpu.make_async_copy(h, v, loc.at[i]) for i, (h, v) in enumerate(pairs)]
    for load in loads:
        load.start()
    stores = []

    def store(src, dst):
        stores.append(pltpu.make_async_copy(src, dst, loc2.at[len(stores)]))
        stores[-1].start()

    own_rows = slot_rows(me.z, me.core)
    buf1[own_rows] = grad[...].astype(BF)
    me.greet(me.layer_partners())
    for load in loads[:3]:
        load.wait()

    def unit(zz):
        rows = span_of(zz * 256, 256)
        hg = mm_nt(buf1[rows], w_d[...])
        gate, up = gate_v[rows], up_v[rows]
        sig = 1.0 / (1.0 + jnp.exp(-gate))
        gu[rows, 0:512] = (hg * up * (sig * (1.0 + gate * (1.0 - sig)))).astype(BF)
        gu[rows, 512:1024] = (hg * (gate * sig)).astype(BF)

    done_ag = all_gather(me, buf1, ag_s, ag_r, unit)
    for load in loads[3:]:
        load.wait()

    def mlp_part(zz):
        rows = span_of(zz * 256, 256)
        return mm_nt(gu[rows, 0:512], w_g[...]) + mm_nt(gu[rows, 512:1024], w_u[...])

    def grad_down(b):
        cols = slice(256 * b, 256 * b + 256)
        d_d[cols] = mm_tn(hid[:, cols], buf1[...]).astype(BF)

    def grad_gu(b):
        cols = slice(256 * b, 256 * b + 256)
        d_gu[cols] = mm_tn(nmlp[:, cols], gu[...]).astype(BF)

    def fill1(n):
        if n == 0:
            grad_down(0)
            grad_down(1)
        elif n == 1:
            grad_gu(0)
            grad_gu(1)
        else:
            grad_gu(2)
            grad_gu(3)

    rs = (parts, give, take, ring_out, ring_in)
    e, done_rs = reduce_scatter(me, mlp_part, *rs, rs_s, rs_r, fill1)
    part, gain_part = norm_back_of(e, middle[...], gains[1:2, :])
    o_gains[1:2, :] = gain_part
    gm = grad[...] + part
    mid_grad[...] = gm
    buf2[own_rows] = gm.astype(BF)
    ax = Exchange(me, mgs, mgr, ax_s, ax_r)

    def mixed_back(zz):
        rows = span_of(zz * 256, 256)
        mgs[rows] = mm_nt(buf2[rows], w_o[...]).astype(BF)
        ax.send(zz * 2)
        ax.send(zz * 2 + 1)

    def hook0():
        split_packed(qr, keys, vals)
        keys_t[...] = flip(keys)
        dk[...] = jnp.zeros_like(dk)
        dv[...] = jnp.zeros_like(dv)

    def hook2():
        grad_gu(4)
        grad_gu(5)

    done_ag2 = all_gather(me, buf2, ag2_s, ag2_r, mixed_back, (hook0, lambda: None, hook2))
    store(d_d, o_dd)
    store(d_gu, o_dgu)
    lanes = mm_tn(mixed[...], buf2[...])
    for head in range(2):
        chunk = [lanes[128 * head + 16 * c : 128 * head + 16 * c + 16] for c in (3, 7, 4, 0, 5, 1)]
        for b in range(8):
            first, shift = 12 * b // 16, 12 * b % 16
            piece = chunk[first][shift:]
            if shift > 4:
                piece = jnp.concatenate([piece, chunk[first + 1][: shift - 4]], axis=0)
            d_o[head, b // 4, b % 4] = padded(piece[0:12])
    store(d_o, o_do)
    ax.arrive()

    @pl.loop(0, 8)
    def _(p):
        rows = span_of(p * 128, 128)
        q = stacked(qr, rows)
        mg = stacked(mgr, rows)
        scores = mm_nt(keys[...], q) * SCALE
        allowed = pcol[...] <= prow[pl.ds(p, 1), :]
        probs = jnp.where(allowed, jnp.exp(scores - lse[pl.ds(p, 1), :]), 0.0)
        pg = mm_nt(vals[...], mg)
        inner = jnp.sum(probs * pg, axis=0, keepdims=True)
        sg = (probs * (pg - inner)).astype(BF)
        dk[...] += mm(sg, q)
        dv[...] += mm(probs.astype(BF), mg)
        dq = jnp.transpose(mm(keys_t[...], sg)) * SCALE
        dqs[rows, 0:128] = dq[0:128]
        dqs[rows, 128:256] = dq[128:256]

    bx = Exchange(me, ps, pr, bx_s, bx_r)
    v0, _, _ = lane_masks(128)

    @pl.loop(0, 8)
    def _(k):
        p = lax.rem(me.c + 1 + k, 8)
        rows = span_of(p * 128, 128)
        value = dv[rows]
        ps[rows, 0:128] = jnp.where(v0, value, dqs[rows, 0:128]).astype(BF)
        ps[rows, 128:256] = jnp.where(v0, pltpu.roll(value, 112, 1), dqs[rows, 128:256]).astype(BF)
        ps[rows, 256:384] = jnp.where(v0, pltpu.roll(value, 96, 1), dk[rows] * SCALE).astype(BF)
        bx.send(p)

    done_rs()
    bx.arrive()
    pre = qr

    def in_part(zz):
        rows = span_of(zz * 256, 256)
        for t in range(3):
            cols = slice(128 * t, 128 * t + 128)
            tile = pr[rows, cols].astype(F32)
            pre[rows, cols] = (tile * cos[...] - pltpu.roll(tile, 64, 1) * sin[...]).astype(BF)
        return mm_nt(pre[rows], w_in[...])

    def fill2(n):
        for b in (2 * n, 2 * n + 1):
            cols = slice(256 * b, 256 * b + 256)
            d_in[cols] = mm_tn(normed[:, cols], pre[...]).astype(BF)

    e, done_rs2 = reduce_scatter(me, in_part, *rs, rs2_s, rs2_r, fill2)
    store(d_in, o_din)
    part, gain_part = norm_back_of(e, stream[...].astype(F32), gains[0:1, :])
    o_gains[0:1, :] = gain_part
    o_grad[...] = mid_grad[...] + part
    for done in (done_ag, done_ag2, ax.finish, bx.finish, done_rs2):
        done()
    for item in stores:
        item.wait()


def padded(rows):
    return jnp.concatenate([rows, jnp.zeros((4, rows.shape[1]), F32)], axis=0).astype(BF)


def reduce_specs(d_in, d_gu, d_d, d_o):
    def split(ref, lo, hi, r, order):
        cols = slice(lo, hi)

        def quarter(axis, i):
            if axis == "x":
                return ref.at[:, i, :, :, :, cols]
            return ref.at[:, :, i // 2, lax.rem(i, 2), :, cols]

        def inner(s, i):
            return s.at[:, i] if order == "yx" else s.at[:, i // 2, lax.rem(i, 2)]

        lead = (2, 4) if order == "yx" else (2, 2, 2)
        return quarter, inner, order, lead + (r, hi - lo), (2, r, hi - lo)

    def out_quarter(axis, i):
        return d_o.at[i // 2, lax.rem(i, 2)]

    return [
        split(d_gu, 0, 512, 48, "yx"),
        split(d_gu, 512, 1024, 48, "xy"),
        split(d_d, 0, 768, 16, "yx"),
        split(d_d, 768, 1536, 16, "xy"),
        split(d_in, 0, 384, 48, "yx"),
        (out_quarter, lambda s, i: s.at[i], "yx", (4, 16, WIDE), (16, WIDE)),
    ]


def reduce_scratch():
    out = []
    for _, _, _, big, small in reduce_specs(None, None, None, None):
        out += [vm(big), vm((3,) + big), vm(big), vm((3,) + small)]
    return out


def grads_kernel(layers, *refs):
    parts, gains = refs[: 4 * layers], refs[4 * layers]
    o_rows, o_down, o_out, o_gains = refs[4 * layers + 1 : 4 * layers + 5]
    scratch = list(refs[4 * layers + 5 :])
    n_red = 6 * layers
    red_scratch, scratch = scratch[: 4 * n_red], scratch[4 * n_red :]
    fin_s, fin_r, down_s, down_r, out_s, out_r, sum_a, sum_b, got_a, got_b, got_c = scratch[:11]
    red_s, red_r, loc, fin_ss, fin_rs, gain_s, gain_r, down_ss, down_rs, out_ss = scratch[11:]
    me = Place()
    reds = []
    for l in range(layers):
        for quarter, inner, order, _, _ in reduce_specs(*parts[4 * l : 4 * l + 4]):
            n = len(reds)
            reds.append(
                Reduce(me, quarter, inner, *red_scratch[4 * n : 4 * n + 4], red_s.at[n], red_r.at[n], loc.at[n], order)
            )
    group = [(k, c) for k in range(4) for c in range(2) if k or c]

    def mate(k, c):
        return {"z": lax.rem(me.z + k, 4), "core": lax.rem(me.core + c, 2)}

    mirror = {"x": me.z, "z": me.x}
    apart = me.x != me.z
    me.greet(
        [me.near("x", k) for k in (1, 2, 3)] + [me.near("y", k) for k in (1, 2, 3)]
        + [mate(*m) for m in group] + [{"yl": 1 - me.yl, "core": me.oc}],
        mirror=True,
    )

    def gain_copy(stage, axis, src, got, k):
        i = 3 * stage + k - 1
        return push(src, got.at[k - 1], gain_s.at[i], gain_r.at[i], me.near(axis, k))

    def gain_sum(stage, axis, src, got, dst):
        total = src[...]
        for k in (1, 2, 3):
            gain_copy(stage, axis, src, got, k).wait_recv()
            total = total + got[k - 1]
        dst[...] = total

    for k in (1, 2, 3):
        gain_copy(0, "y", gains, got_a, k).start()
    for red in reds:
        red.one()
    gain_sum(0, "y", gains, got_a, sum_a)
    for k in (1, 2, 3):
        gain_copy(1, "x", sum_a, got_b, k).start()
    for red in reds:
        red.two()
    gain_sum(1, "x", sum_a, got_b, sum_b)

    def gain_mate(i):
        return push(sum_b, got_c.at[i], gain_s.at[6 + i], gain_r.at[6 + i], mate(*group[i]))

    for i in range(7):
        gain_mate(i).start()
    for l in range(layers):
        gate, up, down_a, down_b, first, out = reds[6 * l : 6 * l + 6]
        for lo, hi, red in ((384, 896, gate), (896, 1408, up), (0, 384, first)):
            total = red.three()
            for dp in range(2):
                for z in range(4):
                    fin_s[dp, z, l, :, lo:hi] = padded(total[dp, 12 * z : 12 * z + 12])
        down_s[:, l, :, 0:768] = down_a.three().astype(BF)
        down_s[:, l, :, 768:1536] = down_b.three().astype(BF)
        out_s[l] = out.three().astype(BF)

    slot = me.z * 2 + me.core

    def fin(i, come):
        k, c = group[i]
        to_z, to_core = lax.rem(me.z + k, 4), lax.rem(me.core + c, 2)
        from_z = lax.rem(me.z + 4 - k, 4)
        dst = fin_r.at[from_z * 2 + to_core] if come else fin_r.at[slot]
        return push(fin_s.at[to_core, to_z], dst, fin_ss.at[i], fin_rs.at[i], mate(k, c))

    def down(dp, half):
        dev = {"core": jnp.int32(dp), "yl": me.core}
        return push(down_s.at[dp], down_r.at[half], down_ss.at[dp], down_rs.at[half], dev)

    mine = me.yl == me.core

    def out_copy():
        return push(out_s, out_r, out_ss.at[0], out_ss.at[1], mirror)

    for i in range(7):
        fin(i, False).start()
    for dp in range(2):
        keep = mine & (me.core == dp)

        @pl.when(jnp.logical_not(keep))
        def _(dp=dp):
            down(dp, me.yl).start()

        @pl.when(keep)
        def _(dp=dp):
            down_r[me.yl] = down_s[dp]

    @pl.when(apart)
    def _():
        out_copy().start()

    @pl.when(jnp.logical_not(apart))
    def _():
        out_r[...] = out_s[...]

    fin_r[slot] = fin_s[me.core, me.z]
    total = sum_b[...]
    for i in range(7):
        gain_mate(i).wait_recv()
        total = total + got_c[i]
    o_gains[...] = total
    for i in range(7):
        fin(i, True).wait_recv()
    o_rows[...] = fin_r[...]
    for half in range(2):

        @pl.when(jnp.logical_not(mine & (me.yl == half)))
        def _(half=half):
            down(0, half).wait_recv()

    o_down[...] = down_r[...]

    @pl.when(apart)
    def _():
        out_copy().wait_recv()

    o_out[...] = out_r[...]
    for red in reds:
        red.finish()
    for k in (1, 2, 3):
        gain_copy(0, "y", gains, got_a, k).wait_send()
        gain_copy(1, "x", sum_a, got_b, k).wait_send()
    for i in range(7):
        gain_mate(i).wait_send()
        fin(i, False).wait_send()
    for dp in range(2):

        @pl.when(jnp.logical_not(mine & (me.core == dp)))
        def _(dp=dp):
            down(dp, me.yl).wait_send()

    @pl.when(apart)
    def _():
        out_copy().wait_send()


def vm(shape, dtype=BF):
    return pltpu.VMEM(shape, dtype)


def rs_scratch():
    return [vm((4, 128, WIDE)), vm((4, 128, WIDE)), vm((6, 64, WIDE)), vm((6, 64, WIDE))]


def dma(*shape):
    return pltpu.SemaphoreType.DMA(shape)


def sems():
    return [dma(n) for n in (13, 13, 13, 13, 10, 10, 10, 10, 8, 8, 8, 8, 12, 16)]


WEIGHTS = [(WIDE, 384), (256, WIDE), (WIDE, 512), (WIDE, 512), (512, WIDE)]
SPLIT = [(2, 4, 2, 2, 48, 384), (4, 64, WIDE), (2, 4, 2, 2, 48, 512), (2, 4, 2, 2, 48, 512), (2, 4, 2, 2, 16, WIDE)]


def run_kernel(kernel, name, cid, ins, in_vmem, outs, out_vmem, scratch, flops):
    place = {True: pltpu.VMEM, False: pl.ANY}
    return pl.pallas_call(
        kernel,
        name=name,
        out_shape=[jax.ShapeDtypeStruct(s, d) for s, d in outs],
        in_specs=[pl.BlockSpec(memory_space=place[i < in_vmem]) for i in range(len(ins))],
        out_specs=[pl.BlockSpec(memory_space=place[i < out_vmem]) for i in range(len(outs))],
        scratch_shapes=scratch,
        cost_estimate=pl.CostEstimate(flops=flops, bytes_accessed=60 * 2**20, transcendentals=0),
        compiler_params=pltpu.CompilerParams(
            collective_id=cid, has_side_effects=True, vmem_limit_bytes=60 * 2**20
        ),
    )(*ins)


def layer_fwd(l, stream, gains, cos, sin, pcol, prow, sources):
    outs = [
        ((128, WIDE), F32), ((128, WIDE), F32), ((8, 256), F32), ((8, WIDE), F32),
        ((1024, WIDE), BF), ((1024, 384), BF), ((1024, 256), BF), ((1024, WIDE), BF),
        ((1024, 512), F32), ((1024, 512), F32), ((1024, 512), BF),
    ] + [(s, BF) for s in SPLIT]
    scratch = [vm(s) for s in SPLIT] + [vm((2, 4, 2, 2, 8, 256), F32)] + [
        vm((1024, WIDE)), vm((1024, WIDE)), vm((1024, 384)), vm((1024, 384)), vm((1024, 256)), vm((1024, 256)),
        vm((1024, 512), F32), vm((1024, 512), F32), vm((1024, 512)),
        vm((1024, 128)), vm((1024, 128)), vm((128, 1024)), vm((128, WIDE), F32), vm((4, 256, WIDE), F32),
    ] + rs_scratch() + sems() + [dma(6, 7), dma(6, 7)]
    ins = [stream, gains, cos, sin, pcol, prow, *sources]
    kernel = functools.partial(fwd_kernel, l == 0)
    return run_kernel(kernel, f"layer_forward_{l}", 1 + l, ins, 6, outs, 4, scratch, 40 * 10**9)


def layer_bwd(l, grad, stream, middle, gains, cos, sin, pcol, prow, lse, weights, saved):
    outs = [((128, WIDE), F32), ((8, WIDE), F32), ((WIDE, 384), BF), ((WIDE, 1024), BF), ((512, WIDE), BF), ((2, 2, 4, 16, WIDE), BF)]
    scratch = [vm(s) for s in WEIGHTS] + [
        vm((1024, WIDE)), vm((1024, WIDE)), vm((1024, 384)), vm((1024, 512), F32), vm((1024, 512), F32),
        vm((1024, 1024)), vm((1024, 256)), vm((1024, 256)),
        vm((1024, 128)), vm((1024, 128)), vm((128, 1024)), vm((1024, 128), F32), vm((1024, 128), F32),
        vm((1024, 256), F32), vm((1024, 384)), vm((1024, 384)), vm((128, WIDE), F32),
        vm((1024, WIDE)), vm((1024, 256)), vm((1024, WIDE)), vm((1024, 512)),
        vm((WIDE, 384)), vm((WIDE, 1024)), vm((512, WIDE)), vm((2, 2, 4, 16, WIDE)), vm((4, 256, WIDE), F32),
    ] + rs_scratch() + sems()
    weights = [w.reshape(s) for w, s in zip(weights, WEIGHTS)]
    ins = [grad, stream, middle, gains, cos, sin, pcol, prow, lse, *weights, *saved]
    return run_kernel(bwd_kernel, f"layer_backward_{l}", 3 + l, ins, 9, outs, 2, scratch, 60 * 10**9)


def reduce_grads(parts, gains):
    layers = len(parts) // 4
    outs = [((8, layers, 16, 1408), BF), ((2, layers, 16, WIDE), BF), ((layers, 16, WIDE), BF), ((8, WIDE), F32)]
    scratch = reduce_scratch() * layers + [
        vm((2, 4, layers, 16, 1408)), vm((8, layers, 16, 1408)), vm((2, layers, 16, WIDE)), vm((2, layers, 16, WIDE)),
        vm((layers, 16, WIDE)), vm((layers, 16, WIDE)), vm((8, WIDE), F32), vm((8, WIDE), F32),
        vm((3, 8, WIDE), F32), vm((3, 8, WIDE), F32), vm((7, 8, WIDE), F32),
        dma(6 * layers, 6), dma(6 * layers, 6), dma(6 * layers), dma(7), dma(7), dma(13), dma(13), dma(2), dma(2), dma(2),
    ]
    kernel = functools.partial(grads_kernel, layers)
    place = {True: pltpu.VMEM, False: pl.ANY}
    ins = [*parts, gains]
    return pl.pallas_call(
        kernel,
        name="reduce_gradients",
        out_shape=[jax.ShapeDtypeStruct(s, d) for s, d in outs],
        in_specs=[pl.BlockSpec(memory_space=place[i == 4 * layers]) for i in range(len(ins))],
        out_specs=[pl.BlockSpec(memory_space=pltpu.VMEM) for _ in outs],
        scratch_shapes=scratch,
        compiler_params=pltpu.CompilerParams(collective_id=5, has_side_effects=True, vmem_limit_bytes=60 * 2**20),
    )(*ins)


def body(
    tokens, span_order, attn_gain, w_query, key_matrix, value_matrix, w_out, mlp_gain, w_gate, w_up,
    w_down, cotangent,
):
    rows = tokens.shape[1]
    core, z, yl = lax.axis_index("core"), lax.axis_index("z"), lax.axis_index("yl")
    ctx = lax.axis_index("x") * 2 + lax.axis_index("yh")
    seq_len = 8 * rows
    span = seq_len // span_order.shape[0]
    cos, sin = rope_tables(place_rows(span_order, ctx * rows, rows, span))
    cos, sin = jnp.tile(cos, (2, 1)), jnp.tile(sin, (2, 1))
    places = place_rows(span_order, 0, seq_len, span)
    pcol = places[:, None]
    prow = jnp.tile(places.reshape(8, rows), (1, 2))

    def pick(values, index, axis):
        return lax.dynamic_index_in_dim(values, index, axis=axis, keepdims=False)

    def half(w):
        return lax.dynamic_slice_in_dim(w, yl * 48, 48, axis=1)

    def heads(w, n):
        return pick(half(w).reshape(LAYERS, 48, 2, 4, n), z, 3)

    s_in = pack_heads(heads(w_query, 192), heads(key_matrix, 96), heads(value_matrix, 96)).transpose(0, 2, 1, 3)

    def hidden(w):
        own = pick(half(w).reshape(LAYERS, 48, 16, 2, 4, 32), z, 4)
        return own.transpose(0, 3, 1, 2, 4).reshape(LAYERS, 2, 48, 512)

    s_g, s_u = hidden(w_gate), hidden(w_up)
    s_d = pick(pick(w_down.reshape(LAYERS, 2, 4, 2, 16, WIDE), z, 2), yl, 2)
    s_o = jnp.stack([spread_rows(w_out[l]) for l in range(LAYERS)])
    s_o = lax.dynamic_slice_in_dim(s_o, yl * 64, 64, axis=1)
    own_gains = jnp.concatenate([attn_gain[:1], mlp_gain[:1], attn_gain[1:], mlp_gain[1:]], axis=0).astype(F32)
    s_gain = lax.dynamic_update_slice(jnp.zeros((8, 256), F32), own_gains, (0, lax.rem(96 * (core * 8 + ctx), 128)))
    s_gain = jnp.stack([s_gain, s_gain])

    stream = tokens[0]
    kept = []
    gains = jnp.zeros((8, WIDE), F32)
    for l in range(LAYERS):
        sources = (s_gain, s_in[l], s_o[l], s_g[l], s_u[l], s_d[l])
        outs = layer_fwd(l, stream, gains, cos, sin, pcol, prow, sources)
        kept.append((stream, gains if l else outs[3], outs))
        stream = outs[0]
        gains = outs[3][2:]
        gains = jnp.concatenate([gains, jnp.zeros((2, WIDE), F32)], axis=0)
    block_out = stream.astype(BF)[None]

    g = cotangent[0].astype(F32)
    gain_parts = [None] * LAYERS
    grads = [None] * LAYERS
    for l in reversed(range(LAYERS)):
        stream, gains, outs = kept[l]
        _, middle, lse, _, normed, qkv, mixed, nmlp, gate, up, hid = outs[:11]
        g, gain_parts[l], d_in, d_gu, d_d, d_o = layer_bwd(
            l, g, stream, middle, gains, cos, sin, pcol, prow, lse, outs[11:], (qkv, gate, up, normed, mixed, nmlp, hid)
        )
        grads[l] = (
            d_in.reshape(2, 4, 2, 2, 48, 384), d_gu.reshape(2, 4, 2, 2, 48, 1024), d_d.reshape(2, 4, 2, 2, 16, WIDE), d_o,
        )
    gp = jnp.concatenate([gain_parts[0][:2], gain_parts[1][:2], jnp.zeros((4, WIDE), F32)], axis=0)
    cols, d_d, d_o, gp = reduce_grads(grads[0] + grads[1], gp)
    cols = cols.reshape(4, 2, LAYERS, 16, 1408)[:, :, :, :12].transpose(2, 3, 1, 0, 4).reshape(LAYERS, 12, 8, 1408)
    cols = cols.astype(F32)
    d_q, d_k, d_v = unpack_grads(cols[..., :384])

    def hidden_join(d):
        return d.reshape(LAYERS, 12, 8, 16, 32).transpose(0, 1, 3, 2, 4).reshape(LAYERS, 12, 4096)

    d_g, d_u = hidden_join(cols[..., 384:896]), hidden_join(cols[..., 896:])
    d_d = d_d.transpose(1, 0, 2, 3).reshape(LAYERS, 32, WIDE).astype(F32)
    d_o = d_o[:, :12].astype(F32)
    owner = (core * 8 + ctx) * 8 + yl * 4 + z
    gp = lax.dynamic_slice(gp, (0, owner * 12), (4, 12)).reshape(2, 2, 12)
    return (block_out, g[None], gp[:, 0], d_q, d_k, d_v, d_o, gp[:, 1], d_g, d_u, d_d)


def solution(mesh):
    fine = Mesh(mesh.devices.reshape(2, 4, 2, 2, 4), ALL)
    seq, ctx, own, every = ("core", "yl", "z"), CTX, OWN, ALL
    act = P(seq, ctx, None)
    in_specs = (act, P(), P(None, own)) + (P(None, own, None),) * 4 + (P(None, own),) + (P(None, own, None),) * 3 + (act,)
    grad = P(None, every, None)
    out_specs = (act, act, P(None, every)) + (grad,) * 4 + (P(None, every),) + (grad,) * 3
    return jax.shard_map(body, mesh=fine, in_specs=in_specs, out_specs=out_specs, check_vma=False)
```

time: 1160 us -> 652 us (0.56)
  waiting for transfers between devices: 394 us -> 0 us
  Pallas kernels: 415 us -> 591 us
  blocking collectives: 100 us -> 0 us
  local copies, waits for them, and re-layouts: 139 us -> 39.2 us
  matrix products: 31.9 us -> 0 us
  starting transfers between devices: 20 us -> 0 us
  other arithmetic: 30 us -> 10.7 us
  between operations: 15.6 us -> 1.77 us
    all_gather x5 -> x0, waiting for transfers between devices: 261 us -> none  [the longest x4 193 us: collect(): got = lax.all_gather(rows, OWN, axis=0, tiled=False)]
    pallas_call x0 -> x1, Pallas kernels: none -> 131 us  [reduce_grads(): pl.pallas_call(kernel, name='reduce_gradients', out_shape=[jax.ShapeDtype...]
    unnamed x13 -> x0, waiting for transfers between devices: 127 us -> none
    unnamed x1 -> x0, blocking collectives: 67.5 us -> none
    pallas_call x4, Pallas kernels: 415 us -> 460 us  [run_kernel(): pl.pallas_call(kernel, name=name, out_shape=[jax.ShapeDtypeStruct(s, d) f...]
    transpose x10 -> x2, local copies, waits for them, and re-layouts: 45 us -> 0.09 us  [hidden(): return own.transpose(0, 3, 1, 2, 4).reshape(LAYERS, 2, 48, 512)]
    all_gather x1 -> x0, blocking collectives: 32.8 us -> none  [body(): lax.all_gather(jnp.concatenate([attn_gain, mlp_gain], axis=0), OWN, axis=...]
    dot_general x10 -> x0, matrix products: 31.9 us -> none  [mm_tn(): lax.dot_general(a, b, (((0,), (0,)), ((), ())), preferred_element_type=F32)]
  transfers between devices with their start and end apart: 13 -> 0, of which waited for: 10 -> 0; matrix products, arithmetic and copies ran while one was open for 13% -> 0% of each run, Pallas kernels for 0% -> 0%
where the time goes in v2:
time: 652 us; the launch traced here: 643 us
  Pallas kernels  591 us (91%)
  local copies, waits for them, and re-layouts  39.2 us (6%)
  other arithmetic  10.7 us (2%)
    pallas_call x4, Pallas kernels, run_kernel(): pl.pallas_call(kernel, name=name, out_shape=[jax.ShapeDtypeStruct(s, d) f...  460 us
    pallas_call x1, Pallas kernels, reduce_grads(): pl.pallas_call(kernel, name='reduce_gradients', out_shape=[jax.ShapeDtype...  131 us

profile of v2, /device:TPU:5, one launch (start us, length us, event | category | flops | bytes accessed | tf_op | source)
XLA Modules:
  0.0 643.0 jit_solution(11692286026251757679)
XLA Ops:
  1.3 0.7 select_reduce_fusion.1
  5.0 1.6 dynamic-slice_bitcast_fusion.2
  13.4 0.9 fusion.pcol
  14.6 0.8 slice_bitcast_fusion
  15.3 1.0 bitcast_convert_fusion.grad
  16.8 1.0 constant_dynamic-slice_fusion.1
  17.8 2.0 copy.94
  20.3 0.9 squeeze.115.s_u
  21.6 1.0 squeeze.110.s_u
  22.6 1.0 copy.93
  24.1 1.0 squeeze.114.s_g
  25.4 1.0 squeeze.108.s_g
  27.0 124.4 %layer_forward_0.1 = (f32[128,1536]{1,0:T(8,128)}, f32[128,1536]{1,0:T(8,128)}, f32[8,256]{1,0:T(8,128)}, f32[8,1536]{1,0:T(8,128)}, bf16[1024,1536]{1,0:T(8,128...) custom-call(bf16[128,1536]{1,0:T(8,128)(2,1)} %bitcast.211, ...), custom_call_target="tpu_custom_call" | custom-call | flops 40000000000 | bytes 62914560 | tf_op jit(solution)/shard_map/layer_forward_0/pallas_call | solution.py:1058
  151.3 0.8 slice.177
  152.8 119.6 %layer_forward_1.1 = (f32[128,1536]{1,0:T(8,128)}, f32[128,1536]{1,0:T(8,128)}, f32[8,256]{1,0:T(8,128)}, f32[8,1536]{1,0:T(8,128)}, bf16[1024,1536]{1,0:T(8,128...) custom-call(f32[128,1536]{1,0:T(8,128)} %get-tuple-element.58.stream, ...), custom_call_target="tpu_custom_call" | custom-call | flops 40000000000 | bytes 62914560 | tf_op jit(solution)/shard_map/layer_forward_1/pallas_call | solution.py:1058
  272.4 1.9 convert_bitcast_fusion.1
  274.3 107.7 %layer_backward_1.1 = (f32[128,1536]{1,0:T(8,128)}, f32[8,1536]{1,0:T(8,128)}, bf16[1536,384]{1,0:T(8,128)(2,1)}, bf16[1536,1024]{1,0:T(8,128)(2,1)}, bf16[512,1...) custom-call(f32[128,1536]{1,0:T(8,128)} %bitcast_convert_fusion.grad, f32[128,1536]{1,0:T(8,128)} %get-tuple-element.58.stream, ...), custom_call_target="tpu_custom_call" | custom-call | flops 60000002048 | bytes 62914560 | tf_op jit(solution)/shard_map/layer_backward_1/pallas_call | solution.py:1058
  382.1 108.2 %layer_backward_0.1 = (f32[128,1536]{1,0:T(8,128)}, f32[8,1536]{1,0:T(8,128)}, bf16[1536,384]{1,0:T(8,128)(2,1)}, bf16[1536,1024]{1,0:T(8,128)(2,1)}, bf16[512,1...) custom-call(f32[128,1536]{1,0:T(8,128)} %get-tuple-element.75.grad, bf16[128,1536]{1,0:T(8,128)(2,1)} %bitcast.212, ...), custom_call_target="tpu_custom_call" | custom-call | flops 60000002048 | bytes 62914560 | tf_op jit(solution)/shard_map/layer_backward_0/pallas_call | solution.py:1058
  490.3 0.8 slice.183
  491.1 0.8 slice.184
  492.6 131.4 %reduce_gradients.1 = (bf16[8,2,16,1408]{3,2,1,0:T(8,128)(2,1)}, bf16[2,2,16,1536]{3,2,1,0:T(8,128)(2,1)}, bf16[2,16,1536]{2,1,0:T(8,128)(2,1)}, f32[8,1536]{1,0:T(8,128)}) custom-call(bf16[2,4,2,2,48,384]{5,4,3,2,1,0:T(8,128)(2,1)} %bitcast.178, bf16[2,4,2,2,48,1024]{5,4,3,2,1,0:T(8,128)(2,1)} %bitcast.174, bf16[2,4,2,2,16,1536]{5,4,3,2,1,0:T(8,128)(2,1)} %bitcast.176, ...), custom_call_target="tpu_custom_call" | custom-call | tf_op jit(solution)/shard_map/reduce_gradients/pallas_call | solution.py:1115
  624.0 0.8 constant_dynamic-slice_fusion
  625.4 0.9 slice_convert_fusion.1
  626.3 0.8 copy.87
  627.1 1.0 convert_bitcast_fusion
  628.0 0.8 copy.86
  630.7 1.0 reshape.363
  632.9 0.9 reshape.364
  634.8 1.6 reshape.366
  636.9 1.8 copy.85
  638.6 3.0 reshape.368
  641.7 0.9 copy.125
  (110 shorter events, 19.3 us)
Async XLA Ops:
  0.6 7.9 %copy-start = (bf16[2,96,1536]{2,1,0:T(8,128)(2,1)S(1)}, bf16[2,96,1536]{2,1,0:T(8,128)(2,1)}, u32[]{:S(2)}) copy-start(bf16[2,96,1536]{2,1,0:T(8,128)(2,1)} %param.15) | copy-start | bytes 1769476
  6.7 3.1 copy-start.8
  6.7 3.1 copy-start.9
  11.7 2.5 copy-start.4
  14.3 1.0 copy-start.5
  14.5 1.8 copy-start.6
  14.5 2.3 copy-start.7
  382.1 109.8 %copy-start.10 = (f32[8]{0:T(128)S(1)}, f32[8]{0:T(128)}, u32[]{:S(2)}) copy-start(f32[8]{0:T(128)} %pad.7.clone) | copy-start | bytes 100
  624.0 4.8 copy-start.3
  636.9 5.7 copy-start.1
  638.6 3.0 copy-start.2

commit v3 on v2

--- a/solution.py
+++ b/solution.py
@@ -21,6 +21,7 @@
 F32 = jnp.float32
 MESH = pl.DeviceIdType.MESH
 SCALE = 1.0 / math.sqrt(HEAD)
+SCALE2 = SCALE * math.log2(math.e)
 WIDE = 1536
 
 
@@ -206,7 +207,7 @@
     return finish
 
 
-def reduce_scatter(me, part, parts, give, take, ring_out, ring_in, ssem, rsem, fill=lambda n: None):
+def reduce_scatter(me, part, whole, keep, give, take, ring_out, ring_in, ssem, rsem, fill=lambda n: None):
     z, zp, zm, zo, core, oc = me.z, me.zp, me.zm, me.zo, me.core, me.oc
     up, down, across = {"z": zp}, {"z": zm}, {"core": oc}
     mine = span_of(core * 128, 128)
@@ -225,13 +226,14 @@
         )
 
     def make(k, zz):
-        parts[k] = part(zz)
-        give[k] = parts[k, theirs].astype(BF)
+        whole[...] = part(zz)
+        give[k] = whole[theirs].astype(BF)
+        keep[k] = whole[mine]
         swap(k).start()
 
     def merged(k, half):
-        rows = span_of(core * 128 + 64 * half, 64)
-        return parts[k, rows] + take[k, 64 * half : 64 * half + 64].astype(F32)
+        rows = slice(64 * half, 64 * half + 64)
+        return keep[k, rows] + take[k, rows].astype(F32)
 
     def push(i, value):
         ring_out[i] = value.astype(BF)
@@ -318,25 +320,32 @@
 
 
 class Gather:
-    def __init__(self, me, src, dst, ssem, rsem, loc, order):
+    def __init__(self, me, src, dst, ssem, rsem, loc, order, cols):
         self.me, self.src, self.dst, self.ssem, self.rsem, self.order = me, src, dst, ssem, rsem, order
-        x, yh, yl = me.x, me.yh, me.yl
-        self.own = lambda: pltpu.make_async_copy(src.at[me.core], dst.at[me.core, x, yh, yl], loc)
-        self.cross = lambda: push(
-            src.at[me.oc], dst.at[me.core, x, yh, yl], ssem.at[0], rsem.at[0], {"core": me.oc}
+        self.loc, self.cols = loc, slice(*cols)
+
+    def own(self):
+        me = self.me
+        return pltpu.make_async_copy(
+            self.src.at[me.core, :, self.cols], self.dst.at[me.core, me.x, me.y, :, self.cols], self.loc
+        )
+
+    def cross(self, come=False):
+        me = self.me
+        row = me.oc if come else me.core
+        return push(
+            self.src.at[me.oc, :, self.cols], self.dst.at[row, me.x, me.y, :, self.cols],
+            self.ssem.at[0], self.rsem.at[0], {"core": me.oc},
         )
 
     def region(self, stage, k):
         me = self.me
+        x, y = (lax.rem(v + 4 - k, 4) for v in (me.x, me.y))
         if stage == 0:
-            back = 4 - k
-            x = lax.rem(me.x + back, 4) if self.order[0] == "x" else me.x
-            y = lax.rem(me.y + back, 4) if self.order[0] == "y" else me.y
-            return self.dst.at[:, x, y // 2, lax.rem(y, 2)]
+            return self.dst.at[:, x if self.order[0] == "x" else me.x, y if self.order[0] == "y" else me.y, :, self.cols]
         if self.order[1] == "y":
-            y = lax.rem(me.y + 4 - k, 4)
-            return self.dst.at[:, :, y // 2, lax.rem(y, 2)]
-        return self.dst.at[:, lax.rem(me.x + 4 - k, 4)]
+            return self.dst.at[:, :, y, :, self.cols]
+        return self.dst.at[:, x, :, :, self.cols]
 
     def copy(self, stage, k, come):
         ref = self.region(stage, k if come else 0)
@@ -348,10 +357,8 @@
         self.cross().start()
 
     def one(self):
-        me = self.me
         self.own().wait()
-        here = self.dst.at[me.oc, me.x, me.yh, me.yl]
-        push(here, here, self.ssem.at[0], self.rsem.at[0], {"core": me.oc}).wait_recv()
+        self.cross(True).wait_recv()
         for k in (2, 1, 3):
             self.copy(0, k, False).start()
 
@@ -421,10 +428,11 @@
 
 
 class Reduce:
-    def __init__(self, me, quarter, inner, mine, got1, sum1, got2, ssem, rsem, loc, order):
-        self.me, self.quarter, self.inner, self.order = me, quarter, inner, order
-        self.mine, self.got1, self.sum1, self.got2, self.ssem, self.rsem = mine, got1, sum1, got2, ssem, rsem
-        self.load = pltpu.make_async_copy(quarter(order[0], self.at(order[0], 0)), mine, loc)
+    def __init__(self, me, spec, mine, got1, sum1, got2, ssem, rsem, loc, land=None, landed=False):
+        self.me = me
+        self.quarter, self.inner, self.order = spec[:3]
+        self.mine, self.got1, self.sum1, self.got2, self.ssem, self.rsem, self.loc = mine, got1, sum1, got2, ssem, rsem, loc
+        self.land, self.landed = land, landed
 
     def at(self, axis, k):
         return lax.rem((self.me.x if axis == "x" else self.me.y) + k, 4)
@@ -433,33 +441,42 @@
         axis = self.order[stage]
         to = self.at(axis, k)
         src = self.inner(self.sum1, to) if stage else self.quarter(axis, to)
-        dst = (self.got2 if stage else self.got1).at[k - 1]
+        dst = (self.got2 if stage else self.got1 if self.land is None else self.land).at[k - 1]
         i = 3 * stage + k - 1
         return push(src, dst, self.ssem.at[i], self.rsem.at[i], self.me.near(axis, k))
 
+    def loads(self):
+        axis = self.order[0]
+        out = [pltpu.make_async_copy(self.quarter(axis, self.at(axis, 0)), self.mine, self.loc.at[0])]
+        if self.land is not None:
+            out.append(pltpu.make_async_copy(self.land, self.got1, self.loc.at[1]))
+        return out
+
+    def load(self):
+        for load in self.loads():
+            load.start()
+
     def one(self):
-        self.load.start()
         for k in (2, 1, 3):
             self.copy(0, k).start()
 
+    def arrive(self):
+        if not self.landed:
+            for k in (1, 2, 3):
+                self.copy(0, k).wait_recv()
+
     def two(self):
-        self.load.wait()
-        for k in (1, 2, 3):
-            self.copy(0, k).wait_recv()
-        lead = math.prod(self.sum1.shape[:-2])
+        for load in self.loads():
+            load.wait()
         dims = self.sum1.shape[:-2]
 
-        @pl.loop(0, lead)
+        @pl.loop(0, math.prod(dims))
         def _(n):
-            at = []
-            for d in reversed(dims):
-                at.insert(0, lax.rem(n, d))
-                n = n // d
-            at = tuple(at)
+            at = (n,) if len(dims) == 1 else (n // dims[1], lax.rem(n, dims[1]))
             total = self.mine[at].astype(F32)
             for k in range(3):
                 total = total + self.got1[(k, *at)].astype(F32)
-            self.sum1[at] = total.astype(self.sum1.dtype)
+            self.sum1[at] = total.astype(BF)
 
         for k in (2, 1, 3):
             self.copy(1, k).start()
@@ -472,10 +489,66 @@
             total = total + self.got2[k].astype(F32)
         return total
 
-    def finish(self):
-        for stage in (0, 1):
+    def finish(self, stages=(0, 1)):
+        for stage in stages:
             for k in (1, 2, 3):
                 self.copy(stage, k).wait_send()
+
+
+def reduce_specs(d_in, d_gu, d_d, d_o):
+    def split(ref, lo, hi, r, order):
+        def quarter(axis, i):
+            return ref.at[:, i, :, :, lo:hi] if axis == "x" else ref.at[:, :, i, :, lo:hi]
+
+        return quarter, lambda q, i: q.at[:, i], order, (2, 4, r, hi - lo), (2, r, hi - lo)
+
+    return {
+        "g": split(d_gu, 0, 512, 48, "yx"),
+        "u": split(d_gu, 512, 1024, 48, "xy"),
+        "da": split(d_d, 0, 768, 16, "yx"),
+        "db": split(d_d, 768, 1536, 16, "xy"),
+        "ia": split(d_in, 0, 256, 48, "yx"),
+        "ib": split(d_in, 256, 384, 48, "xy"),
+        "o": (lambda axis, i: d_o.at[:, i], lambda q, i: q.at[i], "xy", (4, 16, WIDE), (16, WIDE)),
+    }
+
+
+REDUCE = reduce_specs(None, None, None, None)
+MLP = ("g", "u", "da", "db")
+
+
+def reduce_scratch(staged=REDUCE):
+    out = []
+    for name, (_, _, _, big, small) in REDUCE.items():
+        out += [vm(big), vm((3,) + big)] if name in staged else []
+        out += [vm(big), vm((3,) + small)]
+    return out + [dma(7, 6), dma(7, 6), dma(7, 2)]
+
+
+def make_reduces(me, parts, refs, land=None, landed=False, stage=None):
+    out, n = {}, 0
+    for name, spec in reduce_specs(*parts).items():
+        own, got = stage[name] if stage and name in stage else (refs.pop(0), refs.pop(0))
+        sum1, got2 = refs.pop(0), refs.pop(0)
+        out[name] = (spec, own, got, sum1, got2)
+    ssem, rsem, loc = refs.pop(0), refs.pop(0), refs.pop(0)
+    for n, (name, (spec, own, got, sum1, got2)) in enumerate(out.items()):
+        there = land.get(name) if land else None
+        out[name] = Reduce(
+            me, spec, own, got, sum1, got2, ssem.at[n], rsem.at[n], loc.at[n], there, landed and there is not None
+        )
+    return out
+
+
+def finish_reduces(reds, fin, down, out):
+    for lo, hi, name in ((0, 256, "ia"), (256, 384, "ib"), (384, 896, "g"), (896, 1408, "u")):
+        total = reds[name].three()
+        for dp in range(2):
+            for z in range(4):
+                fin[dp, z, :, lo:hi] = padded(total[dp, 12 * z : 12 * z + 12])
+    down[:, :, 0:768] = reds["da"].three().astype(BF)
+    down[:, :, 768:1536] = reds["db"].three().astype(BF)
+    out[...] = reds["o"].three().astype(BF)
 
 
 def lane_masks(rows):
@@ -512,14 +585,24 @@
     return lax.rsqrt(jnp.mean(values * values, axis=-1, keepdims=True) + EPS)
 
 
-def fwd_kernel(
-    first, stream, gains_in, cos, sin, pcol, prow, s_gain, s_in, s_o, s_g, s_u, s_d,
-    o_stream, o_middle, o_lse, o_gains, o_normed, o_qkv, o_mixed, o_nmlp, o_gate, o_up, o_hidden,
-    o_win, o_wo, o_wg, o_wu, o_wd,
-    w_in, w_o, w_g, w_u, w_d, w_gain, buf1, buf2, qs, qr, ms, mr, gate_v, up_v, hid, keys, vals, vals_t, middle,
-    parts, give, take, ring_out, ring_in,
-    ag_s, ag_r, ag2_s, ag2_r, rs_s, rs_r, rs2_s, rs2_r, ax_s, ax_r, bx_s, bx_r, loc, loc2, ga_s, ga_r,
-):
+def fwd_kernel(l, *refs):
+    first = l == 0
+    g_attn, g_mlp = (slice(2 * l + i, 2 * l + i + 1) for i in (0, 1))
+    refs = list(refs)
+    take = lambda n: [refs.pop(0) for _ in range(n)]
+    stream, gains_in, cos, sin, pcol, prow = take(6)
+    (h_in,) = take(1)
+    s_o, s_g, s_u, s_d = take(4)
+    s_gain, s_next = take(2) if first else (None, None)
+    o_stream, o_middle, o_lse = take(3)
+    (o_gains,) = take(1) if first else (gains_in,)
+    o_normed, o_qkv, o_mixed, o_nmlp, o_gate, o_up, o_hidden, o_wo, o_wg, o_wu, o_wd = take(11)
+    o_win, o_next = take(2) if first else (None, None)
+    w_in, w_o, w_g, w_u, w_d = take(5)
+    buf1, buf2, qs, qr, ms, mr, gate_v, up_v, hid, keys, vals, vals_t, middle = take(13)
+    whole, keep, give, got, ring_out, ring_in = take(6)
+    ag_s, ag_r, ag2_s, ag2_r, rs_s, rs_r, rs2_s, rs2_r, ax_s, ax_r, bx_s, bx_r, loc, loc2, ga_s, ga_r = take(16)
+    w_gain, w_next = take(2) if first else (None, None)
     me = Place()
     stores = []
 
@@ -527,67 +610,42 @@
         stores.append(pltpu.make_async_copy(src, dst, loc2.at[len(stores)]))
         stores[-1].start()
 
-    items = ((s_in, w_in, "xy"), (s_g, w_g, "xy"), (s_u, w_u, "yx"), (s_d, w_d, "xy"), (s_gain, w_gain, "yx"))
-    g_in, g_g, g_u, g_d, g_gain = (
-        Gather(me, s, d, ga_s.at[i], ga_r.at[i], loc.at[i], order) for i, (s, d, order) in enumerate(items)
-    )
-    g_o = OutGather(me, s_o, w_o, ga_s.at[5], ga_r.at[5], loc.at[5])
+    n_item = [0]
+
+    def item(src, dst, order, *cols):
+        i = n_item[0]
+        n_item[0] += 1
+        return Gather(me, src, dst, ga_s.at[i], ga_r.at[i], loc.at[i], order, cols)
+
+    g_g, g_u = item(s_g, w_g, "xy", 0, 512), item(s_u, w_u, "yx", 0, 512)
+    g_d = [item(s_d, w_d, "xy", 0, 768), item(s_d, w_d, "yx", 768, WIDE)]
+    g_o = OutGather(me, s_o, w_o, ga_s.at[4], ga_r.at[4], loc.at[4])
+    n_item[0] = 5
+    g_in, g_next, g_gain = [], [], []
+    if first:
+        g_gain = [item(s_gain, w_gain, "yx", 0, 256)]
+        g_in = [item(h_in, w_in, "yx", 0, 256), item(h_in, w_in, "xy", 256, 384)]
+        g_next = [item(s_next, w_next, "yx", 0, 256), item(s_next, w_next, "xy", 256, 384)]
+    everything = g_gain + g_in + [g_o, g_g, g_u] + g_d + g_next
+
+    def each(items, step):
+        for one in items:
+            getattr(one, step)()
+
     own_rows = slot_rows(me.z, me.core)
+    raw = buf2 if first else buf1
     if first:
-        buf2[own_rows] = stream[...]
+        raw[own_rows] = stream[...]
     else:
-        o_gains[...] = gains_in[...]
+        load_in = pltpu.make_async_copy(h_in, w_in, loc.at[5])
+        load_in.start()
         s = stream[...]
-        buf1[own_rows] = (s * rms_of(s) * gains_in[0:1, :]).astype(BF)
+        raw[own_rows] = (s * rms_of(s) * gains_in[g_attn, :]).astype(BF)
     me.greet(me.layer_partners())
-    if first:
-        g_gain.zero()
-    g_in.zero()
-    g_o.zero()
-    g_g.zero()
-    g_u.zero()
-    g_d.zero()
-
-    def hook0():
-        if first:
-            g_gain.one()
-        g_in.one()
-
-    def hook1():
-        if first:
-            g_gain.two()
-        g_in.two()
-
-    def hook2():
-        g_o.one()
-
-    def skip(zz):
-        pass
-
-    done_ag = all_gather(me, buf2 if first else buf1, ag_s, ag_r, skip, (hook0, hook1, hook2))
-    if first:
-        g_gain.three()
-        o_gains[...] = jnp.zeros_like(o_gains)
-        for owner in range(16):
-            base = 96 * owner // 128 * 128
-            width = min(256, WIDE - base)
-            row = w_gain[owner // 8, owner % 8 // 2, owner % 2, 0]
-            o_gains[:, base : base + width] += row[:, :width]
-
-        @pl.loop(0, 8)
-        def _(p):
-            rows = span_of(p * 128, 128)
-            s = buf2[rows].astype(F32)
-            buf1[rows] = (s * rms_of(s) * o_gains[0:1, :]).astype(BF)
-
-    done_ag()
-
+    each(everything, "zero")
     ax = Exchange(me, qs, qr, ax_s, ax_r)
-    g_in.three()
-
-    @pl.loop(0, 4)
-    def _(k):
-        zz = lax.rem(me.z + k, 4)
+
+    def project(zz):
         rows = span_of(zz * 256, 256)
         y = mm(buf1[rows], w_in[...].reshape(WIDE, 384))
         for t in range(3):
@@ -597,9 +655,46 @@
         ax.send(zz * 2)
         ax.send(zz * 2 + 1)
 
+    def normalise(zz):
+        rows = span_of(zz * 256, 256)
+        s = raw[rows].astype(F32)
+        buf1[rows] = (s * rms_of(s) * o_gains[g_attn, :]).astype(BF)
+
+    if first:
+
+        def own_pair():
+            each(g_gain + g_in, "two")
+
+        def gains_here():
+            each(g_gain, "three")
+            o_gains[...] = jnp.zeros_like(o_gains)
+            for owner in range(16):
+                base = 96 * owner // 128 * 128
+                width = min(256, WIDE - base)
+                row = w_gain[owner // 8, owner % 8 // 2, owner % 2 * 2]
+                o_gains[:, base : base + width] += row[:, :width]
+            normalise(me.z)
+            g_o.one()
+
+        hooks = (lambda: each(g_gain + g_in, "one"), own_pair, gains_here)
+
+        def others(zz):
+            if zz is not me.z:
+                normalise(zz)
+
+        done_ag = all_gather(me, raw, ag_s, ag_r, others, hooks)
+        done_ag()
+        each(g_in, "three")
+
+        @pl.loop(0, 4)
+        def _(k):
+            project(lax.rem(me.z + k, 4))
+
+    else:
+        load_in.wait()
+        done_ag = all_gather(me, raw, ag_s, ag_r, project, (g_o.one,))
     g_o.two()
-    g_g.one()
-    g_u.one()
+    each((g_g, g_u), "one")
     ax.arrive()
     store(buf1, o_normed)
     store(qr, o_qkv)
@@ -612,21 +707,20 @@
         p = lax.rem(me.c + 1 + k, 8)
         rows = span_of(p * 128, 128)
         q = stacked(qr, rows)
-        scores = mm_nt(keys[...], q) * SCALE
+        scores = mm_nt(keys[...], q)
         scores = jnp.where(pcol[...] <= prow[pl.ds(p, 1), :], scores, -1e30)
         top = jnp.max(scores, axis=0, keepdims=True)
-        weights = jnp.exp(scores - top)
+        weights = jnp.exp2((scores - top) * SCALE2)
         total = jnp.sum(weights, axis=0, keepdims=True)
-        o_lse[pl.ds(p, 1), :] = top + jnp.log(total)
-        probs = (weights / total).astype(BF)
+        o_lse[pl.ds(p, 1), :] = top * SCALE2 + jnp.log2(total)
+        probs = (weights * (1.0 / total)).astype(BF)
         out = jnp.transpose(mm(vals_t[...], probs)).astype(BF)
         ms[rows, 0:128] = out[0:128]
         ms[rows, 128:256] = out[128:256]
         bx.send(p)
 
-    g_g.two()
-    g_u.two()
-    g_d.one()
+    each((g_g, g_u), "two")
+    each(g_d, "one")
     g_o.three()
     bx.arrive()
     store(mr, o_mixed)
@@ -634,34 +728,36 @@
     def out_part(zz):
         return mm(mr[span_of(zz * 256, 256)], w_o[...].reshape(256, WIDE))
 
-    rs = (parts, give, take, ring_out, ring_in)
+    rs = (whole, keep, give, got, ring_out, ring_in)
     total, done_rs = reduce_scatter(me, out_part, *rs, rs_s, rs_r)
     mid = total + (stream[...].astype(F32) if first else stream[...])
     middle[...] = mid
     o_middle[...] = mid
-    buf2[own_rows] = (mid * rms_of(mid) * o_gains[1:2, :]).astype(BF)
+    buf2[own_rows] = (mid * rms_of(mid) * o_gains[g_mlp, :]).astype(BF)
     waited = []
 
     def gated(zz):
         if not waited:
-            g_g.three()
-            g_u.three()
             waited.append(1)
+            each((g_g, g_u), "three")
         rows = span_of(zz * 256, 256)
         gate = mm(buf2[rows], w_g[...].reshape(WIDE, 512))
-        gate_v[rows] = gate
+        gate_v[rows] = gate.astype(BF)
         up = mm(buf2[rows], w_u[...].reshape(WIDE, 512))
-        up_v[rows] = up
+        up_v[rows] = up.astype(BF)
         hid[rows] = (gate / (1.0 + jnp.exp(-gate)) * up).astype(BF)
 
-    done_ag2 = all_gather(me, buf2, ag2_s, ag2_r, gated, (g_d.two,))
+    hooks = (lambda: each(g_d, "two"), lambda: None, lambda: each(g_next, "one"))
+    done_ag2 = all_gather(me, buf2, ag2_s, ag2_r, gated, hooks)
     store(buf2, o_nmlp)
     store(gate_v, o_gate)
     store(up_v, o_up)
     store(hid, o_hidden)
-    g_d.three()
+    each(g_next, "two")
+    each(g_d, "three")
     done_rs()
-    for w, o in ((w_in, o_win), (w_o, o_wo), (w_g, o_wg), (w_u, o_wu), (w_d, o_wd)):
+    pairs = [(w_o, o_wo), (w_g, o_wg), (w_u, o_wu), (w_d, o_wd)] + ([(w_in, o_win)] if first else [])
+    for w, o in pairs:
         store(w, o)
 
     def down_part(zz):
@@ -669,12 +765,14 @@
 
     total, done_rs2 = reduce_scatter(me, down_part, *rs, rs2_s, rs2_r)
     o_stream[...] = middle[...] + total
-    for done in (ax.finish, bx.finish, done_ag2, done_rs2):
+    each(g_next, "three")
+    if first:
+        store(w_next, o_next)
+    for done in ((() if first else (done_ag,)) + (ax.finish, bx.finish, done_ag2, done_rs2)):
         done()
-    for item in (g_in, g_g, g_u, g_d, g_o) + ((g_gain,) if first else ()):
-        item.finish()
-    for item in stores:
-        item.wait()
+    each(everything, "finish")
+    for copy in stores:
+        copy.wait()
 
 
 def norm_back_of(e, values, gain):
@@ -685,19 +783,28 @@
     return part, jnp.sum(e * n, axis=0, keepdims=True)
 
 
-def bwd_kernel(
-    grad, stream, middle, gains, cos, sin, pcol, prow, lse,
-    h_in, h_o, h_g, h_u, h_d, h_qkv, h_gate, h_up, h_normed, h_mixed, h_nmlp, h_hidden,
-    o_grad, o_gains, o_din, o_dgu, o_dd, o_do,
-    w_in, w_o, w_g, w_u, w_d, buf1, buf2, qr, gate_v, up_v, gu, mgs, mgr, keys, vals, keys_t, dk, dv,
-    dqs, ps, pr, mid_grad, normed, mixed, nmlp, hid, d_in, d_gu, d_d, d_o,
-    parts, give, take, ring_out, ring_in,
-    ag_s, ag_r, ag2_s, ag2_r, rs_s, rs_r, rs2_s, rs2_r, ax_s, ax_r, bx_s, bx_r, loc, loc2,
-):
+def bwd_kernel(l, *refs):
+    last = l == 0
+    g_attn, g_mlp = (slice(2 * l + i, 2 * l + i + 1) for i in (0, 1))
+    refs = list(refs)
+    take = lambda n: [refs.pop(0) for _ in range(n)]
+    grad, stream, middle, gains, cos, sin, pcol, prow, lse = take(9)
+    h_in, h_o, h_g, h_u, h_d, h_qkv, h_gate, h_up, h_normed, h_mixed, h_nmlp, h_hidden = take(12)
+    above = take(4) if last else None
+    o_grad, o_gains = take(2)
+    o_fin, o_down, o_out = take(3) if last else (None,) * 3
+    parts = take(4)
+    o_din, o_dgu, o_dd, o_do = parts
+    landing, landing1 = (dict(zip(MLP, take(4))) if last else {} for _ in range(2))
+    w_in, w_o, w_g, w_u, w_d, buf1, buf2, qr, gate_v, up_v, gu, mgs, mgr = take(13)
+    keys, vals, keys_t, dk, dv, dqs, ps, pr, mid_grad, mixed, nmlp, hid = take(12)
+    d_in, d_gu, d_d, d_o = take(4)
+    whole, keep, give, got, ring_out, ring_in = take(6)
+    ag_s, ag_r, ag2_s, ag2_r, rs_s, rs_r, rs2_s, rs2_r, ax_s, ax_r, bx_s, bx_r, loc, loc2 = take(14)
     me = Place()
     pairs = (
         (h_d, w_d), (h_gate, gate_v), (h_up, up_v), (h_g, w_g), (h_u, w_u), (h_o, w_o), (h_qkv, qr), (h_in, w_in),
-        (h_hidden, hid), (h_nmlp, nmlp), (h_mixed, mixed), (h_normed, normed),
+        (h_hidden, hid), (h_nmlp, nmlp), (h_mixed, mixed),
     )
     loads = [pltpu.make_async_copy(h, v, loc.at[i]) for i, (h, v) in enumerate(pairs)]
     for load in loads:
@@ -708,16 +815,32 @@
         stores.append(pltpu.make_async_copy(src, dst, loc2.at[len(stores)]))
         stores[-1].start()
 
+    reds, early = {}, {}
+    if last:
+        stage = {
+            "g": (w_g.at[3], w_g.at[0:3]), "u": (w_u.at[3], w_u.at[0:3]),
+            "da": (w_d.at[3, :, :, :, 0:768], w_d.at[0:3, :, :, :, 0:768]),
+            "db": (w_d.at[3, :, :, :, 768:WIDE], w_d.at[0:3, :, :, :, 768:WIDE]),
+        }
+        reds = make_reduces(me, above, refs, landing1, False, stage)
+        specs, (es, er) = reduce_specs(*parts), refs
+        early = {
+            name: Reduce(me, specs[name], None, landing[name], None, None, es.at[n], er.at[n], None)
+            for n, name in enumerate(MLP)
+        }
+
     own_rows = slot_rows(me.z, me.core)
     buf1[own_rows] = grad[...].astype(BF)
     me.greet(me.layer_partners())
+    for red in reds.values():
+        red.one()
     for load in loads[:3]:
         load.wait()
 
     def unit(zz):
         rows = span_of(zz * 256, 256)
-        hg = mm_nt(buf1[rows], w_d[...])
-        gate, up = gate_v[rows], up_v[rows]
+        hg = mm_nt(buf1[rows], w_d[...].reshape(512, WIDE))
+        gate, up = gate_v[rows].astype(F32), up_v[rows].astype(F32)
         sig = 1.0 / (1.0 + jnp.exp(-gate))
         gu[rows, 0:512] = (hg * up * (sig * (1.0 + gate * (1.0 - sig)))).astype(BF)
         gu[rows, 512:1024] = (hg * (gate * sig)).astype(BF)
@@ -728,15 +851,16 @@
 
     def mlp_part(zz):
         rows = span_of(zz * 256, 256)
-        return mm_nt(gu[rows, 0:512], w_g[...]) + mm_nt(gu[rows, 512:1024], w_u[...])
+        return mm_nt(gu[rows, 0:512], w_g[...].reshape(WIDE, 512)) + mm_nt(gu[rows, 512:1024], w_u[...].reshape(WIDE, 512))
 
     def grad_down(b):
         cols = slice(256 * b, 256 * b + 256)
-        d_d[cols] = mm_tn(hid[:, cols], buf1[...]).astype(BF)
+        d_d[b] = mm_tn(hid[:, cols], buf1[...]).astype(BF).reshape(4, 4, 16, WIDE)
 
     def grad_gu(b):
-        cols = slice(256 * b, 256 * b + 256)
-        d_gu[cols] = mm_tn(nmlp[:, cols], gu[...]).astype(BF)
+        cols = slice(384 * b, 384 * b + 384)
+        pair = slice(b % 2 * 2, b % 2 * 2 + 2)
+        d_gu[b // 2, pair] = mm_tn(nmlp[:, cols], gu[...]).astype(BF).reshape(2, 4, 48, 1024)
 
     def fill1(n):
         if n == 0:
@@ -749,9 +873,9 @@
             grad_gu(2)
             grad_gu(3)
 
-    rs = (parts, give, take, ring_out, ring_in)
+    rs = (whole, keep, give, got, ring_out, ring_in)
     e, done_rs = reduce_scatter(me, mlp_part, *rs, rs_s, rs_r, fill1)
-    part, gain_part = norm_back_of(e, middle[...], gains[1:2, :])
+    part, gain_part = norm_back_of(e, middle[...], gains[g_mlp, :])
     o_gains[1:2, :] = gain_part
     gm = grad[...] + part
     mid_grad[...] = gm
@@ -770,11 +894,20 @@
         dk[...] = jnp.zeros_like(dk)
         dv[...] = jnp.zeros_like(dv)
 
+    def hook1():
+        for red in reds.values():
+            red.arrive()
+            red.load()
+
     def hook2():
-        grad_gu(4)
-        grad_gu(5)
-
-    done_ag2 = all_gather(me, buf2, ag2_s, ag2_r, mixed_back, (hook0, lambda: None, hook2))
+        for red in reds.values():
+            red.two()
+
+    done_ag2 = all_gather(me, buf2, ag2_s, ag2_r, mixed_back, (hook0, hook1, hook2))
+    done_ag()
+    normed = buf1
+    load_normed = pltpu.make_async_copy(h_normed, normed, loc.at[11])
+    load_normed.start()
     store(d_d, o_dd)
     store(d_gu, o_dgu)
     lanes = mm_tn(mixed[...], buf2[...])
@@ -785,8 +918,12 @@
             piece = chunk[first][shift:]
             if shift > 4:
                 piece = jnp.concatenate([piece, chunk[first + 1][: shift - 4]], axis=0)
-            d_o[head, b // 4, b % 4] = padded(piece[0:12])
+            d_o[head * 2 + b // 4, b % 4] = padded(piece[0:12])
     store(d_o, o_do)
+    if last:
+        stores[0].wait()
+        early["da"].one()
+        early["db"].one()
     ax.arrive()
 
     @pl.loop(0, 8)
@@ -794,9 +931,9 @@
         rows = span_of(p * 128, 128)
         q = stacked(qr, rows)
         mg = stacked(mgr, rows)
-        scores = mm_nt(keys[...], q) * SCALE
+        scores = mm_nt(keys[...], q)
         allowed = pcol[...] <= prow[pl.ds(p, 1), :]
-        probs = jnp.where(allowed, jnp.exp(scores - lse[pl.ds(p, 1), :]), 0.0)
+        probs = jnp.where(allowed, jnp.exp2(scores * SCALE2 - lse[pl.ds(p, 1), :]), 0.0)
         pg = mm_nt(vals[...], mg)
         inner = jnp.sum(probs * pg, axis=0, keepdims=True)
         sg = (probs * (pg - inner)).astype(BF)
@@ -819,7 +956,12 @@
         ps[rows, 256:384] = jnp.where(v0, pltpu.roll(value, 96, 1), dk[rows] * SCALE).astype(BF)
         bx.send(p)
 
+    if last:
+        stores[1].wait()
+        early["g"].one()
+        early["u"].one()
     done_rs()
+    load_normed.wait()
     bx.arrive()
     pre = qr
 
@@ -832,76 +974,45 @@
         return mm_nt(pre[rows], w_in[...])
 
     def fill2(n):
-        for b in (2 * n, 2 * n + 1):
-            cols = slice(256 * b, 256 * b + 256)
-            d_in[cols] = mm_tn(normed[:, cols], pre[...]).astype(BF)
+        for b in ((0, 1), (2,), (3,))[n]:
+            cols = slice(384 * b, 384 * b + 384)
+            pair = slice(b % 2 * 2, b % 2 * 2 + 2)
+            d_in[b // 2, pair] = mm_tn(normed[:, cols], pre[...]).astype(BF).reshape(2, 4, 48, 384)
+        if n == 1 and last:
+            finish_reduces(reds, o_fin, o_down, o_out)
 
     e, done_rs2 = reduce_scatter(me, in_part, *rs, rs2_s, rs2_r, fill2)
     store(d_in, o_din)
-    part, gain_part = norm_back_of(e, stream[...].astype(F32), gains[0:1, :])
+    part, gain_part = norm_back_of(e, stream[...].astype(F32), gains[g_attn, :])
     o_gains[0:1, :] = gain_part
     o_grad[...] = mid_grad[...] + part
-    for done in (done_ag, done_ag2, ax.finish, bx.finish, done_rs2):
+    for done in (done_ag2, ax.finish, bx.finish, done_rs2):
         done()
-    for item in stores:
-        item.wait()
+    for red in reds.values():
+        red.finish()
+    for red in early.values():
+        red.arrive()
+        red.finish((0,))
+    for copy in stores[2 if last else 0 :]:
+        copy.wait()
 
 
 def padded(rows):
     return jnp.concatenate([rows, jnp.zeros((4, rows.shape[1]), F32)], axis=0).astype(BF)
 
 
-def reduce_specs(d_in, d_gu, d_d, d_o):
-    def split(ref, lo, hi, r, order):
-        cols = slice(lo, hi)
-
-        def quarter(axis, i):
-            if axis == "x":
-                return ref.at[:, i, :, :, :, cols]
-            return ref.at[:, :, i // 2, lax.rem(i, 2), :, cols]
-
-        def inner(s, i):
-            return s.at[:, i] if order == "yx" else s.at[:, i // 2, lax.rem(i, 2)]
-
-        lead = (2, 4) if order == "yx" else (2, 2, 2)
-        return quarter, inner, order, lead + (r, hi - lo), (2, r, hi - lo)
-
-    def out_quarter(axis, i):
-        return d_o.at[i // 2, lax.rem(i, 2)]
-
-    return [
-        split(d_gu, 0, 512, 48, "yx"),
-        split(d_gu, 512, 1024, 48, "xy"),
-        split(d_d, 0, 768, 16, "yx"),
-        split(d_d, 768, 1536, 16, "xy"),
-        split(d_in, 0, 384, 48, "yx"),
-        (out_quarter, lambda s, i: s.at[i], "yx", (4, 16, WIDE), (16, WIDE)),
-    ]
-
-
-def reduce_scratch():
-    out = []
-    for _, _, _, big, small in reduce_specs(None, None, None, None):
-        out += [vm(big), vm((3,) + big), vm(big), vm((3,) + small)]
-    return out
-
-
-def grads_kernel(layers, *refs):
-    parts, gains = refs[: 4 * layers], refs[4 * layers]
-    o_rows, o_down, o_out, o_gains = refs[4 * layers + 1 : 4 * layers + 5]
-    scratch = list(refs[4 * layers + 5 :])
-    n_red = 6 * layers
-    red_scratch, scratch = scratch[: 4 * n_red], scratch[4 * n_red :]
-    fin_s, fin_r, down_s, down_r, out_s, out_r, sum_a, sum_b, got_a, got_b, got_c = scratch[:11]
-    red_s, red_r, loc, fin_ss, fin_rs, gain_s, gain_r, down_ss, down_rs, out_ss = scratch[11:]
+def grads_kernel(*refs):
+    refs = list(refs)
+    take = lambda n: [refs.pop(0) for _ in range(n)]
+    gains, fin1, down1, out1 = take(4)
+    parts = take(4)
+    landed = dict(zip(MLP, take(4)))
+    o_rows, o_down, o_out, o_gains = take(4)
+    reds = make_reduces(Place(), parts, refs, landed, True)
+    fin_s, fin_r, down_s, down_r, out_s, out_r, sum_a, sum_b, got_a, got_b, got_c = take(11)
+    fin_ss, fin_rs, gain_s, gain_r, down_ss, down_rs, out_ss = take(7)
     me = Place()
-    reds = []
-    for l in range(layers):
-        for quarter, inner, order, _, _ in reduce_specs(*parts[4 * l : 4 * l + 4]):
-            n = len(reds)
-            reds.append(
-                Reduce(me, quarter, inner, *red_scratch[4 * n : 4 * n + 4], red_s.at[n], red_r.at[n], loc.at[n], order)
-            )
+    mlp, rest = [reds[n] for n in MLP], [reds[n] for n in ("ia", "ib", "o")]
     group = [(k, c) for k in range(4) for c in range(2) if k or c]
 
     def mate(k, c):
@@ -909,6 +1020,8 @@
 
     mirror = {"x": me.z, "z": me.x}
     apart = me.x != me.z
+    for red in reds.values():
+        red.load()
     me.greet(
         [me.near("x", k) for k in (1, 2, 3)] + [me.near("y", k) for k in (1, 2, 3)]
         + [mate(*m) for m in group] + [{"yl": 1 - me.yl, "core": me.oc}],
@@ -928,12 +1041,16 @@
 
     for k in (1, 2, 3):
         gain_copy(0, "y", gains, got_a, k).start()
-    for red in reds:
+    for red in rest:
         red.one()
+    for red in mlp:
+        red.two()
+    for red in rest:
+        red.arrive()
     gain_sum(0, "y", gains, got_a, sum_a)
     for k in (1, 2, 3):
         gain_copy(1, "x", sum_a, got_b, k).start()
-    for red in reds:
+    for red in rest:
         red.two()
     gain_sum(1, "x", sum_a, got_b, sum_b)
 
@@ -942,17 +1059,10 @@
 
     for i in range(7):
         gain_mate(i).start()
-    for l in range(layers):
-        gate, up, down_a, down_b, first, out = reds[6 * l : 6 * l + 6]
-        for lo, hi, red in ((384, 896, gate), (896, 1408, up), (0, 384, first)):
-            total = red.three()
-            for dp in range(2):
-                for z in range(4):
-                    fin_s[dp, z, l, :, lo:hi] = padded(total[dp, 12 * z : 12 * z + 12])
-        down_s[:, l, :, 0:768] = down_a.three().astype(BF)
-        down_s[:, l, :, 768:1536] = down_b.three().astype(BF)
-        out_s[l] = out.three().astype(BF)
-
+    fin_s[:, :, 1] = fin1[...]
+    down_s[:, 1] = down1[...]
+    out_s[1] = out1[...]
+    finish_reduces(reds, fin_s.at[:, :, 0], down_s.at[:, 0], out_s.at[0])
     slot = me.z * 2 + me.core
 
     def fin(i, come):
@@ -1014,7 +1124,9 @@
         out_copy().wait_recv()
 
     o_out[...] = out_r[...]
-    for red in reds:
+    for red in mlp:
+        red.finish((1,))
+    for red in rest:
         red.finish()
     for k in (1, 2, 3):
         gain_copy(0, "y", gains, got_a, k).wait_send()
@@ -1050,10 +1162,12 @@
 
 
 WEIGHTS = [(WIDE, 384), (256, WIDE), (WIDE, 512), (WIDE, 512), (512, WIDE)]
-SPLIT = [(2, 4, 2, 2, 48, 384), (4, 64, WIDE), (2, 4, 2, 2, 48, 512), (2, 4, 2, 2, 48, 512), (2, 4, 2, 2, 16, WIDE)]
-
-
-def run_kernel(kernel, name, cid, ins, in_vmem, outs, out_vmem, scratch, flops):
+SPLIT = [(2, 4, 4, 48, 384), (4, 64, WIDE), (2, 4, 4, 48, 512), (2, 4, 4, 48, 512), (2, 4, 4, 16, WIDE)]
+PARTS = [(2, 4, 4, 48, 384), (2, 4, 4, 48, 1024), (2, 4, 4, 16, WIDE), (4, 4, 16, WIDE)]
+RING = [(256, WIDE), (4, 128, WIDE)]
+
+
+def run_kernel(kernel, name, cid, ins, in_vmem, outs, out_vmem, scratch):
     place = {True: pltpu.VMEM, False: pl.ANY}
     return pl.pallas_call(
         kernel,
@@ -1062,65 +1176,65 @@
         in_specs=[pl.BlockSpec(memory_space=place[i < in_vmem]) for i in range(len(ins))],
         out_specs=[pl.BlockSpec(memory_space=place[i < out_vmem]) for i in range(len(outs))],
         scratch_shapes=scratch,
-        cost_estimate=pl.CostEstimate(flops=flops, bytes_accessed=60 * 2**20, transcendentals=0),
         compiler_params=pltpu.CompilerParams(
-            collective_id=cid, has_side_effects=True, vmem_limit_bytes=60 * 2**20
+            collective_id=cid, has_side_effects=True, vmem_limit_bytes=58 * 2**20
         ),
     )(*ins)
 
 
-def layer_fwd(l, stream, gains, cos, sin, pcol, prow, sources):
-    outs = [
-        ((128, WIDE), F32), ((128, WIDE), F32), ((8, 256), F32), ((8, WIDE), F32),
+def layer_fwd(l, stream, gains, tables, h_in, sources, extra):
+    first = l == 0
+    outs = [((128, WIDE), F32), ((128, WIDE), F32), ((8, 256), F32)] + ([((8, WIDE), F32)] if first else [])
+    n_vmem = len(outs)
+    outs += [
         ((1024, WIDE), BF), ((1024, 384), BF), ((1024, 256), BF), ((1024, WIDE), BF),
-        ((1024, 512), F32), ((1024, 512), F32), ((1024, 512), BF),
-    ] + [(s, BF) for s in SPLIT]
-    scratch = [vm(s) for s in SPLIT] + [vm((2, 4, 2, 2, 8, 256), F32)] + [
+        ((1024, 512), BF), ((1024, 512), BF), ((1024, 512), BF),
+    ] + [(s, BF) for s in SPLIT[1:]] + ([(SPLIT[0], BF)] * 2 if first else [])
+    scratch = [vm(s) for s in SPLIT] + [
         vm((1024, WIDE)), vm((1024, WIDE)), vm((1024, 384)), vm((1024, 384)), vm((1024, 256)), vm((1024, 256)),
-        vm((1024, 512), F32), vm((1024, 512), F32), vm((1024, 512)),
-        vm((1024, 128)), vm((1024, 128)), vm((128, 1024)), vm((128, WIDE), F32), vm((4, 256, WIDE), F32),
-    ] + rs_scratch() + sems() + [dma(6, 7), dma(6, 7)]
-    ins = [stream, gains, cos, sin, pcol, prow, *sources]
-    kernel = functools.partial(fwd_kernel, l == 0)
-    return run_kernel(kernel, f"layer_forward_{l}", 1 + l, ins, 6, outs, 4, scratch, 40 * 10**9)
-
-
-def layer_bwd(l, grad, stream, middle, gains, cos, sin, pcol, prow, lse, weights, saved):
-    outs = [((128, WIDE), F32), ((8, WIDE), F32), ((WIDE, 384), BF), ((WIDE, 1024), BF), ((512, WIDE), BF), ((2, 2, 4, 16, WIDE), BF)]
-    scratch = [vm(s) for s in WEIGHTS] + [
-        vm((1024, WIDE)), vm((1024, WIDE)), vm((1024, 384)), vm((1024, 512), F32), vm((1024, 512), F32),
+        vm((1024, 512)), vm((1024, 512)), vm((1024, 512)),
+        vm((1024, 128)), vm((1024, 128)), vm((128, 1024)), vm((128, WIDE), F32),
+    ] + [vm(s, F32) for s in RING] + rs_scratch() + sems() + [dma(10, 7), dma(10, 7)]
+    if first:
+        scratch += [vm((2, 4, 4, 8, 256), F32), vm(SPLIT[0])]
+    ins = [stream, gains, *tables, h_in, *sources, *extra]
+    kernel = functools.partial(fwd_kernel, l)
+    return run_kernel(kernel, f"layer_forward_{l}", 1 + l, ins, 6, outs, n_vmem, scratch)
+
+
+def layer_bwd(l, grad, stream, middle, gains, tables, lse, weights, saved, above):
+    last = l == 0
+    outs = [((128, WIDE), F32), ((8, WIDE), F32)]
+    outs += [((2, 4, 16, 1408), BF), ((2, 16, WIDE), BF), ((16, WIDE), BF)] if last else []
+    n_vmem = len(outs)
+    outs += [((WIDE, 384), BF), ((WIDE, 1024), BF), ((512, WIDE), BF), ((4, 4, 16, WIDE), BF)]
+    outs = outs[:n_vmem] + [(s, BF) for s in PARTS]
+    outs += [((3,) + REDUCE[n][3], BF) for n in MLP] * 2 if last else []
+    shapes = WEIGHTS[:2] + [(4, 2, 4, 48, 512), (4, 2, 4, 48, 512), (4, 2, 4, 16, WIDE)]
+    scratch = [vm(s) for s in shapes] + [
+        vm((1024, WIDE)), vm((1024, WIDE)), vm((1024, 384)), vm((1024, 512)), vm((1024, 512)),
         vm((1024, 1024)), vm((1024, 256)), vm((1024, 256)),
         vm((1024, 128)), vm((1024, 128)), vm((128, 1024)), vm((1024, 128), F32), vm((1024, 128), F32),
         vm((1024, 256), F32), vm((1024, 384)), vm((1024, 384)), vm((128, WIDE), F32),
-        vm((1024, WIDE)), vm((1024, 256)), vm((1024, WIDE)), vm((1024, 512)),
-        vm((WIDE, 384)), vm((WIDE, 1024)), vm((512, WIDE)), vm((2, 2, 4, 16, WIDE)), vm((4, 256, WIDE), F32),
-    ] + rs_scratch() + sems()
-    weights = [w.reshape(s) for w, s in zip(weights, WEIGHTS)]
-    ins = [grad, stream, middle, gains, cos, sin, pcol, prow, lse, *weights, *saved]
-    return run_kernel(bwd_kernel, f"layer_backward_{l}", 3 + l, ins, 9, outs, 2, scratch, 60 * 10**9)
-
-
-def reduce_grads(parts, gains):
-    layers = len(parts) // 4
-    outs = [((8, layers, 16, 1408), BF), ((2, layers, 16, WIDE), BF), ((layers, 16, WIDE), BF), ((8, WIDE), F32)]
-    scratch = reduce_scratch() * layers + [
-        vm((2, 4, layers, 16, 1408)), vm((8, layers, 16, 1408)), vm((2, layers, 16, WIDE)), vm((2, layers, 16, WIDE)),
-        vm((layers, 16, WIDE)), vm((layers, 16, WIDE)), vm((8, WIDE), F32), vm((8, WIDE), F32),
+        vm((1024, 256)), vm((1024, WIDE)), vm((1024, 512)),
+    ] + [vm(s) for s in PARTS] + [vm(s, F32) for s in RING] + rs_scratch() + sems()
+    if last:
+        scratch += reduce_scratch(("ia", "ib", "o")) + [dma(4, 6), dma(4, 6)]
+    weights = [w.reshape(s) for w, s in zip(weights, shapes)]
+    ins = [grad, stream, middle, gains, *tables, lse, *weights, *saved, *(above or ())]
+    kernel = functools.partial(bwd_kernel, l)
+    return run_kernel(kernel, f"layer_backward_{l}", 3 + l, ins, 9, outs, n_vmem, scratch)
+
+
+def reduce_grads(gains, done, parts, landed):
+    outs = [((8, 2, 16, 1408), BF), ((2, 2, 16, WIDE), BF), ((2, 16, WIDE), BF), ((8, WIDE), F32)]
+    scratch = reduce_scratch() + [
+        vm((2, 4, 2, 16, 1408)), vm((8, 2, 16, 1408)), vm((2, 2, 16, WIDE)), vm((2, 2, 16, WIDE)),
+        vm((2, 16, WIDE)), vm((2, 16, WIDE)), vm((8, WIDE), F32), vm((8, WIDE), F32),
         vm((3, 8, WIDE), F32), vm((3, 8, WIDE), F32), vm((7, 8, WIDE), F32),
-        dma(6 * layers, 6), dma(6 * layers, 6), dma(6 * layers), dma(7), dma(7), dma(13), dma(13), dma(2), dma(2), dma(2),
+        dma(7), dma(7), dma(13), dma(13), dma(2), dma(2), dma(2),
     ]
-    kernel = functools.partial(grads_kernel, layers)
-    place = {True: pltpu.VMEM, False: pl.ANY}
-    ins = [*parts, gains]
-    return pl.pallas_call(
-        kernel,
-        name="reduce_gradients",
-        out_shape=[jax.ShapeDtypeStruct(s, d) for s, d in outs],
-        in_specs=[pl.BlockSpec(memory_space=place[i == 4 * layers]) for i in range(len(ins))],
-        out_specs=[pl.BlockSpec(memory_space=pltpu.VMEM) for _ in outs],
-        scratch_shapes=scratch,
-        compiler_params=pltpu.CompilerParams(collective_id=5, has_side_effects=True, vmem_limit_bytes=60 * 2**20),
-    )(*ins)
+    return run_kernel(grads_kernel, "reduce_gradients", 5, [gains, *done, *parts, *landed], 4, outs, 4, scratch)
 
 
 def body(
@@ -1161,32 +1275,33 @@
     s_gain = lax.dynamic_update_slice(jnp.zeros((8, 256), F32), own_gains, (0, lax.rem(96 * (core * 8 + ctx), 128)))
     s_gain = jnp.stack([s_gain, s_gain])
 
-    stream = tokens[0]
+    tables = (cos, sin, pcol, prow)
+    stream, gains = tokens[0], jnp.zeros((8, WIDE), F32)
     kept = []
-    gains = jnp.zeros((8, WIDE), F32)
     for l in range(LAYERS):
-        sources = (s_gain, s_in[l], s_o[l], s_g[l], s_u[l], s_d[l])
-        outs = layer_fwd(l, stream, gains, cos, sin, pcol, prow, sources)
-        kept.append((stream, gains if l else outs[3], outs))
+        sources = (s_o[l], s_g[l], s_u[l], s_d[l])
+        if l == 0:
+            outs = layer_fwd(l, stream, gains, tables, s_in[0], sources, (s_gain, s_in[1]))
+            gains, w_in, w_next = outs[3], outs[-2], outs[-1]
+            outs = outs[:3] + outs[4:-2]
+        else:
+            w_in = w_next
+            outs = layer_fwd(l, stream, gains, tables, w_in, sources, ())
+        kept.append((stream, w_in, outs))
         stream = outs[0]
-        gains = outs[3][2:]
-        gains = jnp.concatenate([gains, jnp.zeros((2, WIDE), F32)], axis=0)
     block_out = stream.astype(BF)[None]
 
     g = cotangent[0].astype(F32)
-    gain_parts = [None] * LAYERS
-    grads = [None] * LAYERS
+    gain_parts, above = [None] * LAYERS, None
     for l in reversed(range(LAYERS)):
-        stream, gains, outs = kept[l]
-        _, middle, lse, _, normed, qkv, mixed, nmlp, gate, up, hid = outs[:11]
-        g, gain_parts[l], d_in, d_gu, d_d, d_o = layer_bwd(
-            l, g, stream, middle, gains, cos, sin, pcol, prow, lse, outs[11:], (qkv, gate, up, normed, mixed, nmlp, hid)
-        )
-        grads[l] = (
-            d_in.reshape(2, 4, 2, 2, 48, 384), d_gu.reshape(2, 4, 2, 2, 48, 1024), d_d.reshape(2, 4, 2, 2, 16, WIDE), d_o,
-        )
+        stream, w_in, outs = kept[l]
+        _, middle, lse, normed, qkv, mixed, nmlp, gate, up, hid = outs[:10]
+        saved = (qkv, gate, up, normed, mixed, nmlp, hid)
+        res = layer_bwd(l, g, stream, middle, gains, tables, lse, (w_in, *outs[10:]), saved, above)
+        g, gain_parts[l] = res[:2]
+        above = tuple(res[2:6])
     gp = jnp.concatenate([gain_parts[0][:2], gain_parts[1][:2], jnp.zeros((4, WIDE), F32)], axis=0)
-    cols, d_d, d_o, gp = reduce_grads(grads[0] + grads[1], gp)
+    cols, d_d, d_o, gp = reduce_grads(gp, res[2:5], res[5:9], res[9:13])
     cols = cols.reshape(4, 2, LAYERS, 16, 1408)[:, :, :, :12].transpose(2, 3, 1, 0, 4).reshape(LAYERS, 12, 8, 1408)
     cols = cols.astype(F32)
     d_q, d_k, d_v = unpack_grads(cols[..., :384])

time: 652 us -> 564 us (0.87)
  Pallas kernels: 591 us -> 505 us
    pallas_call x1 -> x0, Pallas kernels: 131 us -> none  [reduce_grads(): pl.pallas_call(kernel, name='reduce_gradients', out_shape=[jax.ShapeDtype...]
    pallas_call x4 -> x5, Pallas kernels: 460 us -> 505 us  [run_kernel(): pl.pallas_call(kernel, name=name, out_shape=[jax.ShapeDtypeStruct(s, d) f...]
where the time goes in v3:
time: 564 us; the launch traced here: 555 us
  Pallas kernels  505 us (90%)
  local copies, waits for them, and re-layouts  37.3 us (7%)
  other arithmetic  10.7 us (2%)
    pallas_call x5, Pallas kernels, run_kernel(): pl.pallas_call(kernel, name=name, out_shape=[jax.ShapeDtypeStruct(s, d) f...  505 us

profile of v3, /device:TPU:5, one launch (start us, length us, event | category | flops | bytes accessed | tf_op | source)
XLA Modules:
  0.0 554.9 jit_solution(555998759010795638)
XLA Ops:
  0.8 0.8 select_reduce_fusion.1
  1.6 0.7 slice_bitcast_fusion.18
  4.6 1.6 dynamic-slice_bitcast_fusion.2
  12.9 0.9 fusion.refs_4_.refs_6_
  14.1 0.8 slice_bitcast_fusion
  14.9 1.0 bitcast_convert_fusion.refs_0_
  16.4 1.0 constant_dynamic-slice_fusion.1
  17.4 2.0 copy.94
  19.8 0.9 squeeze.115.refs_9_
  21.1 1.0 squeeze.110.refs_9_
  22.1 1.0 copy.93
  23.6 1.0 squeeze.114.refs_8_
  24.9 1.0 squeeze.108.refs_8_
  26.5 120.3 %layer_forward_0.1 = (f32[128,1536]{1,0:T(8,128)}, f32[128,1536]{1,0:T(8,128)}, f32[8,256]{1,0:T(8,128)}, f32[8,1536]{1,0:T(8,128)}, bf16[1024,1536]{1,0:T(8,128...) custom-call(bf16[128,1536]{1,0:T(8,128)(2,1)} %bitcast.182, ...), custom_call_target="tpu_custom_call" | custom-call | tf_op jit(solution)/shard_map/layer_forward_0/pallas_call | solution.py:1172
  146.8 107.0 %layer_forward_1.1 = (f32[128,1536]{1,0:T(8,128)}, f32[128,1536]{1,0:T(8,128)}, f32[8,256]{1,0:T(8,128)}, bf16[1024,1536]{1,0:T(8,128)(2,1)}, bf16[1024,384]{1,0...) custom-call(f32[128,1536]{1,0:T(8,128)} %get-tuple-element.65.refs_0, ...), custom_call_target="tpu_custom_call" | custom-call | tf_op jit(solution)/shard_map/layer_forward_1/pallas_call | solution.py:1172
  253.9 1.9 convert_bitcast_fusion.1
  255.8 105.7 %layer_backward_1.1 = (f32[128,1536]{1,0:T(8,128)}, f32[8,1536]{1,0:T(8,128)}, bf16[2,4,4,48,384]{4,3,2,1,0:T(8,128)(2,1)}, bf16[2,4,4,48,1024]{4,3,2,1,0:T(8,12...) custom-call(f32[128,1536]{1,0:T(8,128)} %bitcast_convert_fusion.refs_0_, ...), custom_call_target="tpu_custom_call" | custom-call | tf_op jit(solution)/shard_map/layer_backward_1/pallas_call | solution.py:1172
  361.5 123.0 %layer_backward_0.1 = (f32[128,1536]{1,0:T(8,128)}, f32[8,1536]{1,0:T(8,128)}, bf16[2,4,16,1408]{3,2,1,0:T(8,128)(2,1)}, bf16[2,16,1536]{2,1,0:T(8,128)(2,1)}, b...) custom-call(f32[128,1536]{1,0:T(8,128)} %get-tuple-element.82.refs_0, ...), custom_call_target="tpu_custom_call" | custom-call | tf_op jit(solution)/shard_map/layer_backward_0/pallas_call | solution.py:1172
  484.5 0.8 slice.179
  485.3 0.8 slice.180
  486.7 49.1 %reduce_gradients.1 = (bf16[8,2,16,1408]{3,2,1,0:T(8,128)(2,1)}, bf16[2,2,16,1536]{3,2,1,0:T(8,128)(2,1)}, bf16[2,16,1536]{2,1,0:T(8,128)(2,1)}, f32[8,1536]{1,0:T(8,128)}) custom-call(f32[8,1536]{1,0:T(8,128)} %maximum_maximum_fusion.refs_0_, bf16[2,4,16,1408]{3,2,1,0:T(8,128)(2,1)} %get-tuple-element.104.refs_1_, ...), custom_call_target="tpu_custom_call" | custom-call | tf_op jit(solution)/shard_map/reduce_gradients/pallas_call | solution.py:1172
  535.9 0.8 constant_dynamic-slice_fusion
  537.3 0.9 slice_convert_fusion.1
  538.2 0.8 copy.87
  539.0 1.0 convert_bitcast_fusion
  539.9 0.8 copy.86
  542.6 1.0 reshape.339
  544.8 0.9 reshape.340
  546.7 1.6 reshape.342
  548.7 1.8 copy.85
  550.5 3.0 reshape.344
  553.6 0.9 copy.125
  (106 shorter events, 17.5 us)
Async XLA Ops:
  0.6 7.4 %copy-start = (bf16[2,96,1536]{2,1,0:T(8,128)(2,1)S(1)}, bf16[2,96,1536]{2,1,0:T(8,128)(2,1)}, u32[]{:S(2)}) copy-start(bf16[2,96,1536]{2,1,0:T(8,128)(2,1)} %param.15) | copy-start | bytes 1769476
  6.2 3.1 copy-start.8
  6.2 3.1 copy-start.9
  11.2 2.5 copy-start.4
  13.8 1.0 copy-start.5
  14.0 1.8 copy-start.6
  14.0 2.3 copy-start.7
  535.9 4.8 copy-start.3
  548.7 5.7 %copy-start.1 = (bf16[2,96,1536]{2,1,0:T(8,128)(2,1)S(1)}, bf16[2,96,1536]{2,1,0:T(8,128)(2,1)}, u32[]{:S(2)}) copy-start(bf16[2,96,1536]{2,1,0:T(8,128)(2,1)} %param.15) | copy-start | bytes 1769476
  550.5 3.0 copy-start.2

commit v4 on v3

--- a/solution.py
+++ b/solution.py
@@ -37,54 +37,6 @@
     return lax.dot_general(a, b, (((1,), (1,)), ((), ())), preferred_element_type=F32)
 
 
-def place_rows(span_order, first, count, span):
-    ids = first + jnp.arange(count, dtype=jnp.int32)
-    slots = jnp.arange(span_order.shape[0], dtype=jnp.int32)
-    picked = jnp.sum(
-        jnp.where((ids // span)[:, None] == slots[None, :], span_order[None, :], 0), axis=1
-    )
-    return picked * span + ids % span
-
-
-def rope_tables(places):
-    freq = ROPE_BASE ** (-2.0 * jnp.arange(HEAD // 2, dtype=F32) / HEAD)
-    angles = places.astype(F32)[:, None] * freq[None, :]
-    cos, sin = jnp.cos(angles), jnp.sin(angles)
-    one, zero = jnp.ones((places.shape[0], 16), F32), jnp.zeros((places.shape[0], 16), F32)
-    return (
-        jnp.concatenate([cos, one, cos, one], axis=1),
-        jnp.concatenate([-sin, zero, sin, zero], axis=1),
-    )
-
-
-def pack_heads(q, k, v):
-    lead = q.shape[:-1]
-    qk = jnp.concatenate([q.reshape(*lead, 2, HEAD), k.reshape(*lead, 1, HEAD)], axis=-2)
-    v = v.reshape(*lead, 3, 32)
-    tiles = jnp.concatenate([qk[..., :48], v[..., :16], qk[..., 48:], v[..., 16:]], axis=-1)
-    return tiles.reshape(*lead, 384)
-
-
-def unpack_grads(packed):
-    lead = packed.shape[:-2]
-    tiles = packed.reshape(*lead, 8, 3, 128)
-    qk = jnp.concatenate([tiles[..., :48], tiles[..., 64:112]], axis=-1)
-    v = jnp.concatenate([tiles[..., 48:64], tiles[..., 112:]], axis=-1)
-    return (
-        qk[..., :2, :].reshape(*lead, 1536),
-        qk[..., 2, :].reshape(*lead, 768),
-        v.reshape(*lead, 768),
-    )
-
-
-def spread_rows(rows):
-    r = rows.reshape(3, 2, 16, -1)
-    z = jnp.zeros_like(r[0, 0])
-    return jnp.concatenate(
-        [r[1, 1], r[2, 1], z, r[0, 0], r[1, 0], r[2, 0], z, r[0, 1]], axis=0
-    )
-
-
 class Place:
     def __init__(self):
         self.z, self.core = lax.axis_index("z"), lax.axis_index("core")
@@ -142,7 +94,19 @@
     return span_of(base, 128) if half is None else span_of(base + 64 * half, 64)
 
 
-def all_gather(me, buf, ssem, rsem, on_pair, hooks=()):
+def all_gather(*args):
+    return run(gather_steps(*args))
+
+
+def run(steps):
+    while True:
+        try:
+            next(steps)
+        except StopIteration as stop:
+            return stop.value
+
+
+def gather_steps(me, buf, ssem, rsem, on_pair, hooks=()):
     z, zp, zm, zo, core, oc = me.z, me.zp, me.zm, me.zo, me.core, me.oc
     up, down, across = {"z": zp}, {"z": zm}, {"core": oc}
     sent = [
@@ -176,6 +140,7 @@
 
     send(0, 2, 1, 3, 6)
     hook(0)
+    yield
     arrive(6)
     on_pair(z)
     arrive(0)
@@ -188,6 +153,7 @@
     arrive(3)
     send(10)
     hook(2)
+    yield
     arrive(7, 8)
     on_pair(zm)
     arrive(9, 10)
@@ -197,6 +163,7 @@
     send(11)
     arrive(5)
     send(12)
+    yield
     arrive(11, 12)
     on_pair(zo)
 
@@ -207,7 +174,11 @@
     return finish
 
 
-def reduce_scatter(me, part, whole, keep, give, take, ring_out, ring_in, ssem, rsem, fill=lambda n: None):
+def reduce_scatter(*args):
+    return run(reduce_steps(*args))
+
+
+def reduce_steps(me, part, whole, keep, give, take, ring_out, ring_in, ssem, rsem, fill=lambda n: None):
     z, zp, zm, zo, core, oc = me.z, me.zp, me.zm, me.zo, me.core, me.oc
     up, down, across = {"z": zp}, {"z": zm}, {"core": oc}
     mine = span_of(core * 128, 128)
@@ -251,6 +222,7 @@
     push(4, merged(2, 0))
     make(3, z)
     fill(0)
+    yield
     ring(0).wait_recv()
     push(2, merged(1, 0) + ring_in[0].astype(F32))
     ring(3).wait_recv()
@@ -263,6 +235,7 @@
     ring(4).wait_recv()
     own[0] = own[0] + ring_in[4].astype(F32)
     fill(2)
+    yield
     ring(2).wait_recv()
     own[0] = own[0] + ring_in[2].astype(F32)
     ring(5).wait_recv()
@@ -277,40 +250,51 @@
     return jnp.concatenate(own, axis=0), finish
 
 
+def ctx_of(slot):
+    zz, cc = slot // 2, lax.rem(slot, 2)
+    return lax.rem(zz + 2 * cc, 4) * 2 + cc
+
+
+def slot_of(ctx):
+    x, yh = ctx // 2, lax.rem(ctx, 2)
+    return lax.rem(x + 2 * yh, 4) * 2 + yh
+
+
 class Exchange:
-    def __init__(self, me, src, dst, ssem, rsem):
+    def __init__(self, me, src, dst, ssem, rsem, out):
         self.me, self.src, self.dst, self.ssem, self.rsem = me, src, dst, ssem, rsem
-
-    def copy(self, s, come):
+        same = lambda v: v
+        self.to, self.block, self.lands = (ctx_of, slot_of, same) if out else (same, same, slot_of)
+
+    def copy(self, b, come):
         return pltpu.make_async_remote_copy(
-            src_ref=self.src.at[span_of(s * 128, 128)], dst_ref=self.dst.at[span_of(come * 128, 128)],
-            send_sem=self.ssem.at[s], recv_sem=self.rsem.at[come],
-            device_id=at_ctx(s), device_id_type=MESH,
+            src_ref=self.src.at[span_of(b * 128, 128)], dst_ref=self.dst.at[span_of(come * 128, 128)],
+            send_sem=self.ssem.at[b], recv_sem=self.rsem.at[come],
+            device_id=at_ctx(self.to(b)), device_id_type=MESH,
         )
 
-    def send(self, s):
-        c = self.me.c
-
-        @pl.when(s != c)
+    def send(self, b):
+        there, come = self.to(b), self.lands(self.me.c)
+
+        @pl.when(there != self.me.c)
         def _():
-            self.copy(s, c).start()
-
-        @pl.when(s == c)
+            self.copy(b, come).start()
+
+        @pl.when(there == self.me.c)
         def _():
-            rows = span_of(s * 128, 128)
-            self.dst[rows] = self.src[rows]
+            self.dst[span_of(come * 128, 128)] = self.src[span_of(b * 128, 128)]
 
     def arrive(self):
         @pl.loop(1, 8)
         def _(k):
             there = lax.rem(self.me.c + k, 8)
-            self.copy(there, there).wait_recv()
+            self.copy(self.block(there), self.lands(there)).wait_recv()
 
     def finish(self):
         @pl.loop(1, 8)
         def _(k):
             there = lax.rem(self.me.c + k, 8)
-            self.copy(there, self.me.c).wait_send()
+            self.copy(self.block(there), self.lands(self.me.c)).wait_send()
 
 
 def push(src, dst, ssem, rsem, dev):
@@ -327,14 +311,14 @@
     def own(self):
         me = self.me
         return pltpu.make_async_copy(
-            self.src.at[me.core, :, self.cols], self.dst.at[me.core, me.x, me.y, :, self.cols], self.loc
+            self.src(me.core, self.cols), self.dst.at[me.core, me.x, me.y, :, self.cols], self.loc
         )
 
     def cross(self, come=False):
         me = self.me
         row = me.oc if come else me.core
         return push(
-            self.src.at[me.oc, :, self.cols], self.dst.at[row, me.x, me.y, :, self.cols],
+            self.src(me.oc, self.cols), self.dst.at[row, me.x, me.y, :, self.cols],
             self.ssem.at[0], self.rsem.at[0], {"core": me.oc},
         )
 
@@ -382,7 +366,7 @@
 class OutGather:
     def __init__(self, me, src, dst, ssem, rsem, loc):
         self.me, self.dst, self.ssem, self.rsem = me, dst, ssem, rsem
-        self.own = pltpu.make_async_copy(src, dst.at[me.y], loc)
+        self.src, self.loc = src, loc
         self.far = lax.rem(me.x + 4 - me.z, 4)
 
     def copy(self, stage, k, come):
@@ -391,15 +375,27 @@
         ref, i = self.dst.at[y], 3 * stage + k - 1
         return push(ref, ref, self.ssem.at[i], self.rsem.at[i], me.near("xy"[stage], k))
 
+    def own(self):
+        y, yl = self.me.y, self.me.yl
+        return [
+            pltpu.make_async_copy(
+                self.src.at[pl.ds(pl.multiple_of(row, 16), 16)], self.dst.at[y, to : to + 16], self.loc.at[i]
+            )
+            for i, (row, to) in enumerate(((48 - 16 * yl, 0), (80 - 16 * yl, 16), (16 * yl, 48)))
+        ]
+
     def zero(self):
         @pl.when(self.far == 0)
         def _():
-            self.own.start()
+            for copy in self.own():
+                copy.start()
+            self.dst[self.me.y, 32:48] = jnp.zeros((16, WIDE), BF)
 
     def one(self):
         @pl.when(self.far == 0)
         def _():
-            self.own.wait()
+            for copy in self.own():
+                copy.wait()
             for k in (2, 1, 3):
                 self.copy(0, k, False).start()
 
@@ -590,19 +586,25 @@
     g_attn, g_mlp = (slice(2 * l + i, 2 * l + i + 1) for i in (0, 1))
     refs = list(refs)
     take = lambda n: [refs.pop(0) for _ in range(n)]
-    stream, gains_in, cos, sin, pcol, prow = take(6)
+    (stream,) = take(1)
+    (gains_in,) = (None,) if first else take(1)
+    cos, sin, pcol, prow = take(4)
     (h_in,) = take(1)
-    s_o, s_g, s_u, s_d = take(4)
+    w_out, w_down, s_g, s_u = take(4)
     s_gain, s_next = take(2) if first else (None, None)
-    o_stream, o_middle, o_lse = take(3)
+    (cot,) = (None,) if first else take(1)
+    (o_stream,) = take(1) if first else (None,)
+    o_middle, o_lse = take(2)
     (o_gains,) = take(1) if first else (gains_in,)
     o_normed, o_qkv, o_mixed, o_nmlp, o_gate, o_up, o_hidden, o_wo, o_wg, o_wu, o_wd = take(11)
     o_win, o_next = take(2) if first else (None, None)
+    (o_down,) = (None,) if first else take(1)
     w_in, w_o, w_g, w_u, w_d = take(5)
     buf1, buf2, qs, qr, ms, mr, gate_v, up_v, hid, keys, vals, vals_t, middle = take(13)
     whole, keep, give, got, ring_out, ring_in = take(6)
     ag_s, ag_r, ag2_s, ag2_r, rs_s, rs_r, rs2_s, rs2_r, ax_s, ax_r, bx_s, bx_r, loc, loc2, ga_s, ga_r = take(16)
     w_gain, w_next = take(2) if first else (None, None)
+    cot_all, cot_s, cot_r = (None,) * 3 if first else take(3)
     me = Place()
     stores = []
 
@@ -612,20 +614,26 @@
 
     n_item = [0]
 
+    def down_rows(core, cols):
+        row = pl.multiple_of((core * 4 + me.z) * 32 + me.yl * 16, 16)
+        return w_down.at[l, pl.ds(row, 16), cols]
+
     def item(src, dst, order, *cols):
         i = n_item[0]
         n_item[0] += 1
+        if not callable(src):
+            src = lambda core, cols, ref=src: ref.at[core, :, cols]
         return Gather(me, src, dst, ga_s.at[i], ga_r.at[i], loc.at[i], order, cols)
 
-    g_g, g_u = item(s_g, w_g, "xy", 0, 512), item(s_u, w_u, "yx", 0, 512)
-    g_d = [item(s_d, w_d, "xy", 0, 768), item(s_d, w_d, "yx", 768, WIDE)]
-    g_o = OutGather(me, s_o, w_o, ga_s.at[4], ga_r.at[4], loc.at[4])
+    g_g, g_u = item(s_g.at[l], w_g, "xy", 0, 512), item(s_u.at[l], w_u, "yx", 0, 512)
+    g_d = [item(down_rows, w_d, "xy", 0, 768), item(down_rows, w_d, "yx", 768, WIDE)]
+    g_o = OutGather(me, w_out.at[l], w_o, ga_s.at[4], ga_r.at[4], loc.at[pl.ds(10, 3)])
     n_item[0] = 5
     g_in, g_next, g_gain = [], [], []
     if first:
         g_gain = [item(s_gain, w_gain, "yx", 0, 256)]
-        g_in = [item(h_in, w_in, "yx", 0, 256), item(h_in, w_in, "xy", 256, 384)]
-        g_next = [item(s_next, w_next, "yx", 0, 256), item(s_next, w_next, "xy", 256, 384)]
+        g_in = [item(h_in.at[0], w_in, "yx", 0, 256), item(h_in.at[0], w_in, "xy", 256, 384)]
+        g_next = [item(s_next.at[1], w_next, "yx", 0, 256), item(s_next.at[1], w_next, "xy", 256, 384)]
     everything = g_gain + g_in + [g_o, g_g, g_u] + g_d + g_next
 
     def each(items, step):
@@ -639,11 +647,13 @@
     else:
         load_in = pltpu.make_async_copy(h_in, w_in, loc.at[5])
         load_in.start()
+        load_cot = pltpu.make_async_copy(cot, cot_all.at[own_rows], loc.at[6])
+        load_cot.start()
         s = stream[...]
         raw[own_rows] = (s * rms_of(s) * gains_in[g_attn, :]).astype(BF)
     me.greet(me.layer_partners())
     each(everything, "zero")
-    ax = Exchange(me, qs, qr, ax_s, ax_r)
+    ax = Exchange(me, qs, qr, ax_s, ax_r, True)
 
     def project(zz):
         rows = span_of(zz * 256, 256)
@@ -693,14 +703,19 @@
     else:
         load_in.wait()
         done_ag = all_gather(me, raw, ag_s, ag_r, project, (g_o.one,))
+        load_cot.wait()
+        ring = gather_steps(me, cot_all, cot_s, cot_r, lambda zz: None)
+        next(ring)
     g_o.two()
     each((g_g, g_u), "one")
     ax.arrive()
+    if not first:
+        next(ring)
     store(buf1, o_normed)
     store(qr, o_qkv)
     split_packed(qr, keys, vals)
     vals_t[...] = flip(vals)
-    bx = Exchange(me, ms, mr, bx_s, bx_r)
+    bx = Exchange(me, ms, mr, bx_s, bx_r, False)
 
     @pl.loop(0, 8)
     def _(k):
@@ -720,6 +735,8 @@
         bx.send(p)
 
     each((g_g, g_u), "two")
+    if not first:
+        next(ring)
     each(g_d, "one")
     g_o.three()
     bx.arrive()
@@ -760,15 +777,24 @@
     for w, o in pairs:
         store(w, o)
 
+    if not first:
+        done_cot = run(ring)
+        store(cot_all, o_down)
+        for done in (done_ag, ax.finish, bx.finish, done_ag2, done_cot):
+            done()
+        each(everything, "finish")
+        for copy in stores:
+            copy.wait()
+        return
+
     def down_part(zz):
         return mm(hid[span_of(zz * 256, 256)], w_d[...].reshape(512, WIDE))
 
     total, done_rs2 = reduce_scatter(me, down_part, *rs, rs2_s, rs2_r)
     o_stream[...] = middle[...] + total
     each(g_next, "three")
-    if first:
-        store(w_next, o_next)
-    for done in ((() if first else (done_ag,)) + (ax.finish, bx.finish, done_ag2, done_rs2)):
+    store(w_next, o_next)
+    for done in (ax.finish, bx.finish, done_ag2, done_rs2):
         done()
     each(everything, "finish")
     for copy in stores:
@@ -791,7 +817,9 @@
     grad, stream, middle, gains, cos, sin, pcol, prow, lse = take(9)
     h_in, h_o, h_g, h_u, h_d, h_qkv, h_gate, h_up, h_normed, h_mixed, h_nmlp, h_hidden = take(12)
     above = take(4) if last else None
+    (h_down,) = (None,) if last else take(1)
     o_grad, o_gains = take(2)
+    (o_block,) = (None,) if last else take(1)
     o_fin, o_down, o_out = take(3) if last else (None,) * 3
     parts = take(4)
     o_din, o_dgu, o_dd, o_do = parts
@@ -816,6 +844,7 @@
         stores[-1].start()
 
     reds, early = {}, {}
+    rs3 = refs
     if last:
         stage = {
             "g": (w_g.at[3], w_g.at[0:3]), "u": (w_u.at[3], w_u.at[0:3]),
@@ -830,7 +859,11 @@
         }
 
     own_rows = slot_rows(me.z, me.core)
-    buf1[own_rows] = grad[...].astype(BF)
+    if last:
+        buf1[own_rows] = grad[...].astype(BF)
+    else:
+        load_down = pltpu.make_async_copy(h_down, buf1, loc.at[11])
+        load_down.start()
     me.greet(me.layer_partners())
     for red in reds.values():
         red.one()
@@ -845,7 +878,12 @@
         gu[rows, 0:512] = (hg * up * (sig * (1.0 + gate * (1.0 - sig)))).astype(BF)
         gu[rows, 512:1024] = (hg * (gate * sig)).astype(BF)
 
-    done_ag = all_gather(me, buf1, ag_s, ag_r, unit)
+    if last:
+        done_ag = all_gather(me, buf1, ag_s, ag_r, unit)
+    else:
+        load_down.wait()
+        for zz in range(4):
+            unit(zz)
     for load in loads[3:]:
         load.wait()
 
@@ -877,10 +915,10 @@
     e, done_rs = reduce_scatter(me, mlp_part, *rs, rs_s, rs_r, fill1)
     part, gain_part = norm_back_of(e, middle[...], gains[g_mlp, :])
     o_gains[1:2, :] = gain_part
-    gm = grad[...] + part
+    gm = grad[...].astype(F32) + part
     mid_grad[...] = gm
     buf2[own_rows] = gm.astype(BF)
-    ax = Exchange(me, mgs, mgr, ax_s, ax_r)
+    ax = Exchange(me, mgs, mgr, ax_s, ax_r, True)
 
     def mixed_back(zz):
         rows = span_of(zz * 256, 256)
@@ -904,7 +942,8 @@
             red.two()
 
     done_ag2 = all_gather(me, buf2, ag2_s, ag2_r, mixed_back, (hook0, hook1, hook2))
-    done_ag()
+    if last:
+        done_ag()
     normed = buf1
     load_normed = pltpu.make_async_copy(h_normed, normed, loc.at[11])
     load_normed.start()
@@ -920,6 +959,14 @@
                 piece = jnp.concatenate([piece, chunk[first + 1][: shift - 4]], axis=0)
             d_o[head * 2 + b // 4, b % 4] = padded(piece[0:12])
     store(d_o, o_do)
+    if not last:
+
+        def down_part(zz):
+            return mm(hid[span_of(zz * 256, 256)], w_d[...].reshape(512, WIDE))
+
+        done_rs()
+        final = reduce_steps(me, down_part, whole, keep, *rs3)
+        next(final)
     if last:
         stores[0].wait()
         early["da"].one()
@@ -943,7 +990,9 @@
         dqs[rows, 0:128] = dq[0:128]
         dqs[rows, 128:256] = dq[128:256]
 
-    bx = Exchange(me, ps, pr, bx_s, bx_r)
+    if not last:
+        next(final)
+    bx = Exchange(me, ps, pr, bx_s, bx_r, False)
     v0, _, _ = lane_masks(128)
 
     @pl.loop(0, 8)
@@ -960,7 +1009,10 @@
         stores[1].wait()
         early["g"].one()
         early["u"].one()
-    done_rs()
+        done_rs()
+    else:
+        total, done_rs3 = run(final)
+        o_block[...] = (middle[...] + total).astype(BF)
     load_normed.wait()
     bx.arrive()
     pre = qr
@@ -990,6 +1042,8 @@
         done()
     for red in reds.values():
         red.finish()
+    if not last:
+        done_rs3()
     for red in early.values():
         red.arrive()
         red.finish((0,))
@@ -1004,12 +1058,12 @@
 def grads_kernel(*refs):
     refs = list(refs)
     take = lambda n: [refs.pop(0) for _ in range(n)]
-    gains, fin1, down1, out1 = take(4)
+    gp0, gp1, fin1, down1, out1 = take(5)
     parts = take(4)
     landed = dict(zip(MLP, take(4)))
     o_rows, o_down, o_out, o_gains = take(4)
     reds = make_reduces(Place(), parts, refs, landed, True)
-    fin_s, fin_r, down_s, down_r, out_s, out_r, sum_a, sum_b, got_a, got_b, got_c = take(11)
+    gains, fin_s, fin_r, down_s, down_r, out_s, out_r, sum_a, sum_b, got_a, got_b, got_c = take(12)
     fin_ss, fin_rs, gain_s, gain_r, down_ss, down_rs, out_ss = take(7)
     me = Place()
     mlp, rest = [reds[n] for n in MLP], [reds[n] for n in ("ia", "ib", "o")]
@@ -1022,6 +1076,9 @@
     apart = me.x != me.z
     for red in reds.values():
         red.load()
+    gains[...] = jnp.zeros_like(gains)
+    gains[0:2] = gp0[0:2]
+    gains[2:4] = gp1[0:2]
     me.greet(
         [me.near("x", k) for k in (1, 2, 3)] + [me.near("y", k) for k in (1, 2, 3)]
         + [mate(*m) for m in group] + [{"yl": 1 - me.yl, "core": me.oc}],
@@ -1039,10 +1096,22 @@
             total = total + got[k - 1]
         dst[...] = total
 
+    slot = me.z * 2 + me.core
+
+    def fin(l, i, come):
+        k, c = group[i]
+        to_z, to_core = lax.rem(me.z + k, 4), lax.rem(me.core + c, 2)
+        from_z = lax.rem(me.z + 4 - k, 4)
+        dst = fin_r.at[from_z * 2 + to_core, l] if come else fin_r.at[slot, l]
+        return push(fin_s.at[to_core, to_z, l], dst, fin_ss.at[l, i], fin_rs.at[l, i], mate(k, c))
+
     for k in (1, 2, 3):
         gain_copy(0, "y", gains, got_a, k).start()
     for red in rest:
         red.one()
+    fin_s[:, :, 1] = fin1[...]
+    for i in range(7):
+        fin(1, i, False).start()
     for red in mlp:
         red.two()
     for red in rest:
@@ -1059,19 +1128,9 @@
 
     for i in range(7):
         gain_mate(i).start()
-    fin_s[:, :, 1] = fin1[...]
     down_s[:, 1] = down1[...]
     out_s[1] = out1[...]
     finish_reduces(reds, fin_s.at[:, :, 0], down_s.at[:, 0], out_s.at[0])
-    slot = me.z * 2 + me.core
-
-    def fin(i, come):
-        k, c = group[i]
-        to_z, to_core = lax.rem(me.z + k, 4), lax.rem(me.core + c, 2)
-        from_z = lax.rem(me.z + 4 - k, 4)
-        dst = fin_r.at[from_z * 2 + to_core] if come else fin_r.at[slot]
-        return push(fin_s.at[to_core, to_z], dst, fin_ss.at[i], fin_rs.at[i], mate(k, c))
-
     def down(dp, half):
         dev = {"core": jnp.int32(dp), "yl": me.core}
         return push(down_s.at[dp], down_r.at[half], down_ss.at[dp], down_rs.at[half], dev)
@@ -1082,7 +1141,7 @@
         return push(out_s, out_r, out_ss.at[0], out_ss.at[1], mirror)
 
     for i in range(7):
-        fin(i, False).start()
+        fin(0, i, False).start()
     for dp in range(2):
         keep = mine & (me.core == dp)
 
@@ -1109,7 +1168,8 @@
         total = total + got_c[i]
     o_gains[...] = total
     for i in range(7):
-        fin(i, True).wait_recv()
+        fin(0, i, True).wait_recv()
+        fin(1, i, True).wait_recv()
     o_rows[...] = fin_r[...]
     for half in range(2):
 
@@ -1133,7 +1193,8 @@
         gain_copy(1, "x", sum_a, got_b, k).wait_send()
     for i in range(7):
         gain_mate(i).wait_send()
-        fin(i, False).wait_send()
+        fin(0, i, False).wait_send()
+        fin(1, i, False).wait_send()
     for dp in range(2):
 
         @pl.when(jnp.logical_not(mine & (me.core == dp)))
@@ -1158,7 +1219,7 @@
 
 
 def sems():
-    return [dma(n) for n in (13, 13, 13, 13, 10, 10, 10, 10, 8, 8, 8, 8, 12, 16)]
+    return [dma(n) for n in (13, 13, 13, 13, 10, 10, 10, 10, 8, 8, 8, 8, 16, 16)]
 
 
 WEIGHTS = [(WIDE, 384), (256, WIDE), (WIDE, 512), (WIDE, 512), (512, WIDE)]
@@ -1184,12 +1245,12 @@
 
 def layer_fwd(l, stream, gains, tables, h_in, sources, extra):
     first = l == 0
-    outs = [((128, WIDE), F32), ((128, WIDE), F32), ((8, 256), F32)] + ([((8, WIDE), F32)] if first else [])
+    outs = [((128, WIDE), F32)] * (2 if first else 1) + [((8, 256), F32)] + ([((8, WIDE), F32)] if first else [])
     n_vmem = len(outs)
     outs += [
         ((1024, WIDE), BF), ((1024, 384), BF), ((1024, 256), BF), ((1024, WIDE), BF),
         ((1024, 512), BF), ((1024, 512), BF), ((1024, 512), BF),
-    ] + [(s, BF) for s in SPLIT[1:]] + ([(SPLIT[0], BF)] * 2 if first else [])
+    ] + [(s, BF) for s in SPLIT[1:]] + ([(SPLIT[0], BF)] * 2 if first else [((1024, WIDE), BF)])
     scratch = [vm(s) for s in SPLIT] + [
         vm((1024, WIDE)), vm((1024, WIDE)), vm((1024, 384)), vm((1024, 384)), vm((1024, 256)), vm((1024, 256)),
         vm((1024, 512)), vm((1024, 512)), vm((1024, 512)),
@@ -1197,18 +1258,19 @@
     ] + [vm(s, F32) for s in RING] + rs_scratch() + sems() + [dma(10, 7), dma(10, 7)]
     if first:
         scratch += [vm((2, 4, 4, 8, 256), F32), vm(SPLIT[0])]
-    ins = [stream, gains, *tables, h_in, *sources, *extra]
+    else:
+        scratch += [vm((1024, WIDE)), dma(13), dma(13)]
+    ins = [stream] + ([] if first else [gains]) + [*tables, h_in, *sources, *extra]
     kernel = functools.partial(fwd_kernel, l)
-    return run_kernel(kernel, f"layer_forward_{l}", 1 + l, ins, 6, outs, n_vmem, scratch)
+    return run_kernel(kernel, f"layer_forward_{l}", 1 + l, ins, 5 if first else 6, outs, n_vmem, scratch)
 
 
 def layer_bwd(l, grad, stream, middle, gains, tables, lse, weights, saved, above):
     last = l == 0
     outs = [((128, WIDE), F32), ((8, WIDE), F32)]
-    outs += [((2, 4, 16, 1408), BF), ((2, 16, WIDE), BF), ((16, WIDE), BF)] if last else []
+    outs += [((2, 4, 16, 1408), BF), ((2, 16, WIDE), BF), ((16, WIDE), BF)] if last else [((128, WIDE), BF)]
     n_vmem = len(outs)
-    outs += [((WIDE, 384), BF), ((WIDE, 1024), BF), ((512, WIDE), BF), ((4, 4, 16, WIDE), BF)]
-    outs = outs[:n_vmem] + [(s, BF) for s in PARTS]
+    outs += [(s, BF) for s in PARTS]
     outs += [((3,) + REDUCE[n][3], BF) for n in MLP] * 2 if last else []
     shapes = WEIGHTS[:2] + [(4, 2, 4, 48, 512), (4, 2, 4, 48, 512), (4, 2, 4, 16, WIDE)]
     scratch = [vm(s) for s in shapes] + [
@@ -1220,98 +1282,206 @@
     ] + [vm(s) for s in PARTS] + [vm(s, F32) for s in RING] + rs_scratch() + sems()
     if last:
         scratch += reduce_scratch(("ia", "ib", "o")) + [dma(4, 6), dma(4, 6)]
+    else:
+        scratch += rs_scratch() + [dma(10), dma(10)]
     weights = [w.reshape(s) for w, s in zip(weights, shapes)]
     ins = [grad, stream, middle, gains, *tables, lse, *weights, *saved, *(above or ())]
     kernel = functools.partial(bwd_kernel, l)
     return run_kernel(kernel, f"layer_backward_{l}", 3 + l, ins, 9, outs, n_vmem, scratch)
 
 
-def reduce_grads(gains, done, parts, landed):
+def picks(rows, cols, test):
+    r = lax.broadcasted_iota(jnp.int32, (rows, cols), 0)
+    c = lax.broadcasted_iota(jnp.int32, (rows, cols), 1)
+    return jnp.where(test(r, c), 1.0, 0.0).astype(BF)
+
+
+def packed_place(n):
+    t, i = n // 128, n % 128
+    value = ((i >= 48) & (i < 64)) | (i >= 112)
+    feature = jnp.where(value, 32 * t + jnp.where(i < 64, i - 48, i - 96), jnp.where(i < 48, i, i - 16))
+    return t, feature, value
+
+
+def prepare_kernel(
+    order, wq, wk, wv, wg, wu, ga, gm, o_in, o_g, o_u, o_gain, o_cos, o_sin, o_pcol, o_prow, vq, vk, vv, vg, vu, loc
+):
+    core, z, yl = lax.axis_index("core"), lax.axis_index("z"), lax.axis_index("yl")
+    own = pl.ds(pl.multiple_of(yl * 48, 16), 48)
+    loads = [
+        pltpu.make_async_copy(h.at[:, own], v, loc.at[i])
+        for i, (h, v) in enumerate(((wq, vq), (wk, vk), (wv, vv), (wg, vg), (wu, vu)))
+    ]
+    for load in loads:
+        load.start()
+    ctx = lax.axis_index("x") * 2 + lax.axis_index("yh")
+    for span in range(16):
+        o_pcol[64 * span : 64 * span + 64] = order[span] * 64 + lax.broadcasted_iota(jnp.int32, (64, 1), 0)
+    lane = lax.broadcasted_iota(jnp.int32, (1, 256), 1)
+    for p in range(8):
+        start = jnp.where(lane % 128 < 64, order[2 * p], order[2 * p + 1]) * 64
+        o_prow[p : p + 1, :] = start + lane % 64
+    row = lax.broadcasted_iota(jnp.int32, (128, 128), 0)
+    col = lax.broadcasted_iota(jnp.int32, (128, 128), 1)
+    place = jnp.where(row < 64, order[2 * ctx], order[2 * ctx + 1]) * 64 + row % 64
+    turning = (col % 64) < 48
+    freq = jnp.exp((col % 64).astype(F32) * (-2.0 * math.log(ROPE_BASE) / HEAD))
+    angles = place.astype(F32) * freq
+    cos = jnp.where(turning, jnp.cos(angles), 1.0)
+    sin = jnp.where(turning, jnp.sin(angles), 0.0)
+    sin = jnp.where(col < 64, -sin, sin)
+    for half in range(2):
+        o_cos[128 * half : 128 * half + 128] = cos
+        o_sin[128 * half : 128 * half + 128] = sin
+    owner = core * 8 + ctx
+    shift = lax.rem(96 * owner, 128)
+    move = picks(96, 256, lambda r, c: c == r + shift)
+    zero = jnp.zeros((4, 96), F32)
+    both = jnp.concatenate([ga[0:1], gm[0:1], ga[1:2], gm[1:2]], axis=0).astype(F32)
+    placed = mm(jnp.concatenate([both, zero], axis=0).astype(BF), move)
+    o_gain[0] = placed
+    o_gain[1] = placed
+    spread = [
+        picks(1024, 128, lambda r, c, j=cc * 4 + z: (r // 256 == c // 32) & (r % 256 == 32 * j + c % 32)) for cc in range(2)
+    ]
+    spread = jnp.concatenate(spread, axis=1)
+
+    def query(r, n, j):
+        t, f, value = packed_place(n)
+        return jnp.logical_not(value) & (t < 2) & (r == j * 192 + t * 96 + f)
+
+    def key(r, n, j):
+        t, f, value = packed_place(n)
+        return jnp.logical_not(value) & (t == 2) & (r == j * 96 + f)
+
+    def val(r, n, j):
+        t, f, value = packed_place(n)
+        return value & (r == j * 96 + f)
+
+    for load in loads[:3]:
+        load.wait()
+    for cc in range(2):
+        j = cc * 4 + z
+        out = mm(vq[...].reshape(96, WIDE), picks(WIDE, 384, lambda r, n: query(r, n, j)))
+        out = out + mm(vk[...].reshape(96, 768), picks(768, 384, lambda r, n: key(r, n, j)))
+        out = out + mm(vv[...].reshape(96, 768), picks(768, 384, lambda r, n: val(r, n, j)))
+        o_in[:, cc] = out.astype(BF).reshape(LAYERS, 48, 384)
+    for load in loads[3:]:
+        load.wait()
+    for v, o in ((vg, o_g), (vu, o_u)):
+        for b in range(4):
+            out = mm(v[:, :, 1024 * b : 1024 * b + 1024].reshape(96, 1024), spread).astype(BF)
+            for cc in range(2):
+                o[:, cc, :, 128 * b : 128 * b + 128] = out[:, 128 * cc : 128 * cc + 128].reshape(LAYERS, 48, 128)
+
+
+def prepare(order, wq, wk, wv, wg, wu, ga, gm):
+    shapes = [((LAYERS, 2, 48, 384), BF), ((LAYERS, 2, 48, 512), BF), ((LAYERS, 2, 48, 512), BF), ((2, 8, 256), F32)]
+    shapes += [((256, 128), F32), ((256, 128), F32), ((1024, 1), jnp.int32), ((8, 256), jnp.int32)]
+    in_vmem = pl.BlockSpec(memory_space=pltpu.VMEM)
+    return pl.pallas_call(
+        prepare_kernel,
+        name="prepare_sources",
+        out_shape=[jax.ShapeDtypeStruct(s, d) for s, d in shapes],
+        in_specs=[pl.BlockSpec(memory_space=pltpu.SMEM)] + [pl.BlockSpec(memory_space=pl.ANY)] * 5 + [in_vmem] * 2,
+        out_specs=[in_vmem] * 8,
+        scratch_shapes=[vm((LAYERS, 48, n)) for n in (WIDE, 768, 768, 4096, 4096)] + [dma(5)],
+        compiler_params=pltpu.CompilerParams(vmem_limit_bytes=60 * 2**20),
+    )(order, wq, wk, wv, wg, wu, ga, gm)
+
+
+def assemble_kernel(cols, downs, outs, o_q, o_k, o_v, o_o, o_g, o_u, o_d):
+    def member(j, lo, hi):
+        return cols[j % 4 * 2 + j // 4, :, :, lo:hi].reshape(32, hi - lo)
+
+    def put(dst, lo, hi, value):
+        for l in range(LAYERS):
+            dst[:, l, lo:hi] = value[16 * l : 16 * l + 12]
+
+    def query(n, c, i):
+        t, f, value = packed_place(n)
+        return jnp.logical_not(value) & (t < 2) & (c == i * 192 + t * 96 + f)
+
+    def key(n, c, i):
+        t, f, value = packed_place(n)
+        return jnp.logical_not(value) & (t == 2) & (c == i * 96 + f)
+
+    def val(n, c, i):
+        t, f, value = packed_place(n)
+        return value & (c == i * 96 + f)
+
+    for dst, test, per in ((o_q, query, 2), (o_k, key, 4), (o_v, val, 4)):
+        moves = [picks(384, 384, lambda n, c, i=i: test(n, c, i)) for i in range(per)]
+        for m in range(8 // per):
+            total = sum(mm(member(per * m + i, 0, 384), moves[i]) for i in range(per))
+            put(dst, 384 * m, 384 * m + 384, total)
+    back = [picks(128, 1024, lambda r, c, j=j: (c // 256 == r // 32) & (c % 256 == 32 * j + r % 32)) for j in range(8)]
+    for dst, start in ((o_g, 384), (o_u, 896)):
+        for b in range(4):
+            total = sum(mm(member(j, start + 128 * b, start + 128 * b + 128), back[j]) for j in range(8))
+            put(dst, 1024 * b, 1024 * b + 1024, total)
+    for l in range(LAYERS):
+        o_o[:, l, :] = outs[l, 0:12].astype(F32)
+        for h in range(2):
+            o_d[l, 16 * h : 16 * h + 16] = downs[h, l].astype(F32)
+
+
+def assemble(cols, downs, outs):
+    shapes = [(12, LAYERS, n) for n in (WIDE, 768, 768, WIDE, 4096, 4096)] + [(LAYERS, 32, WIDE)]
+    in_vmem = pl.BlockSpec(memory_space=pltpu.VMEM)
+    *grads, d_d = pl.pallas_call(
+        assemble_kernel,
+        name="assemble_gradients",
+        out_shape=[jax.ShapeDtypeStruct(s, F32) for s in shapes],
+        in_specs=[in_vmem] * 3,
+        out_specs=[in_vmem] * 7,
+        compiler_params=pltpu.CompilerParams(vmem_limit_bytes=60 * 2**20),
+    )(cols, downs, outs)
+    return [grad.transpose(1, 0, 2) for grad in grads] + [d_d]
+
+
+def reduce_grads(gain_parts, done, parts, landed):
     outs = [((8, 2, 16, 1408), BF), ((2, 2, 16, WIDE), BF), ((2, 16, WIDE), BF), ((8, WIDE), F32)]
     scratch = reduce_scratch() + [
-        vm((2, 4, 2, 16, 1408)), vm((8, 2, 16, 1408)), vm((2, 2, 16, WIDE)), vm((2, 2, 16, WIDE)),
+        vm((8, WIDE), F32), vm((2, 4, 2, 16, 1408)), vm((8, 2, 16, 1408)), vm((2, 2, 16, WIDE)), vm((2, 2, 16, WIDE)),
         vm((2, 16, WIDE)), vm((2, 16, WIDE)), vm((8, WIDE), F32), vm((8, WIDE), F32),
         vm((3, 8, WIDE), F32), vm((3, 8, WIDE), F32), vm((7, 8, WIDE), F32),
-        dma(7), dma(7), dma(13), dma(13), dma(2), dma(2), dma(2),
+        dma(2, 7), dma(2, 7), dma(13), dma(13), dma(2), dma(2), dma(2),
     ]
-    return run_kernel(grads_kernel, "reduce_gradients", 5, [gains, *done, *parts, *landed], 4, outs, 4, scratch)
+    return run_kernel(grads_kernel, "reduce_gradients", 5, [*gain_parts, *done, *parts, *landed], 5, outs, 4, scratch)
 
 
 def body(
     tokens, span_order, attn_gain, w_query, key_matrix, value_matrix, w_out, mlp_gain, w_gate, w_up,
     w_down, cotangent,
 ):
-    rows = tokens.shape[1]
     core, z, yl = lax.axis_index("core"), lax.axis_index("z"), lax.axis_index("yl")
     ctx = lax.axis_index("x") * 2 + lax.axis_index("yh")
-    seq_len = 8 * rows
-    span = seq_len // span_order.shape[0]
-    cos, sin = rope_tables(place_rows(span_order, ctx * rows, rows, span))
-    cos, sin = jnp.tile(cos, (2, 1)), jnp.tile(sin, (2, 1))
-    places = place_rows(span_order, 0, seq_len, span)
-    pcol = places[:, None]
-    prow = jnp.tile(places.reshape(8, rows), (1, 2))
-
-    def pick(values, index, axis):
-        return lax.dynamic_index_in_dim(values, index, axis=axis, keepdims=False)
-
-    def half(w):
-        return lax.dynamic_slice_in_dim(w, yl * 48, 48, axis=1)
-
-    def heads(w, n):
-        return pick(half(w).reshape(LAYERS, 48, 2, 4, n), z, 3)
-
-    s_in = pack_heads(heads(w_query, 192), heads(key_matrix, 96), heads(value_matrix, 96)).transpose(0, 2, 1, 3)
-
-    def hidden(w):
-        own = pick(half(w).reshape(LAYERS, 48, 16, 2, 4, 32), z, 4)
-        return own.transpose(0, 3, 1, 2, 4).reshape(LAYERS, 2, 48, 512)
-
-    s_g, s_u = hidden(w_gate), hidden(w_up)
-    s_d = pick(pick(w_down.reshape(LAYERS, 2, 4, 2, 16, WIDE), z, 2), yl, 2)
-    s_o = jnp.stack([spread_rows(w_out[l]) for l in range(LAYERS)])
-    s_o = lax.dynamic_slice_in_dim(s_o, yl * 64, 64, axis=1)
-    own_gains = jnp.concatenate([attn_gain[:1], mlp_gain[:1], attn_gain[1:], mlp_gain[1:]], axis=0).astype(F32)
-    s_gain = lax.dynamic_update_slice(jnp.zeros((8, 256), F32), own_gains, (0, lax.rem(96 * (core * 8 + ctx), 128)))
-    s_gain = jnp.stack([s_gain, s_gain])
-
-    tables = (cos, sin, pcol, prow)
-    stream, gains = tokens[0], jnp.zeros((8, WIDE), F32)
+    s_in, s_g, s_u, s_gain, *tables = prepare(
+        span_order, w_query, key_matrix, value_matrix, w_gate, w_up, attn_gain, mlp_gain
+    )
+    stream, gains = tokens[0], None
     kept = []
-    for l in range(LAYERS):
-        sources = (s_o[l], s_g[l], s_u[l], s_d[l])
-        if l == 0:
-            outs = layer_fwd(l, stream, gains, tables, s_in[0], sources, (s_gain, s_in[1]))
-            gains, w_in, w_next = outs[3], outs[-2], outs[-1]
-            outs = outs[:3] + outs[4:-2]
-        else:
-            w_in = w_next
-            outs = layer_fwd(l, stream, gains, tables, w_in, sources, ())
-        kept.append((stream, w_in, outs))
-        stream = outs[0]
-    block_out = stream.astype(BF)[None]
-
-    g = cotangent[0].astype(F32)
-    gain_parts, above = [None] * LAYERS, None
+    sources = (w_out, w_down, s_g, s_u)
+    outs = layer_fwd(0, stream, gains, tables, s_in, sources, (s_gain, s_in))
+    gains, w_next = outs[3], outs[-1]
+    kept.append((stream, outs[1:3], outs[-2], outs[4:-2]))
+    stream = outs[0]
+    outs = layer_fwd(1, stream, gains, tables, w_next, sources, (cotangent[0],))
+    kept.append((stream, outs[:2], w_next, outs[2:-1]))
+    down_grad = outs[-1]
+
+    g, gain_parts, above = cotangent[0], [None] * LAYERS, (down_grad,)
     for l in reversed(range(LAYERS)):
-        stream, w_in, outs = kept[l]
-        _, middle, lse, normed, qkv, mixed, nmlp, gate, up, hid = outs[:10]
+        stream, (middle, lse), w_in, outs = kept[l]
+        normed, qkv, mixed, nmlp, gate, up, hid = outs[:7]
         saved = (qkv, gate, up, normed, mixed, nmlp, hid)
-        res = layer_bwd(l, g, stream, middle, gains, tables, lse, (w_in, *outs[10:]), saved, above)
+        res = layer_bwd(l, g, stream, middle, gains, tables, lse, (w_in, *outs[7:]), saved, above)
         g, gain_parts[l] = res[:2]
-        above = tuple(res[2:6])
-    gp = jnp.concatenate([gain_parts[0][:2], gain_parts[1][:2], jnp.zeros((4, WIDE), F32)], axis=0)
-    cols, d_d, d_o, gp = reduce_grads(gp, res[2:5], res[5:9], res[9:13])
-    cols = cols.reshape(4, 2, LAYERS, 16, 1408)[:, :, :, :12].transpose(2, 3, 1, 0, 4).reshape(LAYERS, 12, 8, 1408)
-    cols = cols.astype(F32)
-    d_q, d_k, d_v = unpack_grads(cols[..., :384])
-
-    def hidden_join(d):
-        return d.reshape(LAYERS, 12, 8, 16, 32).transpose(0, 1, 3, 2, 4).reshape(LAYERS, 12, 4096)
-
-    d_g, d_u = hidden_join(cols[..., 384:896]), hidden_join(cols[..., 896:])
-    d_d = d_d.transpose(1, 0, 2, 3).reshape(LAYERS, 32, WIDE).astype(F32)
-    d_o = d_o[:, :12].astype(F32)
+        if l:
+            block_out, above = res[2][None], tuple(res[3:])
+    cols, d_d, d_o, gp = reduce_grads(gain_parts, res[2:5], res[5:9], res[9:13])
+    d_q, d_k, d_v, d_o, d_g, d_u, d_d = assemble(cols, d_d, d_o)
     owner = (core * 8 + ctx) * 8 + yl * 4 + z
     gp = lax.dynamic_slice(gp, (0, owner * 12), (4, 12)).reshape(2, 2, 12)
     return (block_out, g[None], gp[:, 0], d_q, d_k, d_v, d_o, gp[:, 1], d_g, d_u, d_d)

time: 564 us -> 490 us (0.87)
  local copies, waits for them, and re-layouts: 37.3 us -> 2.97 us
  Pallas kernels: 505 us -> 481 us
  other arithmetic: 10.7 us -> 0 us
    pallas_call x5, Pallas kernels: 505 us -> 472 us  [run_kernel(): pl.pallas_call(kernel, name=name, out_shape=[jax.ShapeDtypeStruct(s, d) f...]
    pallas_call x0 -> x2, Pallas kernels: none -> 9.38 us  [the longest x1 5.02 us: assemble(): pl.pallas_call(assemble_kernel, name='assemble_gradients', out_shape=[jax...]
    reshape x11 -> x0, local copies, waits for them, and re-layouts: 8.38 us -> none  [the longest x4 5.44 us: hidden_join(): d.reshape(LAYERS, 12, 8, 16, 32).transpose(0, 1, 3, 2, 4)]
    squeeze x7 -> x0, local copies, waits for them, and re-layouts: 6.9 us -> none  [the longest x6 6.23 us: body(): sources = (s_o[l], s_g[l], s_u[l], s_d[l])]
where the time goes in v4:
time: 490 us; the launch traced here: 485 us
  Pallas kernels  481 us (98%)
    pallas_call x5, Pallas kernels, run_kernel(): pl.pallas_call(kernel, name=name, out_shape=[jax.ShapeDtypeStruct(s, d) f...  472 us

profile of v4, /device:TPU:5, one launch (start us, length us, event | category | flops | bytes accessed | tf_op | source)
XLA Modules:
  0.0 485.2 jit_solution(15866860871130625793)
XLA Ops:
  0.6 4.4 prepare_sources.1
  5.0 117.9 %layer_forward_0.1 = (f32[128,1536]{1,0:T(8,128)}, f32[128,1536]{1,0:T(8,128)}, f32[8,256]{1,0:T(8,128)}, f32[8,1536]{1,0:T(8,128)}, bf16[1024,1536]{1,0:T(8,128...) custom-call(bf16[128,1536]{1,0:T(8,128)(2,1)} %bitcast.32, ...), custom_call_target="tpu_custom_call" | custom-call | tf_op jit(solution)/shard_map/layer_forward_0/pallas_call | solution.py:1233
  122.9 97.7 %layer_forward_1.1 = (f32[128,1536]{1,0:T(8,128)}, f32[8,256]{1,0:T(8,128)}, bf16[1024,1536]{1,0:T(8,128)(2,1)}, bf16[1024,384]{1,0:T(8,128)(2,1)}, bf16[1024,25...) custom-call(f32[128,1536]{1,0:T(8,128)} %get-tuple-element.89.refs_0, ...), custom_call_target="tpu_custom_call" | custom-call | tf_op jit(solution)/shard_map/layer_forward_1/pallas_call | solution.py:1233
  220.6 94.8 %layer_backward_1.1 = (f32[128,1536]{1,0:T(8,128)}, f32[8,1536]{1,0:T(8,128)}, bf16[128,1536]{1,0:T(8,128)(2,1)}, bf16[2,4,4,48,384]{4,3,2,1,0:T(8,128)(2,1)}, b...) custom-call(bf16[128,1536]{1,0:T(8,128)(2,1)} %bitcast.31, ...), custom_call_target="tpu_custom_call" | custom-call | tf_op jit(solution)/shard_map/layer_backward_1/pallas_call | solution.py:1233
  315.4 116.6 %layer_backward_0.1 = (f32[128,1536]{1,0:T(8,128)}, f32[8,1536]{1,0:T(8,128)}, bf16[2,4,16,1408]{3,2,1,0:T(8,128)(2,1)}, bf16[2,16,1536]{2,1,0:T(8,128)(2,1)}, b...) custom-call(f32[128,1536]{1,0:T(8,128)} %get-tuple-element.107.refs_, ...), custom_call_target="tpu_custom_call" | custom-call | tf_op jit(solution)/shard_map/layer_backward_0/pallas_call | solution.py:1233
  432.1 0.0 copy-start.1
  432.1 44.9 %reduce_gradients.1 = (bf16[8,2,16,1408]{3,2,1,0:T(8,128)(2,1)}, bf16[2,2,16,1536]{3,2,1,0:T(8,128)(2,1)}, bf16[2,16,1536]{2,1,0:T(8,128)(2,1)}, f32[8,1536]{1,0:T(8,128)}) custom-call(f32[8,1536]{1,0:T(8,128)} %get-tuple-element.127.refs_0_, f32[8,1536]{1,0:T(8,128)} %get-tuple-element.128.refs_1_, bf16[2,4,16,1408]{3,2,1,0:T(8,128)(2,1)} %get-tuple-element.129.refs_2_, ...), custom_call_target="tpu_custom_call" | custom-call | tf_op jit(solution)/shard_map/reduce_gradients/pallas_call | solution.py:1233
  477.0 0.0 copy-start
  477.0 5.0 %assemble_gradients.1 = (f32[12,2,1536]{2,1,0:T(2,128)}, f32[12,2,768]{2,1,0:T(2,128)}, f32[12,2,768]{2,1,0:T(2,128)}, f32[12,2,1536]{2,1,0:T(2,128)}, f32[12,2,...) custom-call(bf16[8,2,16,1408]{3,2,1,0:T(8,128)(2,1)} %get-tuple-element.141.cols, ...), custom_call_target="tpu_custom_call" | custom-call | tf_op jit(solution)/shard_map/assemble_gradients/pallas_call | solution.py:1432
  482.0 0.8 constant_dynamic-slice_fusion
  482.8 0.6 fusion
  483.4 0.0 copy-done.1
  483.4 0.7 copy.25
  484.1 0.0 copy-done
  484.1 0.9 copy.26
Async XLA Ops:
  432.1 51.3 %copy-start.1 = (bf16[128,1536]{1,0:T(8,128)(2,1)S(1)}, bf16[128,1536]{1,0:T(8,128)(2,1)}, u32[]{:S(2)}) copy-start(bf16[128,1536]{1,0:T(8,128)(2,1)} %get-tuple-element.106) | copy-start | bytes 1179652
  477.0 7.1 %copy-start = (f32[128,1536]{1,0:T(8,128)S(1)}, f32[128,1536]{1,0:T(8,128)}, u32[]{:S(2)}) copy-start(f32[128,1536]{1,0:T(8,128)} %get-tuple-element.126) | copy-start | bytes 2359300

commit v5 on v4

--- a/solution.py
+++ b/solution.py
@@ -199,12 +199,12 @@
     def make(k, zz):
         whole[...] = part(zz)
         give[k] = whole[theirs].astype(BF)
-        keep[k] = whole[mine]
+        keep[k] = whole[mine].astype(BF)
         swap(k).start()
 
     def merged(k, half):
         rows = slice(64 * half, 64 * half + 64)
-        return keep[k, rows] + take[k, rows].astype(F32)
+        return keep[k, rows].astype(F32) + take[k, rows].astype(F32)
 
     def push(i, value):
         ring_out[i] = value.astype(BF)
@@ -250,21 +250,22 @@
     return jnp.concatenate(own, axis=0), finish
 
 
-def ctx_of(slot):
+def ctx_of(slot, core):
     zz, cc = slot // 2, lax.rem(slot, 2)
-    return lax.rem(zz + 2 * cc, 4) * 2 + cc
-
-
-def slot_of(ctx):
+    return lax.rem(zz + 2 * cc + core, 4) * 2 + cc
+
+
+def slot_of(ctx, core):
     x, yh = ctx // 2, lax.rem(ctx, 2)
-    return lax.rem(x + 2 * yh, 4) * 2 + yh
+    return lax.rem(x + 2 * yh + 3 * core, 4) * 2 + yh
 
 
 class Exchange:
     def __init__(self, me, src, dst, ssem, rsem, out):
         self.me, self.src, self.dst, self.ssem, self.rsem = me, src, dst, ssem, rsem
         same = lambda v: v
-        self.to, self.block, self.lands = (ctx_of, slot_of, same) if out else (same, same, slot_of)
+        ctx, slot = (lambda v, f=f: f(v, me.core) for f in (ctx_of, slot_of))
+        self.to, self.block, self.lands = (ctx, slot, same) if out else (same, same, slot)
 
     def copy(self, b, come):
         return pltpu.make_async_remote_copy(
@@ -437,7 +438,7 @@
         axis = self.order[stage]
         to = self.at(axis, k)
         src = self.inner(self.sum1, to) if stage else self.quarter(axis, to)
-        dst = (self.got2 if stage else self.got1 if self.land is None else self.land).at[k - 1]
+        dst = self.got2.at[k - 1] if stage else self.got1[k - 1] if self.land is None else self.land.at[k - 1]
         i = 3 * stage + k - 1
         return push(src, dst, self.ssem.at[i], self.rsem.at[i], self.me.near(axis, k))
 
@@ -445,7 +446,8 @@
         axis = self.order[0]
         out = [pltpu.make_async_copy(self.quarter(axis, self.at(axis, 0)), self.mine, self.loc.at[0])]
         if self.land is not None:
-            out.append(pltpu.make_async_copy(self.land, self.got1, self.loc.at[1]))
+            for k in range(3):
+                out.append(pltpu.make_async_copy(self.land.at[k], self.got1[k], self.loc.at[1 + k]))
         return out
 
     def load(self):
@@ -471,7 +473,7 @@
             at = (n,) if len(dims) == 1 else (n // dims[1], lax.rem(n, dims[1]))
             total = self.mine[at].astype(F32)
             for k in range(3):
-                total = total + self.got1[(k, *at)].astype(F32)
+                total = total + self.got1[k][at].astype(F32)
             self.sum1[at] = total.astype(BF)
 
         for k in (2, 1, 3):
@@ -510,41 +512,49 @@
 
 
 REDUCE = reduce_specs(None, None, None, None)
-MLP = ("g", "u", "da", "db")
-
-
-def reduce_scratch(staged=REDUCE):
+def reduce_scratch(names, staged):
     out = []
-    for name, (_, _, _, big, small) in REDUCE.items():
+    for name in names:
+        big, small = REDUCE[name][3:]
         out += [vm(big), vm((3,) + big)] if name in staged else []
         out += [vm(big), vm((3,) + small)]
-    return out + [dma(7, 6), dma(7, 6), dma(7, 2)]
-
-
-def make_reduces(me, parts, refs, land=None, landed=False, stage=None):
-    out, n = {}, 0
-    for name, spec in reduce_specs(*parts).items():
-        own, got = stage[name] if stage and name in stage else (refs.pop(0), refs.pop(0))
-        sum1, got2 = refs.pop(0), refs.pop(0)
-        out[name] = (spec, own, got, sum1, got2)
+    n = len(names)
+    return out + [dma(n, 6), dma(n, 6), dma(n, 4)]
+
+
+def make_reduces(me, names, parts, refs, land=None, landed=(), stage=None):
+    specs, out = reduce_specs(*parts), {}
+    for name in names:
+        if stage and name in stage:
+            own, got = stage[name]
+        else:
+            own, got = refs.pop(0), refs.pop(0)
+            got = [got.at[k] for k in range(3)]
+        out[name] = (own, got, refs.pop(0), refs.pop(0))
     ssem, rsem, loc = refs.pop(0), refs.pop(0), refs.pop(0)
-    for n, (name, (spec, own, got, sum1, got2)) in enumerate(out.items()):
+    for n, (name, bufs) in enumerate(out.items()):
         there = land.get(name) if land else None
-        out[name] = Reduce(
-            me, spec, own, got, sum1, got2, ssem.at[n], rsem.at[n], loc.at[n], there, landed and there is not None
-        )
+        out[name] = Reduce(me, specs[name], *bufs, ssem.at[n], rsem.at[n], loc.at[n], there, name in landed)
     return out
 
 
-def finish_reduces(reds, fin, down, out):
-    for lo, hi, name in ((0, 256, "ia"), (256, 384, "ib"), (384, 896, "g"), (896, 1408, "u")):
+COLUMNS = {"ia": (0, 256), "ib": (256, 384), "g": (384, 896), "u": (896, 1408)}
+MLP = ("g", "u", "da", "db")
+REST = ("ia", "ib", "o")
+
+
+def finish_columns(reds, names, fin):
+    for name in names:
+        lo, hi = COLUMNS[name]
         total = reds[name].three()
         for dp in range(2):
             for z in range(4):
                 fin[dp, z, :, lo:hi] = padded(total[dp, 12 * z : 12 * z + 12])
+
+
+def finish_down(reds, down):
     down[:, :, 0:768] = reds["da"].three().astype(BF)
     down[:, :, 768:1536] = reds["db"].three().astype(BF)
-    out[...] = reds["o"].three().astype(BF)
 
 
 def lane_masks(rows):
@@ -763,19 +773,20 @@
         up = mm(buf2[rows], w_u[...].reshape(WIDE, 512))
         up_v[rows] = up.astype(BF)
         hid[rows] = (gate / (1.0 + jnp.exp(-gate)) * up).astype(BF)
-
-    hooks = (lambda: each(g_d, "two"), lambda: None, lambda: each(g_next, "one"))
+        for src, dst in ((buf2, o_nmlp), (gate_v, o_gate), (up_v, o_up), (hid, o_hidden)):
+            store(src.at[rows], dst.at[rows])
+
+    def weights_out():
+        each(g_next, "one")
+        for w, o in [(w_o, o_wo), (w_g, o_wg), (w_u, o_wu)] + ([(w_in, o_win)] if first else []):
+            store(w, o)
+
+    hooks = (lambda: each(g_d, "two"), lambda: None, weights_out)
     done_ag2 = all_gather(me, buf2, ag2_s, ag2_r, gated, hooks)
-    store(buf2, o_nmlp)
-    store(gate_v, o_gate)
-    store(up_v, o_up)
-    store(hid, o_hidden)
     each(g_next, "two")
     each(g_d, "three")
+    store(w_d, o_wd)
     done_rs()
-    pairs = [(w_o, o_wo), (w_g, o_wg), (w_u, o_wu), (w_d, o_wd)] + ([(w_in, o_win)] if first else [])
-    for w, o in pairs:
-        store(w, o)
 
     if not first:
         done_cot = run(ring)
@@ -816,14 +827,16 @@
     take = lambda n: [refs.pop(0) for _ in range(n)]
     grad, stream, middle, gains, cos, sin, pcol, prow, lse = take(9)
     h_in, h_o, h_g, h_u, h_d, h_qkv, h_gate, h_up, h_normed, h_mixed, h_nmlp, h_hidden = take(12)
-    above = take(4) if last else None
+    above, landed = (take(4), dict(zip(MLP, take(4)))) if last else (None, None)
     (h_down,) = (None,) if last else take(1)
     o_grad, o_gains = take(2)
     (o_block,) = (None,) if last else take(1)
     o_fin, o_down, o_out = take(3) if last else (None,) * 3
     parts = take(4)
     o_din, o_dgu, o_dd, o_do = parts
-    landing, landing1 = (dict(zip(MLP, take(4))) if last else {} for _ in range(2))
+    landing = dict(zip(MLP, take(4)))
+    if last:
+        landing["o"] = take(1)[0]
     w_in, w_o, w_g, w_u, w_d, buf1, buf2, qr, gate_v, up_v, gu, mgs, mgr = take(13)
     keys, vals, keys_t, dk, dv, dqs, ps, pr, mid_grad, mixed, nmlp, hid = take(12)
     d_in, d_gu, d_d, d_o = take(4)
@@ -843,20 +856,39 @@
         stores.append(pltpu.make_async_copy(src, dst, loc2.at[len(stores)]))
         stores[-1].start()
 
-    reds, early = {}, {}
     rs3 = refs
+    local = (d_in, d_gu, d_d, d_o)
+    upper = {}
     if last:
         stage = {
-            "g": (w_g.at[3], w_g.at[0:3]), "u": (w_u.at[3], w_u.at[0:3]),
-            "da": (w_d.at[3, :, :, :, 0:768], w_d.at[0:3, :, :, :, 0:768]),
-            "db": (w_d.at[3, :, :, :, 768:WIDE], w_d.at[0:3, :, :, :, 768:WIDE]),
+            "g": [d_gu.at[:, :, k, :, 0:512] for k in range(4)], "u": [d_gu.at[:, :, k, :, 512:1024] for k in range(4)],
+            "da": [d_d.at[:, :, k, :, 0:768] for k in range(4)], "db": [d_d.at[:, :, k, :, 768:WIDE] for k in range(4)],
         }
-        reds = make_reduces(me, above, refs, landing1, False, stage)
-        specs, (es, er) = reduce_specs(*parts), refs
-        early = {
-            name: Reduce(me, specs[name], None, landing[name], None, None, es.at[n], er.at[n], None)
+        stage["ia"] = [d_in.at[:, :, k, :, 0:256] for k in range(4)]
+        stage["ib"] = [d_in.at[:, :, k, :, 256:384] for k in range(4)]
+        stage["o"] = [d_o.at[:, k] for k in range(4)]
+        stage = {name: (views[3], views[:3]) for name, views in stage.items()}
+        upper = make_reduces(me, MLP + REST, above, refs, landed, MLP, stage)
+        stage = {
+            "g": [w_g.at[k] for k in range(4)], "u": [w_u.at[k] for k in range(4)],
+            "da": [w_d.at[k, :, :, :, 0:768] for k in range(4)], "db": [w_d.at[k, :, :, :, 768:WIDE] for k in range(4)],
+        }
+        stage = {name: (views[3], views[:3]) for name, views in stage.items()}
+        own = make_reduces(me, MLP, local, refs, landing, (), stage)
+        es, er = refs
+        own["o"] = Reduce(me, reduce_specs(*local)["o"], None, None, None, None, es, er, None, landing["o"])
+    else:
+        es, er = rs3[6:]
+        specs = reduce_specs(*local)
+        own = {
+            name: Reduce(me, specs[name], None, None, None, None, es.at[n], er.at[n], None, landing[name])
             for n, name in enumerate(MLP)
         }
+
+    def each(reds, names, step):
+        for name in names:
+            if name in reds:
+                getattr(reds[name], step)()
 
     own_rows = slot_rows(me.z, me.core)
     if last:
@@ -865,8 +897,8 @@
         load_down = pltpu.make_async_copy(h_down, buf1, loc.at[11])
         load_down.start()
     me.greet(me.layer_partners())
-    for red in reds.values():
-        red.one()
+    each(upper, MLP, "load")
+    each(upper, REST, "one")
     for load in loads[:3]:
         load.wait()
 
@@ -879,7 +911,8 @@
         gu[rows, 512:1024] = (hg * (gate * sig)).astype(BF)
 
     if last:
-        done_ag = all_gather(me, buf1, ag_s, ag_r, unit)
+        hooks = (lambda: each(upper, REST, "load"), lambda: None, lambda: each(upper, MLP, "two"))
+        done_ag = all_gather(me, buf1, ag_s, ag_r, unit, hooks)
     else:
         load_down.wait()
         for zz in range(4):
@@ -910,6 +943,7 @@
         else:
             grad_gu(2)
             grad_gu(3)
+            each(own, ("g", "u"), "one")
 
     rs = (whole, keep, give, got, ring_out, ring_in)
     e, done_rs = reduce_scatter(me, mlp_part, *rs, rs_s, rs_r, fill1)
@@ -932,16 +966,11 @@
         dk[...] = jnp.zeros_like(dk)
         dv[...] = jnp.zeros_like(dv)
 
-    def hook1():
-        for red in reds.values():
-            red.arrive()
-            red.load()
-
     def hook2():
-        for red in reds.values():
-            red.two()
-
-    done_ag2 = all_gather(me, buf2, ag2_s, ag2_r, mixed_back, (hook0, hook1, hook2))
+        each(upper, REST, "arrive")
+        each(upper, REST, "two")
+
+    done_ag2 = all_gather(me, buf2, ag2_s, ag2_r, mixed_back, (hook0, lambda: None, hook2))
     if last:
         done_ag()
     normed = buf1
@@ -965,13 +994,10 @@
             return mm(hid[span_of(zz * 256, 256)], w_d[...].reshape(512, WIDE))
 
         done_rs()
-        final = reduce_steps(me, down_part, whole, keep, *rs3)
+        final = reduce_steps(me, down_part, whole, keep, *rs3[:6])
         next(final)
-    if last:
-        stores[0].wait()
-        early["da"].one()
-        early["db"].one()
     ax.arrive()
+    each(own, ("da", "db"), "one")
 
     @pl.loop(0, 8)
     def _(p):
@@ -987,8 +1013,8 @@
         dk[...] += mm(sg, q)
         dv[...] += mm(probs.astype(BF), mg)
         dq = jnp.transpose(mm(keys_t[...], sg)) * SCALE
-        dqs[rows, 0:128] = dq[0:128]
-        dqs[rows, 128:256] = dq[128:256]
+        dqs[rows, 0:128] = dq[0:128].astype(BF)
+        dqs[rows, 128:256] = dq[128:256].astype(BF)
 
     if not last:
         next(final)
@@ -1000,15 +1026,14 @@
         p = lax.rem(me.c + 1 + k, 8)
         rows = span_of(p * 128, 128)
         value = dv[rows]
-        ps[rows, 0:128] = jnp.where(v0, value, dqs[rows, 0:128]).astype(BF)
-        ps[rows, 128:256] = jnp.where(v0, pltpu.roll(value, 112, 1), dqs[rows, 128:256]).astype(BF)
+        ps[rows, 0:128] = jnp.where(v0, value, dqs[rows, 0:128].astype(F32)).astype(BF)
+        ps[rows, 128:256] = jnp.where(v0, pltpu.roll(value, 112, 1), dqs[rows, 128:256].astype(F32)).astype(BF)
         ps[rows, 256:384] = jnp.where(v0, pltpu.roll(value, 96, 1), dk[rows] * SCALE).astype(BF)
         bx.send(p)
 
     if last:
-        stores[1].wait()
-        early["g"].one()
-        early["u"].one()
+        each(own, MLP, "arrive")
+        each(own, MLP, "load")
         done_rs()
     else:
         total, done_rs3 = run(final)
@@ -1030,8 +1055,13 @@
             cols = slice(384 * b, 384 * b + 384)
             pair = slice(b % 2 * 2, b % 2 * 2 + 2)
             d_in[b // 2, pair] = mm_tn(normed[:, cols], pre[...]).astype(BF).reshape(2, 4, 48, 384)
+        if n == 0 and last:
+            each(own, MLP, "two")
+            each(own, ("o",), "one")
         if n == 1 and last:
-            finish_reduces(reds, o_fin, o_down, o_out)
+            finish_columns(upper, COLUMNS, o_fin.at[:, :, 1])
+            finish_down(upper, o_down.at[:, 1])
+            o_out[...] = upper["o"].three().astype(BF)
 
     e, done_rs2 = reduce_scatter(me, in_part, *rs, rs2_s, rs2_r, fill2)
     store(d_in, o_din)
@@ -1040,14 +1070,18 @@
     o_grad[...] = mid_grad[...] + part
     for done in (done_ag2, ax.finish, bx.finish, done_rs2):
         done()
-    for red in reds.values():
-        red.finish()
-    if not last:
+    for name, red in upper.items():
+        red.finish((1,) if name in MLP else (0, 1))
+    if last:
+        finish_columns(own, ("g", "u"), o_fin.at[:, :, 0])
+        finish_down(own, o_down.at[:, 0])
+        own["o"].arrive()
+    else:
         done_rs3()
-    for red in early.values():
-        red.arrive()
-        red.finish((0,))
-    for copy in stores[2 if last else 0 :]:
+        each(own, MLP, "arrive")
+    for name, red in own.items():
+        red.finish((0, 1) if last and name in MLP else (0,))
+    for copy in stores:
         copy.wait()
 
 
@@ -1058,15 +1092,14 @@
 def grads_kernel(*refs):
     refs = list(refs)
     take = lambda n: [refs.pop(0) for _ in range(n)]
-    gp0, gp1, fin1, down1, out1 = take(5)
-    parts = take(4)
-    landed = dict(zip(MLP, take(4)))
+    gp0, gp1, fin_in, down_s, out1 = take(5)
+    d_in, d_o, land_o = take(3)
     o_rows, o_down, o_out, o_gains = take(4)
-    reds = make_reduces(Place(), parts, refs, landed, True)
-    gains, fin_s, fin_r, down_s, down_r, out_s, out_r, sum_a, sum_b, got_a, got_b, got_c = take(12)
+    me = Place()
+    reds = make_reduces(me, REST, (d_in, None, None, d_o), refs, {"o": land_o}, ("o",))
+    gains, fin_s, fin_r, down_r, out_s, out_r, sum_a, sum_b, got_a, got_b, got_c = take(11)
     fin_ss, fin_rs, gain_s, gain_r, down_ss, down_rs, out_ss = take(7)
-    me = Place()
-    mlp, rest = [reds[n] for n in MLP], [reds[n] for n in ("ia", "ib", "o")]
+    rest = [reds["ia"], reds["ib"]]
     group = [(k, c) for k in range(4) for c in range(2) if k or c]
 
     def mate(k, c):
@@ -1103,17 +1136,34 @@
         to_z, to_core = lax.rem(me.z + k, 4), lax.rem(me.core + c, 2)
         from_z = lax.rem(me.z + 4 - k, 4)
         dst = fin_r.at[from_z * 2 + to_core, l] if come else fin_r.at[slot, l]
-        return push(fin_s.at[to_core, to_z, l], dst, fin_ss.at[l, i], fin_rs.at[l, i], mate(k, c))
+        src = fin_in.at[to_core, to_z, l] if l else fin_s.at[to_core, to_z]
+        return push(src, dst, fin_ss.at[l, i], fin_rs.at[l, i], mate(k, c))
+
+    def down(dp, half):
+        dev = {"core": jnp.int32(dp), "yl": me.core}
+        return push(down_s.at[dp], down_r.at[half], down_ss.at[dp], down_rs.at[half], dev)
+
+    mine = me.yl == me.core
 
     for k in (1, 2, 3):
         gain_copy(0, "y", gains, got_a, k).start()
     for red in rest:
         red.one()
-    fin_s[:, :, 1] = fin1[...]
     for i in range(7):
         fin(1, i, False).start()
-    for red in mlp:
-        red.two()
+    for dp in range(2):
+        keep = mine & (me.core == dp)
+
+        @pl.when(jnp.logical_not(keep))
+        def _(dp=dp):
+            down(dp, me.yl).start()
+
+        @pl.when(keep)
+        def _(dp=dp):
+            down_r[me.yl] = down_s[dp]
+
+    reds["o"].two()
+    fin_s[...] = fin_in[:, :, 0]
     for red in rest:
         red.arrive()
     gain_sum(0, "y", gains, got_a, sum_a)
@@ -1128,31 +1178,15 @@
 
     for i in range(7):
         gain_mate(i).start()
-    down_s[:, 1] = down1[...]
     out_s[1] = out1[...]
-    finish_reduces(reds, fin_s.at[:, :, 0], down_s.at[:, 0], out_s.at[0])
-    def down(dp, half):
-        dev = {"core": jnp.int32(dp), "yl": me.core}
-        return push(down_s.at[dp], down_r.at[half], down_ss.at[dp], down_rs.at[half], dev)
-
-    mine = me.yl == me.core
+    finish_columns(reds, ("ia", "ib"), fin_s)
+    out_s[0] = reds["o"].three().astype(BF)
 
     def out_copy():
         return push(out_s, out_r, out_ss.at[0], out_ss.at[1], mirror)
 
     for i in range(7):
         fin(0, i, False).start()
-    for dp in range(2):
-        keep = mine & (me.core == dp)
-
-        @pl.when(jnp.logical_not(keep))
-        def _(dp=dp):
-            down(dp, me.yl).start()
-
-        @pl.when(keep)
-        def _(dp=dp):
-            down_r[me.yl] = down_s[dp]
-
     @pl.when(apart)
     def _():
         out_copy().start()
@@ -1161,7 +1195,8 @@
     def _():
         out_r[...] = out_s[...]
 
-    fin_r[slot] = fin_s[me.core, me.z]
+    fin_r[slot, 0] = fin_s[me.core, me.z]
+    fin_r[slot, 1] = fin_in[me.core, me.z, 1]
     total = sum_b[...]
     for i in range(7):
         gain_mate(i).wait_recv()
@@ -1184,8 +1219,7 @@
         out_copy().wait_recv()
 
     o_out[...] = out_r[...]
-    for red in mlp:
-        red.finish((1,))
+    reds["o"].finish((1,))
     for red in rest:
         red.finish()
     for k in (1, 2, 3):
@@ -1219,13 +1253,13 @@
 
 
 def sems():
-    return [dma(n) for n in (13, 13, 13, 13, 10, 10, 10, 10, 8, 8, 8, 8, 16, 16)]
+    return [dma(n) for n in (13, 13, 13, 13, 10, 10, 10, 10, 8, 8, 8, 8, 16, 32)]
 
 
 WEIGHTS = [(WIDE, 384), (256, WIDE), (WIDE, 512), (WIDE, 512), (512, WIDE)]
 SPLIT = [(2, 4, 4, 48, 384), (4, 64, WIDE), (2, 4, 4, 48, 512), (2, 4, 4, 48, 512), (2, 4, 4, 16, WIDE)]
 PARTS = [(2, 4, 4, 48, 384), (2, 4, 4, 48, 1024), (2, 4, 4, 16, WIDE), (4, 4, 16, WIDE)]
-RING = [(256, WIDE), (4, 128, WIDE)]
+RING = [((256, WIDE), F32), ((4, 128, WIDE), BF)]
 
 
 def run_kernel(kernel, name, cid, ins, in_vmem, outs, out_vmem, scratch):
@@ -1255,7 +1289,7 @@
         vm((1024, WIDE)), vm((1024, WIDE)), vm((1024, 384)), vm((1024, 384)), vm((1024, 256)), vm((1024, 256)),
         vm((1024, 512)), vm((1024, 512)), vm((1024, 512)),
         vm((1024, 128)), vm((1024, 128)), vm((128, 1024)), vm((128, WIDE), F32),
-    ] + [vm(s, F32) for s in RING] + rs_scratch() + sems() + [dma(10, 7), dma(10, 7)]
+    ] + [vm(*s) for s in RING] + rs_scratch() + sems() + [dma(10, 7), dma(10, 7)]
     if first:
         scratch += [vm((2, 4, 4, 8, 256), F32), vm(SPLIT[0])]
     else:
@@ -1268,22 +1302,22 @@
 def layer_bwd(l, grad, stream, middle, gains, tables, lse, weights, saved, above):
     last = l == 0
     outs = [((128, WIDE), F32), ((8, WIDE), F32)]
-    outs += [((2, 4, 16, 1408), BF), ((2, 16, WIDE), BF), ((16, WIDE), BF)] if last else [((128, WIDE), BF)]
+    outs += [((2, 4, 2, 16, 1408), BF), ((2, 2, 16, WIDE), BF), ((16, WIDE), BF)] if last else [((128, WIDE), BF)]
     n_vmem = len(outs)
     outs += [(s, BF) for s in PARTS]
-    outs += [((3,) + REDUCE[n][3], BF) for n in MLP] * 2 if last else []
+    outs += [((3,) + REDUCE[n][3], BF) for n in (MLP + ("o",) if last else MLP)]
     shapes = WEIGHTS[:2] + [(4, 2, 4, 48, 512), (4, 2, 4, 48, 512), (4, 2, 4, 16, WIDE)]
     scratch = [vm(s) for s in shapes] + [
         vm((1024, WIDE)), vm((1024, WIDE)), vm((1024, 384)), vm((1024, 512)), vm((1024, 512)),
         vm((1024, 1024)), vm((1024, 256)), vm((1024, 256)),
         vm((1024, 128)), vm((1024, 128)), vm((128, 1024)), vm((1024, 128), F32), vm((1024, 128), F32),
-        vm((1024, 256), F32), vm((1024, 384)), vm((1024, 384)), vm((128, WIDE), F32),
+        vm((1024, 256)), vm((1024, 384)), vm((1024, 384)), vm((128, WIDE), F32),
         vm((1024, 256)), vm((1024, WIDE)), vm((1024, 512)),
-    ] + [vm(s) for s in PARTS] + [vm(s, F32) for s in RING] + rs_scratch() + sems()
+    ] + [vm(s) for s in PARTS] + [vm(*s) for s in RING] + rs_scratch() + sems()
     if last:
-        scratch += reduce_scratch(("ia", "ib", "o")) + [dma(4, 6), dma(4, 6)]
+        scratch += reduce_scratch(MLP + REST, ()) + reduce_scratch(MLP, ()) + [dma(6), dma(6)]
     else:
-        scratch += rs_scratch() + [dma(10), dma(10)]
+        scratch += rs_scratch() + [dma(10), dma(10), dma(4, 6), dma(4, 6)]
     weights = [w.reshape(s) for w, s in zip(weights, shapes)]
     ins = [grad, stream, middle, gains, *tables, lse, *weights, *saved, *(above or ())]
     kernel = functools.partial(bwd_kernel, l)
@@ -1440,15 +1474,15 @@
     return [grad.transpose(1, 0, 2) for grad in grads] + [d_d]
 
 
-def reduce_grads(gain_parts, done, parts, landed):
+def reduce_grads(gain_parts, done, parts):
     outs = [((8, 2, 16, 1408), BF), ((2, 2, 16, WIDE), BF), ((2, 16, WIDE), BF), ((8, WIDE), F32)]
-    scratch = reduce_scratch() + [
-        vm((8, WIDE), F32), vm((2, 4, 2, 16, 1408)), vm((8, 2, 16, 1408)), vm((2, 2, 16, WIDE)), vm((2, 2, 16, WIDE)),
+    scratch = reduce_scratch(REST, REST) + [
+        vm((8, WIDE), F32), vm((2, 4, 16, 1408)), vm((8, 2, 16, 1408)), vm((2, 2, 16, WIDE)),
         vm((2, 16, WIDE)), vm((2, 16, WIDE)), vm((8, WIDE), F32), vm((8, WIDE), F32),
         vm((3, 8, WIDE), F32), vm((3, 8, WIDE), F32), vm((7, 8, WIDE), F32),
         dma(2, 7), dma(2, 7), dma(13), dma(13), dma(2), dma(2), dma(2),
     ]
-    return run_kernel(grads_kernel, "reduce_gradients", 5, [*gain_parts, *done, *parts, *landed], 5, outs, 4, scratch)
+    return run_kernel(grads_kernel, "reduce_gradients", 5, [*gain_parts, *done, *parts], 5, outs, 4, scratch)
 
 
 def body(
@@ -1480,7 +1514,7 @@
         g, gain_parts[l] = res[:2]
         if l:
             block_out, above = res[2][None], tuple(res[3:])
-    cols, d_d, d_o, gp = reduce_grads(gain_parts, res[2:5], res[5:9], res[9:13])
+    cols, d_d, d_o, gp = reduce_grads(gain_parts, res[2:5], (res[5], res[8], res[13]))
     d_q, d_k, d_v, d_o, d_g, d_u, d_d = assemble(cols, d_d, d_o)
     owner = (core * 8 + ctx) * 8 + yl * 4 + z
     gp = lax.dynamic_slice(gp, (0, owner * 12), (4, 12)).reshape(2, 2, 12)

time: 490 us -> 479 us (0.978)
  Pallas kernels: 481 us -> 472 us
    pallas_call x5, Pallas kernels: 472 us -> 462 us  [run_kernel(): pl.pallas_call(kernel, name=name, out_shape=[jax.ShapeDtypeStruct(s, d) f...]
where the time goes in v5:
time: 479 us; the launch traced here: 476 us
  Pallas kernels  472 us (99%)
    pallas_call x5, Pallas kernels, run_kernel(): pl.pallas_call(kernel, name=name, out_shape=[jax.ShapeDtypeStruct(s, d) f...  462 us

profile of v5, /device:TPU:5, one launch (start us, length us, event | category | flops | bytes accessed | tf_op | source)
XLA Modules:
  0.0 475.7 jit_solution(12688472722535526716)
XLA Ops:
  0.6 4.4 prepare_sources.1
  5.0 119.2 %layer_forward_0.1 = (f32[128,1536]{1,0:T(8,128)}, f32[128,1536]{1,0:T(8,128)}, f32[8,256]{1,0:T(8,128)}, f32[8,1536]{1,0:T(8,128)}, bf16[1024,1536]{1,0:T(8,128...) custom-call(bf16[128,1536]{1,0:T(8,128)(2,1)} %bitcast.32, ...), custom_call_target="tpu_custom_call" | custom-call | tf_op jit(solution)/shard_map/layer_forward_0/pallas_call | solution.py:1267
  124.2 93.3 %layer_forward_1.1 = (f32[128,1536]{1,0:T(8,128)}, f32[8,256]{1,0:T(8,128)}, bf16[1024,1536]{1,0:T(8,128)(2,1)}, bf16[1024,384]{1,0:T(8,128)(2,1)}, bf16[1024,25...) custom-call(f32[128,1536]{1,0:T(8,128)} %get-tuple-element.88.refs_0, ...), custom_call_target="tpu_custom_call" | custom-call | tf_op jit(solution)/shard_map/layer_forward_1/pallas_call | solution.py:1267
  217.6 97.9 %layer_backward_1.1 = (f32[128,1536]{1,0:T(8,128)}, f32[8,1536]{1,0:T(8,128)}, bf16[128,1536]{1,0:T(8,128)(2,1)}, bf16[2,4,4,48,384]{4,3,2,1,0:T(8,128)(2,1)}, b...) custom-call(bf16[128,1536]{1,0:T(8,128)(2,1)} %bitcast.28, ...), custom_call_target="tpu_custom_call" | custom-call | tf_op jit(solution)/shard_map/layer_backward_1/pallas_call | solution.py:1267
  315.5 112.1 %layer_backward_0.1 = (f32[128,1536]{1,0:T(8,128)}, f32[8,1536]{1,0:T(8,128)}, bf16[2,4,2,16,1408]{4,3,2,1,0:T(8,128)(2,1)}, bf16[2,2,16,1536]{3,2,1,0:T(8,128)(...) custom-call(f32[128,1536]{1,0:T(8,128)} %get-tuple-element.106.refs_, ...), custom_call_target="tpu_custom_call" | custom-call | tf_op jit(solution)/shard_map/layer_backward_0/pallas_call | solution.py:1267
  427.6 0.0 copy-start.1
  427.6 39.8 %reduce_gradients.1 = (bf16[8,2,16,1408]{3,2,1,0:T(8,128)(2,1)}, bf16[2,2,16,1536]{3,2,1,0:T(8,128)(2,1)}, bf16[2,16,1536]{2,1,0:T(8,128)(2,1)}, f32[8,1536]{1,0:T(8,128)}) custom-call(f32[8,1536]{1,0:T(8,128)} %get-tuple-element.130.refs_0_, f32[8,1536]{1,0:T(8,128)} %get-tuple-element.131.refs_1_, bf16[2,4,2,16,1408]{4,3,2,1,0:T(8,128)(2,1)} %get-tuple-element.132.refs_2_, ...), custom_call_target="tpu_custom_call" | custom-call | tf_op jit(solution)/shard_map/reduce_gradients/pallas_call | solution.py:1267
  467.4 0.0 copy-start
  467.4 5.0 %assemble_gradients.1 = (f32[12,2,1536]{2,1,0:T(2,128)}, f32[12,2,768]{2,1,0:T(2,128)}, f32[12,2,768]{2,1,0:T(2,128)}, f32[12,2,1536]{2,1,0:T(2,128)}, f32[12,2,...) custom-call(bf16[8,2,16,1408]{3,2,1,0:T(8,128)(2,1)} %get-tuple-element.139.cols, ...), custom_call_target="tpu_custom_call" | custom-call | tf_op jit(solution)/shard_map/assemble_gradients/pallas_call | solution.py:1466
  472.4 0.8 constant_dynamic-slice_fusion
  473.2 0.6 fusion
  473.8 0.0 copy-done.1
  473.8 0.7 copy.25
  474.5 0.0 copy-done
  474.5 0.9 copy.26
Async XLA Ops:
  427.6 46.2 %copy-start.1 = (bf16[128,1536]{1,0:T(8,128)(2,1)S(1)}, bf16[128,1536]{1,0:T(8,128)(2,1)}, u32[]{:S(2)}) copy-start(bf16[128,1536]{1,0:T(8,128)(2,1)} %get-tuple-element.105) | copy-start | bytes 1179652
  467.4 7.1 %copy-start = (f32[128,1536]{1,0:T(8,128)S(1)}, f32[128,1536]{1,0:T(8,128)}, u32[]{:S(2)}) copy-start(f32[128,1536]{1,0:T(8,128)} %get-tuple-element.129) | copy-start | bytes 2359300

commit v6 on v5

--- a/solution.py
+++ b/solution.py
@@ -762,6 +762,9 @@
     o_middle[...] = mid
     buf2[own_rows] = (mid * rms_of(mid) * o_gains[g_mlp, :]).astype(BF)
     waited = []
+    if not first:
+        done_cot = run(ring)
+        store(cot_all, o_down)
 
     def gated(zz):
         if not waited:
@@ -781,16 +784,16 @@
         for w, o in [(w_o, o_wo), (w_g, o_wg), (w_u, o_wu)] + ([(w_in, o_win)] if first else []):
             store(w, o)
 
-    hooks = (lambda: each(g_d, "two"), lambda: None, weights_out)
+    def down_here():
+        each(g_d, "three")
+        store(w_d, o_wd)
+
+    hooks = (lambda: each(g_d, "two"), lambda: None, weights_out, down_here)
     done_ag2 = all_gather(me, buf2, ag2_s, ag2_r, gated, hooks)
     each(g_next, "two")
-    each(g_d, "three")
-    store(w_d, o_wd)
     done_rs()
 
     if not first:
-        done_cot = run(ring)
-        store(cot_all, o_down)
         for done in (done_ag, ax.finish, bx.finish, done_ag2, done_cot):
             done()
         each(everything, "finish")
@@ -801,10 +804,13 @@
     def down_part(zz):
         return mm(hid[span_of(zz * 256, 256)], w_d[...].reshape(512, WIDE))
 
-    total, done_rs2 = reduce_scatter(me, down_part, *rs, rs2_s, rs2_r)
+    def fill(n):
+        if n == 2:
+            each(g_next, "three")
+            store(w_next, o_next)
+
+    total, done_rs2 = reduce_scatter(me, down_part, *rs, rs2_s, rs2_r, fill)
     o_stream[...] = middle[...] + total
-    each(g_next, "three")
-    store(w_next, o_next)
     for done in (ax.finish, bx.finish, done_ag2, done_rs2):
         done()
     each(everything, "finish")
@@ -848,7 +854,7 @@
         (h_hidden, hid), (h_nmlp, nmlp), (h_mixed, mixed),
     )
     loads = [pltpu.make_async_copy(h, v, loc.at[i]) for i, (h, v) in enumerate(pairs)]
-    for load in loads:
+    for load in loads if last else loads[:5]:
         load.start()
     stores = []
 
@@ -917,8 +923,10 @@
         load_down.wait()
         for zz in range(4):
             unit(zz)
-    for load in loads[3:]:
+    for load in loads[3:5]:
         load.wait()
+    for load in () if last else loads[5:]:
+        load.start()
 
     def mlp_part(zz):
         rows = span_of(zz * 256, 256)
@@ -935,6 +943,8 @@
 
     def fill1(n):
         if n == 0:
+            for load in loads[5:]:
+                load.wait()
             grad_down(0)
             grad_down(1)
         elif n == 1:
@@ -1055,6 +1065,8 @@
             cols = slice(384 * b, 384 * b + 384)
             pair = slice(b % 2 * 2, b % 2 * 2 + 2)
             d_in[b // 2, pair] = mm_tn(normed[:, cols], pre[...]).astype(BF).reshape(2, 4, 48, 384)
+        if n == 2:
+            store(d_in, o_din)
         if n == 0 and last:
             each(own, MLP, "two")
             each(own, ("o",), "one")
@@ -1064,7 +1076,6 @@
             o_out[...] = upper["o"].three().astype(BF)
 
     e, done_rs2 = reduce_scatter(me, in_part, *rs, rs2_s, rs2_r, fill2)
-    store(d_in, o_din)
     part, gain_part = norm_back_of(e, stream[...].astype(F32), gains[g_attn, :])
     o_gains[0:1, :] = gain_part
     o_grad[...] = mid_grad[...] + part

time: 479 us -> 476 us (level)
  no operation moved by 1% of the time
where the time goes in v6:
time: 476 us; the launch traced here: 472 us
  Pallas kernels  468 us (98%)
    pallas_call x5, Pallas kernels, run_kernel(): pl.pallas_call(kernel, name=name, out_shape=[jax.ShapeDtypeStruct(s, d) f...  459 us

profile of v6, /device:TPU:5, one launch (start us, length us, event | category | flops | bytes accessed | tf_op | source)
XLA Modules:
  0.0 471.9 jit_solution(1552991997273455254)
XLA Ops:
  0.6 4.4 prepare_sources.1
  5.0 118.6 %layer_forward_0.1 = (f32[128,1536]{1,0:T(8,128)}, f32[128,1536]{1,0:T(8,128)}, f32[8,256]{1,0:T(8,128)}, f32[8,1536]{1,0:T(8,128)}, bf16[1024,1536]{1,0:T(8,128...) custom-call(bf16[128,1536]{1,0:T(8,128)(2,1)} %bitcast.32, ...), custom_call_target="tpu_custom_call" | custom-call | tf_op jit(solution)/shard_map/layer_forward_0/pallas_call | solution.py:1278
  123.6 91.8 %layer_forward_1.1 = (f32[128,1536]{1,0:T(8,128)}, f32[8,256]{1,0:T(8,128)}, bf16[1024,1536]{1,0:T(8,128)(2,1)}, bf16[1024,384]{1,0:T(8,128)(2,1)}, bf16[1024,25...) custom-call(f32[128,1536]{1,0:T(8,128)} %get-tuple-element.88.refs_0, ...), custom_call_target="tpu_custom_call" | custom-call | tf_op jit(solution)/shard_map/layer_forward_1/pallas_call | solution.py:1278
  215.4 95.5 %layer_backward_1.1 = (f32[128,1536]{1,0:T(8,128)}, f32[8,1536]{1,0:T(8,128)}, bf16[128,1536]{1,0:T(8,128)(2,1)}, bf16[2,4,4,48,384]{4,3,2,1,0:T(8,128)(2,1)}, b...) custom-call(bf16[128,1536]{1,0:T(8,128)(2,1)} %bitcast.28, ...), custom_call_target="tpu_custom_call" | custom-call | tf_op jit(solution)/shard_map/layer_backward_1/pallas_call | solution.py:1278
  310.9 111.8 %layer_backward_0.1 = (f32[128,1536]{1,0:T(8,128)}, f32[8,1536]{1,0:T(8,128)}, bf16[2,4,2,16,1408]{4,3,2,1,0:T(8,128)(2,1)}, bf16[2,2,16,1536]{3,2,1,0:T(8,128)(...) custom-call(f32[128,1536]{1,0:T(8,128)} %get-tuple-element.106.refs_, ...), custom_call_target="tpu_custom_call" | custom-call | tf_op jit(solution)/shard_map/layer_backward_0/pallas_call | solution.py:1278
  422.7 0.0 copy-start.1
  422.7 40.9 %reduce_gradients.1 = (bf16[8,2,16,1408]{3,2,1,0:T(8,128)(2,1)}, bf16[2,2,16,1536]{3,2,1,0:T(8,128)(2,1)}, bf16[2,16,1536]{2,1,0:T(8,128)(2,1)}, f32[8,1536]{1,0:T(8,128)}) custom-call(f32[8,1536]{1,0:T(8,128)} %get-tuple-element.130.refs_0_, f32[8,1536]{1,0:T(8,128)} %get-tuple-element.131.refs_1_, bf16[2,4,2,16,1408]{4,3,2,1,0:T(8,128)(2,1)} %get-tuple-element.132.refs_2_, ...), custom_call_target="tpu_custom_call" | custom-call | tf_op jit(solution)/shard_map/reduce_gradients/pallas_call | solution.py:1278
  463.7 0.0 copy-start
  463.7 5.0 %assemble_gradients.1 = (f32[12,2,1536]{2,1,0:T(2,128)}, f32[12,2,768]{2,1,0:T(2,128)}, f32[12,2,768]{2,1,0:T(2,128)}, f32[12,2,1536]{2,1,0:T(2,128)}, f32[12,2,...) custom-call(bf16[8,2,16,1408]{3,2,1,0:T(8,128)(2,1)} %get-tuple-element.139.cols, ...), custom_call_target="tpu_custom_call" | custom-call | tf_op jit(solution)/shard_map/assemble_gradients/pallas_call | solution.py:1477
  468.7 0.8 constant_dynamic-slice_fusion
  469.5 0.6 fusion
  470.0 0.0 copy-done.1
  470.0 0.7 copy.25
  470.8 0.0 copy-done
  470.8 0.9 copy.26
Async XLA Ops:
  422.7 47.3 %copy-start.1 = (bf16[128,1536]{1,0:T(8,128)(2,1)S(1)}, bf16[128,1536]{1,0:T(8,128)(2,1)}, u32[]{:S(2)}) copy-start(bf16[128,1536]{1,0:T(8,128)(2,1)} %get-tuple-element.105) | copy-start | bytes 1179652
  463.7 7.1 %copy-start = (f32[128,1536]{1,0:T(8,128)S(1)}, f32[128,1536]{1,0:T(8,128)}, u32[]{:S(2)}) copy-start(f32[128,1536]{1,0:T(8,128)} %get-tuple-element.129) | copy-start | bytes 2359300

commit v7 on v6

--- a/solution.py
+++ b/solution.py
@@ -1382,7 +1382,8 @@
     shift = lax.rem(96 * owner, 128)
     move = picks(96, 256, lambda r, c: c == r + shift)
     zero = jnp.zeros((4, 96), F32)
-    both = jnp.concatenate([ga[0:1], gm[0:1], ga[1:2], gm[1:2]], axis=0).astype(F32)
+    attn, mlp = ga[...].astype(F32), gm[...].astype(F32)
+    both = jnp.concatenate([attn[0:1], mlp[0:1], attn[1:2], mlp[1:2]], axis=0)
     placed = mm(jnp.concatenate([both, zero], axis=0).astype(BF), move)
     o_gain[0] = placed
     o_gain[1] = placed
@@ -1466,7 +1467,7 @@
             total = sum(mm(member(j, start + 128 * b, start + 128 * b + 128), back[j]) for j in range(8))
             put(dst, 1024 * b, 1024 * b + 1024, total)
     for l in range(LAYERS):
-        o_o[:, l, :] = outs[l, 0:12].astype(F32)
+        o_o[:, l, :] = outs[l].astype(F32)[0:12]
         for h in range(2):
             o_d[l, 16 * h : 16 * h + 16] = downs[h, l].astype(F32)
 

time: 476 us -> 475 us (level)
  no operation moved by 1% of the time
where the time goes in v7:
time: 475 us; the launch traced here: 472 us
  Pallas kernels  468 us (99%)
    pallas_call x5, Pallas kernels, run_kernel(): pl.pallas_call(kernel, name=name, out_shape=[jax.ShapeDtypeStruct(s, d) f...  459 us

profile of v7, /device:TPU:5, one launch (start us, length us, event | category | flops | bytes accessed | tf_op | source)
XLA Modules:
  0.0 471.9 jit_solution(7996356468217302196)
XLA Ops:
  0.6 4.4 prepare_sources.1
  5.0 118.6 %layer_forward_0.1 = (f32[128,1536]{1,0:T(8,128)}, f32[128,1536]{1,0:T(8,128)}, f32[8,256]{1,0:T(8,128)}, f32[8,1536]{1,0:T(8,128)}, bf16[1024,1536]{1,0:T(8,128...) custom-call(bf16[128,1536]{1,0:T(8,128)(2,1)} %bitcast.32, ...), custom_call_target="tpu_custom_call" | custom-call | tf_op jit(solution)/shard_map/layer_forward_0/pallas_call | solution.py:1278
  123.6 91.8 %layer_forward_1.1 = (f32[128,1536]{1,0:T(8,128)}, f32[8,256]{1,0:T(8,128)}, bf16[1024,1536]{1,0:T(8,128)(2,1)}, bf16[1024,384]{1,0:T(8,128)(2,1)}, bf16[1024,25...) custom-call(f32[128,1536]{1,0:T(8,128)} %get-tuple-element.88.refs_0, ...), custom_call_target="tpu_custom_call" | custom-call | tf_op jit(solution)/shard_map/layer_forward_1/pallas_call | solution.py:1278
  215.4 95.5 %layer_backward_1.1 = (f32[128,1536]{1,0:T(8,128)}, f32[8,1536]{1,0:T(8,128)}, bf16[128,1536]{1,0:T(8,128)(2,1)}, bf16[2,4,4,48,384]{4,3,2,1,0:T(8,128)(2,1)}, b...) custom-call(bf16[128,1536]{1,0:T(8,128)(2,1)} %bitcast.28, ...), custom_call_target="tpu_custom_call" | custom-call | tf_op jit(solution)/shard_map/layer_backward_1/pallas_call | solution.py:1278
  310.9 111.8 %layer_backward_0.1 = (f32[128,1536]{1,0:T(8,128)}, f32[8,1536]{1,0:T(8,128)}, bf16[2,4,2,16,1408]{4,3,2,1,0:T(8,128)(2,1)}, bf16[2,2,16,1536]{3,2,1,0:T(8,128)(...) custom-call(f32[128,1536]{1,0:T(8,128)} %get-tuple-element.106.refs_, ...), custom_call_target="tpu_custom_call" | custom-call | tf_op jit(solution)/shard_map/layer_backward_0/pallas_call | solution.py:1278
  422.7 0.0 copy-start.1
  422.7 40.9 %reduce_gradients.1 = (bf16[8,2,16,1408]{3,2,1,0:T(8,128)(2,1)}, bf16[2,2,16,1536]{3,2,1,0:T(8,128)(2,1)}, bf16[2,16,1536]{2,1,0:T(8,128)(2,1)}, f32[8,1536]{1,0:T(8,128)}) custom-call(f32[8,1536]{1,0:T(8,128)} %get-tuple-element.130.refs_0_, f32[8,1536]{1,0:T(8,128)} %get-tuple-element.131.refs_1_, bf16[2,4,2,16,1408]{4,3,2,1,0:T(8,128)(2,1)} %get-tuple-element.132.refs_2_, ...), custom_call_target="tpu_custom_call" | custom-call | tf_op jit(solution)/shard_map/reduce_gradients/pallas_call | solution.py:1278
  463.7 0.0 copy-start
  463.7 5.0 %assemble_gradients.1 = (f32[12,2,1536]{2,1,0:T(2,128)}, f32[12,2,768]{2,1,0:T(2,128)}, f32[12,2,768]{2,1,0:T(2,128)}, f32[12,2,1536]{2,1,0:T(2,128)}, f32[12,2,...) custom-call(bf16[8,2,16,1408]{3,2,1,0:T(8,128)(2,1)} %get-tuple-element.139.cols, ...), custom_call_target="tpu_custom_call" | custom-call | tf_op jit(solution)/shard_map/assemble_gradients/pallas_call | solution.py:1478
  468.7 0.8 constant_dynamic-slice_fusion
  469.5 0.6 fusion
  470.0 0.0 copy-done.1
  470.0 0.7 copy.25
  470.8 0.0 copy-done
  470.8 0.9 copy.26
Async XLA Ops:
  422.7 47.3 %copy-start.1 = (bf16[128,1536]{1,0:T(8,128)(2,1)S(1)}, bf16[128,1536]{1,0:T(8,128)(2,1)}, u32[]{:S(2)}) copy-start(bf16[128,1536]{1,0:T(8,128)(2,1)} %get-tuple-element.105) | copy-start | bytes 1179652
  463.7 7.1 %copy-start = (f32[128,1536]{1,0:T(8,128)S(1)}, f32[128,1536]{1,0:T(8,128)}, u32[]{:S(2)}) copy-start(f32[128,1536]{1,0:T(8,128)} %get-tuple-element.129) | copy-start | bytes 2359300
